TPU v7x, 1024 devices: a whole 4x8x16 slice. The times are simulated.
1024 devices in a mesh: gx: 64 (over y, x, core), gy: 16 (over z).
Axes of the slice: x: 4, y: 8, z: 16, core: 2. Of those that a mesh axis runs over, the one named last changes fastest.
Arguments:
- density: int32 [256, 128, 512], P('gx', 'gy'), may hold values from 0 to 255
- fixed: int32 [256, 128, 512], P('gx', 'gy'), may hold values from 0 to 1
- loaded: int32 [256, 128, 512], P('gx', 'gy'), may hold values 0 or 1
- load: float32 [3, 256, 128, 512], P(None, 'gx', 'gy'), may hold values from -6 to 6
Outputs:
- correction: float32 [3, 256, 128, 512], P(None, 'gx', 'gy')
All inputs are finite; a program needn't handle non-finite values. No bound on the sum of `loaded` on one device may be relied on, other than what follows from the above.
Results may differ from a plain program's by a relative error of at most 0.0001.
Values sent between devices are 32-bit elements; how exact they have to be, the bound alone decides.
No kernel may reach another device: no remote copies, remote signals or barrier semaphores. Data moves between devices by JAX's collectives and lax.ppermute only.
A program may use at most 64 MiB of HBM per device.

v0:
```python
import jax
import jax.numpy as jnp
from jax import lax
from jax.sharding import PartitionSpec as P

SWEEPS = 4


COUPLING = 0.25
DAMPING = 0.8


def with_halo(cells, sides, width):
    for axis, dim in sides:
        count = lax.axis_size(axis)
        ends = count - 1
        head = lax.slice_in_dim(cells, 0, width, axis=dim)
        tail = lax.slice_in_dim(cells, cells.shape[dim] - width, cells.shape[dim], axis=dim)
        cells = jnp.concatenate(
            [
                lax.ppermute(tail, axis, [(i, (i + 1) % count) for i in range(ends)]),
                cells,
                lax.ppermute(head, axis, [((i + 1) % count, i) for i in range(ends)]),
            ],
            axis=dim,
        )
    return cells


def neighbour_offsets():
    result = []
    for shift_x in (-1, 0, 1):
        for shift_y in (-1, 0, 1):
            for shift_z in (-1, 0, 1):
                if (shift_x, shift_y, shift_z) != (0, 0, 0):
                    result.append((shift_x, shift_y, shift_z))
    return result


def stencil(padded, scale):
    a = padded.shape[1] - 2
    b = padded.shape[2] - 2
    c = padded.shape[3] - 2
    centre = padded[:, 1 : a + 1, 1 : b + 1, 1 : c + 1]
    stiff = centre[3]
    parts = [0.1 * stiff * centre[first] for first in range(3)]
    for offset in neighbour_offsets():
        count = sum((1 for value in offset if value != 0))
        weight = 0.5 ** (count - 1)
        near = padded[
            :,
            1 + offset[0] : 1 + offset[0] + a,
            1 + offset[1] : 1 + offset[1] + b,
            1 + offset[2] : 1 + offset[2] + c,
        ]
        couple = weight * 0.5 * (stiff + near[3])
        for first in range(3):
            term = centre[first] - near[first]
            for second in range(3):
                if second != first and offset[first] * offset[second] != 0:
                    term = term - COUPLING * offset[first] * offset[second] * near[second]
            parts[first] = parts[first] + couple * term
    return scale * jnp.stack(parts)


def block_sum(field):
    k, a, b, c = field.shape
    return field.reshape(k, a // 2, 2, b // 2, 2, c // 2, 2).sum(axis=(2, 4, 6))


def block_max(field):
    k, a, b, c = field.shape
    return field.reshape(k, a // 2, 2, b // 2, 2, c // 2, 2).max(axis=(2, 4, 6))


def prolong(field):
    return jnp.repeat(jnp.repeat(jnp.repeat(field, 2, axis=1), 2, axis=2), 2, axis=3)


def pad_depth(stacked):
    return jnp.pad(stacked, ((0, 0), (0, 0), (0, 0), (1, 1)))


def face_image(update, stiff, border, scale):
    stacked = with_halo(jnp.concatenate([update, stiff]), (("gx", 1), ("gy", 2)), 1)
    return stencil(pad_depth(stacked), scale)


def first_step(force, stiff, free, scale):
    return free * DAMPING * force / (scale * (7.1 * stiff + 7.5))


def smooth(update, force, stiff, free, border, scale, imager):
    image = imager(update, stiff, border, scale)
    return update + free * DAMPING * (force - image) / (scale * (7.1 * stiff + 7.5))


def residual_of(update, force, stiff, free, border, scale, imager):
    image = imager(update, stiff, border, scale)
    return free * (force - image)


def coarse_sweeps(force, stiff, free, border, imager):
    update = first_step(force, stiff, free, 4.0)
    for sweep in range(SWEEPS - 1):
        update = smooth(update, force, stiff, free, border, 4.0, imager)
    return update


def per_device(density, fixed, loaded, load):
    level = (density.astype(jnp.float32) + 1.0) / 256.0
    stiff_fine = (0.05 + level * level * level)[None]
    free_fine = (1 - fixed).astype(jnp.float32)[None]
    force_fine = free_fine * loaded.astype(jnp.float32)[None] * load
    stiff_mid = block_sum(stiff_fine) / 8.0
    free_mid = block_max(free_fine)
    stiff_low = block_sum(stiff_mid) / 8.0
    free_low = block_max(free_mid)
    fine_update = first_step(force_fine, stiff_fine, free_fine, 1.0)
    force_mid = block_sum(
        residual_of(fine_update, force_fine, stiff_fine, free_fine, stiff_fine, 1.0, face_image)
    )
    mid_update = first_step(force_mid, stiff_mid, free_mid, 2.0)
    force_low = block_sum(
        residual_of(mid_update, force_mid, stiff_mid, free_mid, stiff_mid, 2.0, face_image)
    )
    low_update = coarse_sweeps(force_low, stiff_low, free_low, stiff_low, face_image)
    mid_update = mid_update + free_mid * prolong(low_update)
    mid_update = smooth(mid_update, force_mid, stiff_mid, free_mid, stiff_mid, 2.0, face_image)
    fine_update = fine_update + free_fine * prolong(mid_update)
    return smooth(fine_update, force_fine, stiff_fine, free_fine, stiff_fine, 1.0, face_image)


def solution(mesh):
    return jax.shard_map(
        per_device,
        mesh=mesh,
        in_specs=(
            P("gx", "gy", None),
            P("gx", "gy", None),
            P("gx", "gy", None),
            P(None, "gx", "gy", None),
        ),
        out_specs=P(None, "gx", "gy", None),
        check_vma=False,
    )
```

profile of v0, /device:TPU:31, one launch (start us, length us, event | category | flops | bytes accessed | tf_op | source)
XLA Modules:
  0.0 210.4 jit_solution(5862355815465968463)
XLA Ops:
  2.0 4.9 %collective-permute-start = (f32[4,1,8,512]{3,2,1,0:T(8,128)S(1)}, f32[4,1,8,512]{3,2,1,0:T(8,128)S(1)}, u32[]{:S(2)}, u32[]{:S(2)}) collective-permute-start(f32[4,1,8,512]{3,2,1,0:T(8,128)S(1)} %get-tuple-element.19), channel_id=1, source_target_pairs={{0,16},{16,32},{32,48},{48,64},{64,80},{80,96},{96,112},{112,128},... | collective-permute-start | bytes 196616 | tf_op jit(solution)/shard_map/ppermute | solution.py:21
  11.3 5.5 %reshape_broadcast_in_dim.7 = f32[2,2,4,2,256,2]{5,4,3,2,1,0:T(8,128)} reshape(f32[4,8,512]{2,1,0:T(8,128)S(1)} %get-tuple-element.32) | data formatting | bytes 131072 | tf_op jit(solution)/shard_map/reshape;broadcast_in_dim | solution.py:68
  19.3 5.5 %reshape_broadcast_in_dim.6 = f32[2,2,4,2,256,2]{5,4,3,2,1,0:T(8,128)} reshape(f32[4,8,512]{2,1,0:T(8,128)S(1)} %subtract_convert_fusion) | data formatting | bytes 131072 | tf_op jit(solution)/shard_map/reshape;broadcast_in_dim | solution.py:73
  29.2 4.6 %collective-permute-start.2 = (f32[4,6,1,512]{3,0,2,1:T(4,128)S(1)}, f32[4,6,1,512]{3,0,2,1:T(4,128)S(1)}, u32[]{:S(2)}, u32[]{:S(2)}) collective-permute-start(f32[4,6,1,512]{3,0,2,1:T(4,128)S(1)} %copy.831), channel_id=1, source_target_pairs={{0,1},{1,2},{2,3},{3,4},{4,5},{5,6},{6,7},{7,8},{8,9},{9,10},{10,1... | collective-permute-start | bytes 147464 | tf_op jit(solution)/shard_map/ppermute | solution.py:21
  39.3 13.9 %reshape.3575 = f32[3,2,2,4,2,256,2]{6,5,4,3,2,1,0:T(8,128)} reshape(f32[3,4,8,512]{3,2,1,0:T(8,128)S(1)} %fusion.28) | data formatting | bytes 393216 | tf_op jit(solution)/shard_map/reshape | solution.py:68
  53.2 5.5 %reduce_sum.43 = f32[3,2,4,256]{3,2,1,0:T(4,128)S(1)} reduce(f32[3,2,2,4,2,256,2]{6,5,4,3,2,1,0:T(8,128)} %reshape.3575, f32[]{:T(128)} %constant.30.clone.1), dimensions={2,4,6}, to_apply=%region_1.0 | reduce | flops 43008 | bytes 221188 | tf_op jit(solution)/shard_map/reduce_sum | solution.py:68
  58.8 7.5 %collective-permute-start.4 = (f32[4,1,4,256]{3,2,1,0:T(4,128)S(1)}, f32[4,1,4,256]{3,2,1,0:T(4,128)S(1)}, u32[]{:S(2)}, u32[]{:S(2)}) collective-permute-start(f32[4,1,4,256]{3,2,1,0:T(4,128)S(1)} %get-tuple-element.41), channel_id=1, source_target_pairs={{0,16},{16,32},{32,48},{48,64},{64,80},{80,96},{96,112},{112,128},... | collective-permute-start | bytes 49160 | tf_op jit(solution)/shard_map/ppermute | solution.py:21
  68.2 6.4 %collective-permute-done.5 = f32[4,1,4,256]{3,2,1,0:T(4,128)S(1)} collective-permute-done((f32[4,1,4,256]{3,2,1,0:T(4,128)S(1)}, f32[4,1,4,256]{3,2,1,0:T(4,128)S(1)}, u32[]{:S(2)}, u32[]{:S(2)}) %collective-permute-start.5) | collective-permute-done | bytes 16416 | tf_op jit(solution)/shard_map/ppermute | solution.py:23
  74.7 4.0 %collective-permute-start.6 = (f32[4,4,1,256]{3,2,1,0:T(1,128)S(1)}, f32[4,4,1,256]{3,2,1,0:T(1,128)S(1)}, u32[]{:S(2)}, u32[]{:S(2)}) collective-permute-start(f32[4,4,1,256]{3,2,1,0:T(1,128)S(1)} %get-tuple-element.30), channel_id=1, source_target_pairs={{0,1},{1,2},{2,3},{3,4},{4,5},{5,6},{6,7},{7,8},{8,9},{9,10},{10,1... | collective-permute-start | bytes 49160 | tf_op jit(solution)/shard_map/ppermute | solution.py:21
  80.2 3.6 %collective-permute-done.7 = f32[4,4,1,256]{3,2,1,0:T(1,128)S(1)} collective-permute-done((f32[4,4,1,256]{3,2,1,0:T(1,128)S(1)}, f32[4,4,1,256]{3,2,1,0:T(1,128)S(1)}, u32[]{:S(2)}, u32[]{:S(2)}) %collective-permute-start.7) | collective-permute-done | bytes 16416 | tf_op jit(solution)/shard_map/ppermute | solution.py:23
  87.8 7.0 %collective-permute-start.8 = (f32[4,1,2,128]{3,2,1,0:T(2,128)S(1)}, f32[4,1,2,128]{3,2,1,0:T(2,128)S(1)}, u32[]{:S(2)}, u32[]{:S(2)}) collective-permute-start(f32[4,1,2,128]{3,2,1,0:T(2,128)S(1)} %pad_maximum_fusion.42), channel_id=1, source_target_pairs={{0,16},{16,32},{32,48},{48,64},{64,80},{80,96},{96,112},{112,128},... | collective-permute-start | bytes 12296 | tf_op jit(solution)/shard_map/ppermute | solution.py:21
  95.6 5.2 %collective-permute-start.10 = (f32[4,3,1,128]{3,2,1,0:T(1,128)S(1)}, f32[4,3,1,128]{3,2,1,0:T(1,128)S(1)}, u32[]{:S(2)}, u32[]{:S(2)}) collective-permute-start(f32[4,3,1,128]{3,2,1,0:T(1,128)S(1)} %get-tuple-element.53), channel_id=1, source_target_pairs={{0,1},{1,2},{2,3},{3,4},{4,5},{5,6},{6,7},{7,8},{8,9},{9,10},{10,1... | collective-permute-start | bytes 18440 | tf_op jit(solution)/shard_map/ppermute | solution.py:21
  102.1 4.9 %collective-permute-done.11 = f32[4,3,1,128]{3,2,1,0:T(1,128)S(1)} collective-permute-done((f32[4,3,1,128]{3,2,1,0:T(1,128)S(1)}, f32[4,3,1,128]{3,2,1,0:T(1,128)S(1)}, u32[]{:S(2)}, u32[]{:S(2)}) %collective-permute-start.11) | collective-permute-done | bytes 6176 | tf_op jit(solution)/shard_map/ppermute | solution.py:23
  109.4 8.7 %collective-permute-start.12 = (f32[4,1,2,128]{3,2,1,0:T(2,128)S(1)}, f32[4,1,2,128]{3,2,1,0:T(2,128)S(1)}, u32[]{:S(2)}, u32[]{:S(2)}) collective-permute-start(f32[4,1,2,128]{3,2,1,0:T(2,128)S(1)} %pad_maximum_fusion.41), channel_id=1, source_target_pairs={{0,16},{16,32},{32,48},{48,64},{64,80},{80,96},{96,112},{112,128},... | collective-permute-start | bytes 12296 | tf_op jit(solution)/shard_map/ppermute | solution.py:21
  118.8 4.6 %collective-permute-start.14 = (f32[4,3,1,128]{3,2,1,0:T(1,128)S(1)}, f32[4,3,1,128]{3,2,1,0:T(1,128)S(1)}, u32[]{:S(2)}, u32[]{:S(2)}) collective-permute-start(f32[4,3,1,128]{3,2,1,0:T(1,128)S(1)} %get-tuple-element.49), channel_id=1, source_target_pairs={{0,1},{1,2},{2,3},{3,4},{4,5},{5,6},{6,7},{7,8},{8,9},{9,10},{10,1... | collective-permute-start | bytes 18440 | tf_op jit(solution)/shard_map/ppermute | solution.py:21
  130.5 8.7 %collective-permute-start.16 = (f32[4,1,2,128]{3,2,1,0:T(2,128)S(1)}, f32[4,1,2,128]{3,2,1,0:T(2,128)S(1)}, u32[]{:S(2)}, u32[]{:S(2)}) collective-permute-start(f32[4,1,2,128]{3,2,1,0:T(2,128)S(1)} %pad_maximum_fusion.40), channel_id=1, source_target_pairs={{0,16},{16,32},{32,48},{48,64},{64,80},{80,96},{96,112},{112,128},... | collective-permute-start | bytes 12296 | tf_op jit(solution)/shard_map/ppermute | solution.py:21
  139.9 3.8 %collective-permute-start.18 = (f32[4,3,1,128]{3,2,1,0:T(1,128)S(1)}, f32[4,3,1,128]{3,2,1,0:T(1,128)S(1)}, u32[]{:S(2)}, u32[]{:S(2)}) collective-permute-start(f32[4,3,1,128]{3,2,1,0:T(1,128)S(1)} %get-tuple-element.45), channel_id=1, source_target_pairs={{0,1},{1,2},{2,3},{3,4},{4,5},{5,6},{6,7},{7,8},{8,9},{9,10},{10,1... | collective-permute-start | bytes 18440 | tf_op jit(solution)/shard_map/ppermute | solution.py:21
  145.0 4.9 %collective-permute-done.19 = f32[4,3,1,128]{3,2,1,0:T(1,128)S(1)} collective-permute-done((f32[4,3,1,128]{3,2,1,0:T(1,128)S(1)}, f32[4,3,1,128]{3,2,1,0:T(1,128)S(1)}, u32[]{:S(2)}, u32[]{:S(2)}) %collective-permute-start.19) | collective-permute-done | bytes 6176 | tf_op jit(solution)/shard_map/ppermute | solution.py:23
  150.9 8.7 %collective-permute-start.20 = (f32[4,1,4,256]{3,2,1,0:T(4,128)S(1)}, f32[4,1,4,256]{3,2,1,0:T(4,128)S(1)}, u32[]{:S(2)}, u32[]{:S(2)}) collective-permute-start(f32[4,1,4,256]{3,2,1,0:T(4,128)S(1)} %get-tuple-element.37), channel_id=1, source_target_pairs={{0,16},{16,32},{32,48},{48,64},{64,80},{80,96},{96,112},{112,128},... | collective-permute-start | bytes 49160 | tf_op jit(solution)/shard_map/ppermute | solution.py:21
  161.5 6.4 %collective-permute-done.21 = f32[4,1,4,256]{3,2,1,0:T(4,128)S(1)} collective-permute-done((f32[4,1,4,256]{3,2,1,0:T(4,128)S(1)}, f32[4,1,4,256]{3,2,1,0:T(4,128)S(1)}, u32[]{:S(2)}, u32[]{:S(2)}) %collective-permute-start.21) | collective-permute-done | bytes 16416 | tf_op jit(solution)/shard_map/ppermute | solution.py:23
  168.0 4.8 %collective-permute-start.22 = (f32[4,4,1,256]{3,2,1,0:T(1,128)S(1)}, f32[4,4,1,256]{3,2,1,0:T(1,128)S(1)}, u32[]{:S(2)}, u32[]{:S(2)}) collective-permute-start(f32[4,4,1,256]{3,2,1,0:T(1,128)S(1)} %get-tuple-element.23), channel_id=1, source_target_pairs={{0,1},{1,2},{2,3},{3,4},{4,5},{5,6},{6,7},{7,8},{8,9},{9,10},{10,1... | collective-permute-start | bytes 49160 | tf_op jit(solution)/shard_map/ppermute | solution.py:21
  174.2 3.4 %collective-permute-done.23 = f32[4,4,1,256]{3,2,1,0:T(1,128)S(1)} collective-permute-done((f32[4,4,1,256]{3,2,1,0:T(1,128)S(1)}, f32[4,4,1,256]{3,2,1,0:T(1,128)S(1)}, u32[]{:S(2)}, u32[]{:S(2)}) %collective-permute-start.23) | collective-permute-done | bytes 16416 | tf_op jit(solution)/shard_map/ppermute | solution.py:23
  190.9 7.0 %collective-permute-done.25 = f32[4,1,8,512]{3,2,1,0:T(8,128)S(1)} collective-permute-done((f32[4,1,8,512]{3,2,1,0:T(8,128)S(1)}, f32[4,1,8,512]{3,2,1,0:T(8,128)S(1)}, u32[]{:S(2)}, u32[]{:S(2)}) %collective-permute-start.25) | collective-permute-done | bytes 65568 | tf_op jit(solution)/shard_map/ppermute | solution.py:23
  199.3 5.2 %collective-permute-start.26 = (f32[4,6,1,512]{3,0,2,1:T(4,128)S(1)}, f32[4,6,1,512]{3,0,2,1:T(4,128)S(1)}, u32[]{:S(2)}, u32[]{:S(2)}) collective-permute-start(f32[4,6,1,512]{3,0,2,1:T(4,128)S(1)} %copy.833), channel_id=1, source_target_pairs={{0,1},{1,2},{2,3},{3,4},{4,5},{5,6},{6,7},{7,8},{8,9},{9,10},{10,1... | collective-permute-start | bytes 147464 | tf_op jit(solution)/shard_map/ppermute | solution.py:21
  (157 shorter events, 64.7 us)
Async XLA Ops:
  2.0 25.7 %collective-permute-start = (f32[4,1,8,512]{3,2,1,0:T(8,128)S(1)}, f32[4,1,8,512]{3,2,1,0:T(8,128)S(1)}, u32[]{:S(2)}, u32[]{:S(2)}) collective-permute-start(f32[4,1,8,512]{3,2,1,0:T(8,128)S(1)} %get-tuple-element.19), channel_id=1, source_target_pairs={{0,16},{16,32},{32,48},{48,64},{64,80},{80,96},{96,112},{112,128},... | collective-permute-start | bytes 196616 | tf_op jit(solution)/shard_map/ppermute | solution.py:21
  6.9 20.9 %collective-permute-start.1 = (f32[4,1,8,512]{3,2,1,0:T(8,128)S(1)}, f32[4,1,8,512]{3,2,1,0:T(8,128)S(1)}, u32[]{:S(2)}, u32[]{:S(2)}) collective-permute-start(f32[4,1,8,512]{3,2,1,0:T(8,128)S(1)} %get-tuple-element.20), channel_id=1, source_target_pairs={{16,0},{32,16},{48,32},{64,48},{80,64},{96,80},{112,96},{128,112},... | collective-permute-start | bytes 196616 | tf_op jit(solution)/shard_map/ppermute | solution.py:23
  27.9 6.0 %collective-permute-start.3 = (f32[4,6,1,512]{3,0,2,1:T(4,128)S(1)}, f32[4,6,1,512]{3,0,2,1:T(4,128)S(1)}, u32[]{:S(2)}, u32[]{:S(2)}) collective-permute-start(f32[4,6,1,512]{3,0,2,1:T(4,128)S(1)} %copy.832), channel_id=1, source_target_pairs={{1,0},{2,1},{3,2},{4,3},{5,4},{6,5},{7,6},{8,7},{9,8},{10,9},{11,1... | collective-permute-start | bytes 147464 | tf_op jit(solution)/shard_map/ppermute | solution.py:23
  29.2 6.1 %collective-permute-start.2 = (f32[4,6,1,512]{3,0,2,1:T(4,128)S(1)}, f32[4,6,1,512]{3,0,2,1:T(4,128)S(1)}, u32[]{:S(2)}, u32[]{:S(2)}) collective-permute-start(f32[4,6,1,512]{3,0,2,1:T(4,128)S(1)} %copy.831), channel_id=1, source_target_pairs={{0,1},{1,2},{2,3},{3,4},{4,5},{5,6},{6,7},{7,8},{8,9},{9,10},{10,1... | collective-permute-start | bytes 147464 | tf_op jit(solution)/shard_map/ppermute | solution.py:21
  58.8 9.4 %collective-permute-start.4 = (f32[4,1,4,256]{3,2,1,0:T(4,128)S(1)}, f32[4,1,4,256]{3,2,1,0:T(4,128)S(1)}, u32[]{:S(2)}, u32[]{:S(2)}) collective-permute-start(f32[4,1,4,256]{3,2,1,0:T(4,128)S(1)} %get-tuple-element.41), channel_id=1, source_target_pairs={{0,16},{16,32},{32,48},{48,64},{64,80},{80,96},{96,112},{112,128},... | collective-permute-start | bytes 49160 | tf_op jit(solution)/shard_map/ppermute | solution.py:21
  66.3 8.4 %collective-permute-start.5 = (f32[4,1,4,256]{3,2,1,0:T(4,128)S(1)}, f32[4,1,4,256]{3,2,1,0:T(4,128)S(1)}, u32[]{:S(2)}, u32[]{:S(2)}) collective-permute-start(f32[4,1,4,256]{3,2,1,0:T(4,128)S(1)} %get-tuple-element.42), channel_id=1, source_target_pairs={{16,0},{32,16},{48,32},{64,48},{80,64},{96,80},{112,96},{128,112},... | collective-permute-start | bytes 49160 | tf_op jit(solution)/shard_map/ppermute | solution.py:23
  74.7 5.5 %collective-permute-start.6 = (f32[4,4,1,256]{3,2,1,0:T(1,128)S(1)}, f32[4,4,1,256]{3,2,1,0:T(1,128)S(1)}, u32[]{:S(2)}, u32[]{:S(2)}) collective-permute-start(f32[4,4,1,256]{3,2,1,0:T(1,128)S(1)} %get-tuple-element.30), channel_id=1, source_target_pairs={{0,1},{1,2},{2,3},{3,4},{4,5},{5,6},{6,7},{7,8},{8,9},{9,10},{10,1... | collective-permute-start | bytes 49160 | tf_op jit(solution)/shard_map/ppermute | solution.py:21
  85.9 8.9 %collective-permute-start.9 = (f32[4,1,2,128]{3,2,1,0:T(2,128)S(1)}, f32[4,1,2,128]{3,2,1,0:T(2,128)S(1)}, u32[]{:S(2)}, u32[]{:S(2)}) collective-permute-start(f32[4,1,2,128]{3,2,1,0:T(2,128)S(1)} %pad_maximum_fusion.42), channel_id=1, source_target_pairs={{16,0},{32,16},{48,32},{64,48},{80,64},{96,80},{112,96},{128,112},... | collective-permute-start | bytes 12296 | tf_op jit(solution)/shard_map/ppermute | solution.py:23
  87.8 7.7 %collective-permute-start.8 = (f32[4,1,2,128]{3,2,1,0:T(2,128)S(1)}, f32[4,1,2,128]{3,2,1,0:T(2,128)S(1)}, u32[]{:S(2)}, u32[]{:S(2)}) collective-permute-start(f32[4,1,2,128]{3,2,1,0:T(2,128)S(1)} %pad_maximum_fusion.42), channel_id=1, source_target_pairs={{0,16},{16,32},{32,48},{48,64},{64,80},{80,96},{96,112},{112,128},... | collective-permute-start | bytes 12296 | tf_op jit(solution)/shard_map/ppermute | solution.py:21
  95.6 6.5 %collective-permute-start.10 = (f32[4,3,1,128]{3,2,1,0:T(1,128)S(1)}, f32[4,3,1,128]{3,2,1,0:T(1,128)S(1)}, u32[]{:S(2)}, u32[]{:S(2)}) collective-permute-start(f32[4,3,1,128]{3,2,1,0:T(1,128)S(1)} %get-tuple-element.53), channel_id=1, source_target_pairs={{0,1},{1,2},{2,3},{3,4},{4,5},{5,6},{6,7},{7,8},{8,9},{9,10},{10,1... | collective-permute-start | bytes 18440 | tf_op jit(solution)/shard_map/ppermute | solution.py:21
  100.8 6.2 %collective-permute-start.11 = (f32[4,3,1,128]{3,2,1,0:T(1,128)S(1)}, f32[4,3,1,128]{3,2,1,0:T(1,128)S(1)}, u32[]{:S(2)}, u32[]{:S(2)}) collective-permute-start(f32[4,3,1,128]{3,2,1,0:T(1,128)S(1)} %get-tuple-element.54), channel_id=1, source_target_pairs={{1,0},{2,1},{3,2},{4,3},{5,4},{6,5},{7,6},{8,7},{9,8},{10,9},{11,1... | collective-permute-start | bytes 18440 | tf_op jit(solution)/shard_map/ppermute | solution.py:23
  107.5 10.6 %collective-permute-start.13 = (f32[4,1,2,128]{3,2,1,0:T(2,128)S(1)}, f32[4,1,2,128]{3,2,1,0:T(2,128)S(1)}, u32[]{:S(2)}, u32[]{:S(2)}) collective-permute-start(f32[4,1,2,128]{3,2,1,0:T(2,128)S(1)} %pad_maximum_fusion.41), channel_id=1, source_target_pairs={{16,0},{32,16},{48,32},{64,48},{80,64},{96,80},{112,96},{128,112},... | collective-permute-start | bytes 12296 | tf_op jit(solution)/shard_map/ppermute | solution.py:23
  109.4 9.4 %collective-permute-start.12 = (f32[4,1,2,128]{3,2,1,0:T(2,128)S(1)}, f32[4,1,2,128]{3,2,1,0:T(2,128)S(1)}, u32[]{:S(2)}, u32[]{:S(2)}) collective-permute-start(f32[4,1,2,128]{3,2,1,0:T(2,128)S(1)} %pad_maximum_fusion.41), channel_id=1, source_target_pairs={{0,16},{16,32},{32,48},{48,64},{64,80},{80,96},{96,112},{112,128},... | collective-permute-start | bytes 12296 | tf_op jit(solution)/shard_map/ppermute | solution.py:21
  118.8 5.9 %collective-permute-start.14 = (f32[4,3,1,128]{3,2,1,0:T(1,128)S(1)}, f32[4,3,1,128]{3,2,1,0:T(1,128)S(1)}, u32[]{:S(2)}, u32[]{:S(2)}) collective-permute-start(f32[4,3,1,128]{3,2,1,0:T(1,128)S(1)} %get-tuple-element.49), channel_id=1, source_target_pairs={{0,1},{1,2},{2,3},{3,4},{4,5},{5,6},{6,7},{7,8},{8,9},{9,10},{10,1... | collective-permute-start | bytes 18440 | tf_op jit(solution)/shard_map/ppermute | solution.py:21
  128.6 10.6 %collective-permute-start.17 = (f32[4,1,2,128]{3,2,1,0:T(2,128)S(1)}, f32[4,1,2,128]{3,2,1,0:T(2,128)S(1)}, u32[]{:S(2)}, u32[]{:S(2)}) collective-permute-start(f32[4,1,2,128]{3,2,1,0:T(2,128)S(1)} %pad_maximum_fusion.40), channel_id=1, source_target_pairs={{16,0},{32,16},{48,32},{64,48},{80,64},{96,80},{112,96},{128,112},... | collective-permute-start | bytes 12296 | tf_op jit(solution)/shard_map/ppermute | solution.py:23
  130.5 9.4 %collective-permute-start.16 = (f32[4,1,2,128]{3,2,1,0:T(2,128)S(1)}, f32[4,1,2,128]{3,2,1,0:T(2,128)S(1)}, u32[]{:S(2)}, u32[]{:S(2)}) collective-permute-start(f32[4,1,2,128]{3,2,1,0:T(2,128)S(1)} %pad_maximum_fusion.40), channel_id=1, source_target_pairs={{0,16},{16,32},{32,48},{48,64},{64,80},{80,96},{96,112},{112,128},... | collective-permute-start | bytes 12296 | tf_op jit(solution)/shard_map/ppermute | solution.py:21
  139.9 5.1 %collective-permute-start.18 = (f32[4,3,1,128]{3,2,1,0:T(1,128)S(1)}, f32[4,3,1,128]{3,2,1,0:T(1,128)S(1)}, u32[]{:S(2)}, u32[]{:S(2)}) collective-permute-start(f32[4,3,1,128]{3,2,1,0:T(1,128)S(1)} %get-tuple-element.45), channel_id=1, source_target_pairs={{0,1},{1,2},{2,3},{3,4},{4,5},{5,6},{6,7},{7,8},{8,9},{9,10},{10,1... | collective-permute-start | bytes 18440 | tf_op jit(solution)/shard_map/ppermute | solution.py:21
  143.7 6.2 %collective-permute-start.19 = (f32[4,3,1,128]{3,2,1,0:T(1,128)S(1)}, f32[4,3,1,128]{3,2,1,0:T(1,128)S(1)}, u32[]{:S(2)}, u32[]{:S(2)}) collective-permute-start(f32[4,3,1,128]{3,2,1,0:T(1,128)S(1)} %get-tuple-element.46), channel_id=1, source_target_pairs={{1,0},{2,1},{3,2},{4,3},{5,4},{6,5},{7,6},{8,7},{9,8},{10,9},{11,1... | collective-permute-start | bytes 18440 | tf_op jit(solution)/shard_map/ppermute | solution.py:23
  150.9 10.6 %collective-permute-start.20 = (f32[4,1,4,256]{3,2,1,0:T(4,128)S(1)}, f32[4,1,4,256]{3,2,1,0:T(4,128)S(1)}, u32[]{:S(2)}, u32[]{:S(2)}) collective-permute-start(f32[4,1,4,256]{3,2,1,0:T(4,128)S(1)} %get-tuple-element.37), channel_id=1, source_target_pairs={{0,16},{16,32},{32,48},{48,64},{64,80},{80,96},{96,112},{112,128},... | collective-permute-start | bytes 49160 | tf_op jit(solution)/shard_map/ppermute | solution.py:21
  159.6 8.4 %collective-permute-start.21 = (f32[4,1,4,256]{3,2,1,0:T(4,128)S(1)}, f32[4,1,4,256]{3,2,1,0:T(4,128)S(1)}, u32[]{:S(2)}, u32[]{:S(2)}) collective-permute-start(f32[4,1,4,256]{3,2,1,0:T(4,128)S(1)} %get-tuple-element.38), channel_id=1, source_target_pairs={{16,0},{32,16},{48,32},{64,48},{80,64},{96,80},{112,96},{128,112},... | collective-permute-start | bytes 49160 | tf_op jit(solution)/shard_map/ppermute | solution.py:23
  168.0 6.2 %collective-permute-start.22 = (f32[4,4,1,256]{3,2,1,0:T(1,128)S(1)}, f32[4,4,1,256]{3,2,1,0:T(1,128)S(1)}, u32[]{:S(2)}, u32[]{:S(2)}) collective-permute-start(f32[4,4,1,256]{3,2,1,0:T(1,128)S(1)} %get-tuple-element.23), channel_id=1, source_target_pairs={{0,1},{1,2},{2,3},{3,4},{4,5},{5,6},{6,7},{7,8},{8,9},{9,10},{10,1... | collective-permute-start | bytes 49160 | tf_op jit(solution)/shard_map/ppermute | solution.py:21
  189.0 8.9 %collective-permute-start.25 = (f32[4,1,8,512]{3,2,1,0:T(8,128)S(1)}, f32[4,1,8,512]{3,2,1,0:T(8,128)S(1)}, u32[]{:S(2)}, u32[]{:S(2)}) collective-permute-start(f32[4,1,8,512]{3,2,1,0:T(8,128)S(1)} %get-tuple-element.16), channel_id=1, source_target_pairs={{16,0},{32,16},{48,32},{64,48},{80,64},{96,80},{112,96},{128,112},... | collective-permute-start | bytes 196616 | tf_op jit(solution)/shard_map/ppermute | solution.py:23
  198.0 6.6 %collective-permute-start.27 = (f32[4,6,1,512]{3,0,2,1:T(4,128)S(1)}, f32[4,6,1,512]{3,0,2,1:T(4,128)S(1)}, u32[]{:S(2)}, u32[]{:S(2)}) collective-permute-start(f32[4,6,1,512]{3,0,2,1:T(4,128)S(1)} %copy.834), channel_id=1, source_target_pairs={{1,0},{2,1},{3,2},{4,3},{5,4},{6,5},{7,6},{8,7},{9,8},{10,9},{11,1... | collective-permute-start | bytes 147464 | tf_op jit(solution)/shard_map/ppermute | solution.py:23
  199.3 6.4 %collective-permute-start.26 = (f32[4,6,1,512]{3,0,2,1:T(4,128)S(1)}, f32[4,6,1,512]{3,0,2,1:T(4,128)S(1)}, u32[]{:S(2)}, u32[]{:S(2)}) collective-permute-start(f32[4,6,1,512]{3,0,2,1:T(4,128)S(1)} %copy.833), channel_id=1, source_target_pairs={{0,1},{1,2},{2,3},{3,4},{4,5},{5,6},{6,7},{7,8},{8,9},{9,10},{10,1... | collective-permute-start | bytes 147464 | tf_op jit(solution)/shard_map/ppermute | solution.py:21
  (11 other events, 86.0 us)
where the time goes:
time: 211 us; the launch traced here: 210 us
  starting transfers between devices  103 us (49%)
  waiting for transfers between devices  44.5 us (21%)
  local copies, waits for them, and re-layouts  34.1 us (16%)
  other arithmetic  27.4 us (13%)
    ppermute x14, starting transfers between devices, with_halo(): lax.ppermute(tail, axis, [(i, (i + 1) % count) for i in range(ends)])  80.7 us
    ppermute x14, waiting for transfers between devices, with_halo(): lax.ppermute(head, axis, [((i + 1) % count, i) for i in range(ends)])  40 us
    ppermute x14, starting transfers between devices, with_halo(): lax.ppermute(head, axis, [((i + 1) % count, i) for i in range(ends)])  22.7 us
    reshape x1, local copies, waits for them, and re-layouts, block_sum(): return field.reshape(k, a // 2, 2, b // 2, 2, c // 2, 2).sum(axis=(2, 4, 6))  13.9 us
    add x18, other arithmetic, stencil(): parts[first] = parts[first] + couple * term  9.61 us
    reduce_sum x6, other arithmetic, block_sum(): return field.reshape(k, a // 2, 2, b // 2, 2, c // 2, 2).sum(axis=(2, 4, 6))  8.38 us
    another operation x1, local copies, waits for them, and re-layouts, block_sum(): return field.reshape(k, a // 2, 2, b // 2, 2, c // 2, 2).sum(axis=(2, 4, 6))  5.51 us
    another operation x1, local copies, waits for them, and re-layouts, block_max(): return field.reshape(k, a // 2, 2, b // 2, 2, c // 2, 2).max(axis=(2, 4, 6))  5.5 us
  transfers between devices with their start and end apart: 28, of which 13 were waited for; matrix products, arithmetic and copies ran while one was open for 9% of the time, Pallas kernels for 0%

commit v1 on v0

v1 whole, which is shorter than its diff:
```python
import jax
import jax.numpy as jnp
from jax import lax
from jax.experimental import pallas as pl
from jax.experimental.pallas import tpu as pltpu
from jax.sharding import PartitionSpec as P

F32 = jnp.float32
VMEM = pl.BlockSpec(memory_space=pltpu.VMEM)
PARAMS = pltpu.CompilerParams(vmem_limit_bytes=48 * 1024 * 1024)


def iota(shape, dim):
    return lax.broadcasted_iota(jnp.int32, shape, dim)


def exact_dot(a, b):
    return jnp.dot(a, b, precision=lax.Precision.HIGHEST, preferred_element_type=F32)


def pool_matrix(n):
    shape = (n, n // 2)
    return (iota(shape, 0) // 2 == iota(shape, 1)).astype(F32)


def spread_matrix(n):
    shape = (n, 2 * n)
    return (iota(shape, 0) == iota(shape, 1) // 2).astype(F32)


def z_parts(tiles):
    t, d = [], []
    for a in tiles:
        n = a.shape[1]
        lane = iota(a.shape, 1)
        after = jnp.where(lane == n - 1, 0.0, pltpu.roll(a, n - 1, 1))
        before = jnp.where(lane == 0, 0.0, pltpu.roll(a, 1, 1))
        t.append((after + before) + 2.0 * a)
        d.append(after - before)
    return tuple(t), tuple(d)


def y_pair(tiles):
    a = tiles[0]
    n = a.shape[0]
    if len(tiles) == 1:
        return pltpu.roll(a, n - 1, 0), pltpu.roll(a, 1, 0)
    row = iota(a.shape, 0)
    after = pltpu.roll(jnp.where(row == 0, tiles[1], a), n - 1, 0)
    before = pltpu.roll(jnp.where(row == n - 1, tiles[1], a), 1, 0)
    return after, before


def y_t(tiles):
    after, before = y_pair(tiles)
    return (after + before) + 2.0 * tiles[0]


def y_d(tiles):
    after, before = y_pair(tiles)
    return after - before


def y_both(tiles):
    after, before = y_pair(tiles)
    return (after + before) + 2.0 * tiles[0], after - before


def plane_terms(v):
    (tx, dx), (ty, dy), (tz, dz) = [z_parts(c) for c in v]
    xt, xd = y_both(tx)
    xc = y_t(dx)
    yt, yd = y_both(ty)
    yc = y_d(dy)
    zt = y_t(tz)
    zb, zc = y_both(dz)
    return (
        (xt, yt + 0.25 * zc, zt + 0.25 * yc),
        (0.25 * (yd + zb), 0.25 * xd, 0.25 * xc),
    )


def scalar_terms(s):
    t, _ = z_parts(s)
    return y_t(t)


def times(a, b):
    return tuple(p * q for p, q in zip(a, b))


def stiff_sums(s, planes):
    terms = {p: scalar_terms(s[p]) for p in range(planes[0] - 1, planes[-1] + 2)}
    return {p: 2.0 * terms[p] + (terms[p + 1] + terms[p - 1]) for p in planes}


def stencil(v, s, sums, planes):
    own, scaled = {}, {}
    result = {}
    for p in range(planes[0] - 1, planes[-1] + 2):
        for store, field in ((own, v[p]), (scaled, [times(c, s[p]) for c in v[p]])):
            even, odd = plane_terms(field)
            store[p] = (
                [2.0 * e for e in even],
                [e + o for e, o in zip(even, odd)],
                [e - o for e, o in zip(even, odd)],
            )
        q = p - 1
        if q in planes:
            here = []
            for c in range(3):
                plain = own[q][0][c] + (own[q + 1][1][c] + own[q - 1][2][c])
                heavy = scaled[q][0][c] + (scaled[q + 1][1][c] + scaled[q - 1][2][c])
                u, k = v[q][c][0], s[q][0]
                here.append(8.1 * (k * u) + 0.125 * (u * sums[q] - (k * plain + heavy)))
            result[q] = here
    return result


def gain(stiff, free):
    return free * 0.8 / (7.1 * stiff + 7.5)


def prepare_kernel(density, fixed, loaded, load, fine, low_side, high_side):
    for p in range(4):
        level = (density[p].astype(F32) + 1.0) * (1.0 / 256.0)
        stiff = 0.05 + level * level * level
        free = (1 - fixed[p]).astype(F32)
        factor = gain(stiff, free) * loaded[p].astype(F32)
        values = [factor * load[c, p] for c in range(3)] + [stiff, free]
        for f in range(5):
            fine[f, p] = values[f]
            if p == 0:
                low_side[f] = values[f]
            if p == 3:
                high_side[f] = values[f]


def fine_tiles(fine, before, after, row_before, row_after):
    row = iota((8, fine.shape[3]), 0)
    result = []
    for p in range(6):
        here = []
        for f in range(5):
            main = before[f] if p == 0 else after[f] if p == 5 else fine[f, p - 1]
            rim = jnp.where(
                row == 0, row_after[f, pl.ds(p, 1), :], row_before[f, pl.ds(p, 1), :]
            )
            here.append((main, rim))
        result.append(here)
    return result


def fine_residual_kernel(fine, before, after, row_before, row_after, mid):
    tiles = fine_tiles(fine, before, after, row_before, row_after)
    v = [t[:3] for t in tiles]
    s = [t[3] for t in tiles]
    planes = range(1, 5)
    image = stencil(v, s, stiff_sums(s, planes), planes)
    rows = [[], [], [], [], []]
    for p in planes:
        stiff, free = s[p][0], tiles[p][4][0]
        back = 1.25 * (7.1 * stiff + 7.5)
        for c in range(3):
            rows[c].append(free * (back * v[p][c][0] - image[p][c]))
        rows[3].append(stiff)
        rows[4].append(free)
    pairs = []
    for f in range(5):
        pairs += [rows[f][0] + rows[f][1], rows[f][2] + rows[f][3]]
    wide = jnp.concatenate(pairs, axis=0)
    short = exact_dot(wide, pool_matrix(wide.shape[1]))
    shape = (40, 80)
    left = (iota(shape, 0) == iota(shape, 1) // 2).astype(F32)
    sums = exact_dot(left, short)
    mid[0:24] = sums[0:24]
    mid[24:32] = sums[24:32] * 0.125
    mid[32:40] = (sums[32:40] > 0.5).astype(F32)


def mid_fields(mid):
    v, s, free, gains = [], [], [], []
    for p in range(6):
        stiff, open_ = mid[3, p], mid[4, p]
        g = gain(stiff, open_)
        v.append([(0.5 * g * mid[c, p],) for c in range(3)])
        s.append((stiff,))
        free.append(open_)
        gains.append(g)
    return v, s, free, gains


def mid_residual_kernel(mid, low):
    v, s, free, _ = mid_fields(mid)
    planes = range(2, 4)
    image = stencil(v, s, stiff_sums(s, planes), planes)
    pairs = []
    for c in range(3):
        pairs.append(
            sum(free[p] * (mid[c, p] - 2.0 * image[p][c]) for p in planes)
        )
    pairs.append(s[2][0] + s[3][0])
    pairs.append(free[2] + free[3])
    wide = jnp.concatenate(pairs, axis=0)
    short = exact_dot(wide, pool_matrix(wide.shape[1]))
    shape = (10, 40)
    out, source = iota(shape, 0), iota(shape, 1)
    left = (source // 8 == out // 2) & (source % 8 // 2 == 1 + out % 2)
    sums = exact_dot(left.astype(F32), short)
    low[0:6] = sums[0:6]
    low[6:8] = sums[6:8] * 0.125
    low[8:10] = (sums[8:10] > 0.5).astype(F32)


def finish_kernel(low, mid, fine, before, after, row_before, row_after, out):
    s = [(low[3, p],) for p in range(9)]
    gains = [gain(low[3, p], low[4, p]) for p in range(9)]
    first = [[0.25 * gains[p] * low[c, p] for c in range(3)] for p in range(9)]
    v = {p: [(c,) for c in first[p]] for p in range(9)}
    sums = stiff_sums(s, range(1, 8))
    for reach in (1, 2, 3):
        planes = range(reach, 9 - reach)
        image = stencil(v, s, sums, planes)
        v = {
            p: [
                (v[p][c][0] + first[p][c] - gains[p] * image[p][c],) for c in range(3)
            ]
            for p in planes
        }
    wide = jnp.concatenate([v[p][c][0] for c in range(3) for p in (3, 4, 5)], axis=0)
    shape = (72, 144)
    to, source = iota(shape, 0), iota(shape, 1)
    left = (source // 16 == to // 8) & (source % 16 == 3 + to % 8 // 2)
    raised = exact_dot(exact_dot(left.astype(F32), wide), spread_matrix(wide.shape[1]))
    first, s, free, gains = mid_fields(mid)
    v = []
    for p in range(6):
        here = []
        for c in range(3):
            at = (c * 3 + p // 2) * 8
            here.append((first[p][c][0] + free[p] * raised[at : at + 8],))
        v.append(here)
    planes = range(1, 5)
    image = stencil(v, s, stiff_sums(s, planes), planes)
    wide = jnp.concatenate(
        [
            v[p][c][0] + first[p][c][0] - gains[p] * image[p][c]
            for c in range(3)
            for p in planes
        ],
        axis=0,
    )
    shape = (192, 96)
    to, source = iota(shape, 0), iota(shape, 1)
    inner = to % 16
    row = jnp.where(inner < 8, 2 + inner // 2, jnp.where(inner == 8, 6, 1))
    left = (source // 8 == to // 16) & (source % 8 == row)
    raised = exact_dot(exact_dot(left.astype(F32), wide), spread_matrix(wide.shape[1]))
    tiles = fine_tiles(fine, before, after, row_before, row_after)
    s = [t[3] for t in tiles]
    v = []
    for p in range(6):
        here = []
        for c in range(3):
            at = (c * 4 + (p + 1) // 2) * 16
            here.append(
                tuple(
                    tiles[p][c][k]
                    + tiles[p][4][k] * raised[at + 8 * k : at + 8 * k + 8]
                    for k in range(2)
                )
            )
        v.append(here)
    image = stencil(v, s, stiff_sums(s, planes), planes)
    for p in planes:
        g = gain(s[p][0], tiles[p][4][0])
        for c in range(3):
            out[c, p - 1] = v[p][c][0] + tiles[p][c][0] - g * image[p][c]


def call(kernel, shapes, *args):
    outs = [jax.ShapeDtypeStruct(shape, F32) for shape in shapes]
    return pl.pallas_call(
        kernel,
        out_shape=outs if len(outs) > 1 else outs[0],
        in_specs=[VMEM] * len(args),
        out_specs=[VMEM] * len(outs) if len(outs) > 1 else VMEM,
        compiler_params=PARAMS,
    )(*args)


def up(value, axis):
    n = lax.axis_size(axis)
    return lax.ppermute(value, axis, [(i, i + 1) for i in range(n - 1)])


def down(value, axis):
    n = lax.axis_size(axis)
    return lax.ppermute(value, axis, [(i + 1, i) for i in range(n - 1)])


def both_sides(low, high, axis):
    n = lax.axis_size(axis)
    even = lax.axis_index(axis) % 2 == 0
    inner = lax.ppermute(
        jnp.where(even, high, low), axis, [(i, i ^ 1) for i in range(n)]
    )
    outer = lax.ppermute(
        jnp.where(even, low, high),
        axis,
        [(i, ((i + 1) ^ 1) - 1) for i in range(1, n - 1)],
    )
    return jnp.where(even, outer, inner), jnp.where(even, inner, outer)


def gather_x(low):
    n = lax.axis_size("gx")
    groups = [[8 * g + i for i in range(8)] for g in range(n // 8)]
    row = lax.all_to_all(
        jnp.broadcast_to(low[None], (8,) + low.shape),
        "gx",
        0,
        0,
        axis_index_groups=groups,
    )
    place = lax.axis_index("gx") % 8
    first = place < 4
    moves = [(j, j + 8) for j in range(n - 8) if j % 8 < 4]
    moves += [(j, j - 8) for j in range(8, n) if j % 8 >= 4]
    other = lax.ppermute(jnp.where(first, row[4:], row[:4]), "gx", moves)
    planes = jnp.where(
        first, jnp.concatenate([other, row]), jnp.concatenate([row, other])
    )
    return lax.dynamic_slice_in_dim(planes, place % 4, 9, 0)


def per_device(density, fixed, loaded, load):
    nz = density.shape[2]
    fine, low_side, high_side = call(
        prepare_kernel,
        [(5, 4, 8, nz), (5, 8, nz), (5, 8, nz)],
        density,
        fixed,
        loaded,
        load,
    )
    before, after = both_sides(low_side, high_side, "gx")

    def edge(row):
        return jnp.concatenate(
            [before[:, None, row], fine[:, :, row], after[:, None, row]], axis=1
        )

    rims = (up(edge(7), "gy"), down(edge(0), "gy"))
    fine_args = (fine, before, after, *rims)
    mid = call(fine_residual_kernel, [(40, nz // 2)], *fine_args)

    sides = both_sides(mid, mid, "gx")
    shape = (5, 2, 4, nz // 2)
    mid = jnp.concatenate([a.reshape(shape) for a in (sides[0], mid, sides[1])], axis=1)
    rows_before = up(mid[:, :, 2:].reshape(60, nz // 2), "gy")
    rows_after = down(mid[:, :, :2].reshape(60, nz // 2), "gy")
    shape = (5, 6, 2, nz // 2)
    mid = jnp.concatenate(
        [rows_before.reshape(shape), mid, rows_after.reshape(shape)], axis=2
    )
    low = call(mid_residual_kernel, [(10, nz // 4)], mid)

    low = gather_x(low).reshape(90, nz // 4)
    near = up(low, "gy"), down(low, "gy")
    far = [up(near[0], "gy"), near[0], low, near[1], down(near[1], "gy")]
    low = jnp.stack(far).reshape(5, 9, 5, 2, nz // 4)
    low = low.transpose(2, 1, 0, 3, 4).reshape(5, 9, 10, nz // 4)
    low = jnp.pad(low, ((0, 0), (0, 0), (0, 6), (0, 0)))
    return call(finish_kernel, [(3, 4, 8, nz)], low, mid, *fine_args)


def solution(mesh):
    return jax.shard_map(
        per_device,
        mesh=mesh,
        in_specs=(
            P("gx", "gy", None),
            P("gx", "gy", None),
            P("gx", "gy", None),
            P(None, "gx", "gy", None),
        ),
        out_specs=P(None, "gx", "gy", None),
        check_vma=False,
    )
```

time: 211 us -> 91.7 us (0.43)
  the two profiles are of different devices: /device:TPU:31 before, /device:TPU:480 now
where the time goes in v1:
time: 91.7 us; the launch traced here: 91 us
  starting transfers between devices  46 us (50%)
  waiting for transfers between devices  32.7 us (36%)
  Pallas kernels  6.55 us (7%)
  local copies, waits for them, and re-layouts  5.11 us (6%)
    ppermute x4, starting transfers between devices, up(): return lax.ppermute(value, axis, [(i, i + 1) for i in range(n - 1)])  21.3 us
    ppermute x4, waiting for transfers between devices, down(): return lax.ppermute(value, axis, [(i + 1, i) for i in range(n - 1)])  10.9 us
    ppermute x2, waiting for transfers between devices, both_sides(): lax.ppermute(jnp.where(even, low, high), axis, [(i, (i + 1 ^ 1) - 1) for...  9.54 us
    ppermute x2, starting transfers between devices, both_sides(): lax.ppermute(jnp.where(even, low, high), axis, [(i, (i + 1 ^ 1) - 1) for...  7.88 us
    ppermute x4, starting transfers between devices, down(): return lax.ppermute(value, axis, [(i + 1, i) for i in range(n - 1)])  7.68 us
    pallas_call x4, Pallas kernels, call(): pl.pallas_call(kernel, out_shape=outs if len(outs) > 1 else outs[0], in_s...  6.55 us
    all_to_all x1, waiting for transfers between devices, gather_x(): lax.all_to_all(jnp.broadcast_to(low[None], (8,) + low.shape), 'gx', 0, 0,...  5.53 us
    ppermute x1, waiting for transfers between devices, gather_x(): other = lax.ppermute(jnp.where(first, row[4:], row[:4]), 'gx', moves)  5.07 us
  transfers between devices with their start and end apart: 14, of which 9 were waited for; matrix products, arithmetic and copies ran while one was open for 1% of the time, Pallas kernels for 0%

profile of v1, /device:TPU:480, one launch (start us, length us, event | category | flops | bytes accessed | tf_op | source)
XLA Modules:
  0.0 91.0 jit_solution(2449958431319146877)
XLA Ops:
  0.0 0.9 %copy-done = f32[3,4,8,512]{3,2,1,0:T(8,128)S(1)} copy-done((f32[3,4,8,512]{3,2,1,0:T(8,128)S(1)}, f32[3,4,8,512]{3,2,1,0:T(8,128)}, u32[]{:S(2)}) %copy-start) | copy-done | bytes 196632
  3.5 1.9 %collective-permute-start.1 = (f32[5,8,512]{2,1,0:T(8,128)S(1)}, f32[5,8,512]{2,1,0:T(8,128)S(1)}, u32[]{:S(2)}, u32[]{:S(2)}) collective-permute-start(f32[5,8,512]{2,1,0:T(8,128)S(1)} %get-tuple-element.15), channel_id=1, source_target_pairs={{0,16},{16,0},{32,48},{48,32},{64,80},{80,64},{96,112},{112,96},{1... | collective-permute-start | bytes 245768 | tf_op jit(solution)/shard_map/ppermute | solution.py:305
  5.5 4.7 %collective-permute-start = (f32[5,8,512]{2,1,0:T(8,128)S(1)}, f32[5,8,512]{2,1,0:T(8,128)S(1)}, u32[]{:S(2)}, u32[]{:S(2)}) collective-permute-start(f32[5,8,512]{2,1,0:T(8,128)S(1)} %get-tuple-element.16), channel_id=1, source_target_pairs={{16,32},{32,16},{48,64},{64,48},{80,96},{96,80},{112,128},{128,112... | collective-permute-start | bytes 245768 | tf_op jit(solution)/shard_map/ppermute | solution.py:308
  10.4 4.2 %collective-permute-done = f32[5,8,512]{2,1,0:T(8,128)S(1)} collective-permute-done((f32[5,8,512]{2,1,0:T(8,128)S(1)}, f32[5,8,512]{2,1,0:T(8,128)S(1)}, u32[]{:S(2)}, u32[]{:S(2)}) %collective-permute-start) | collective-permute-done | bytes 81952 | tf_op jit(solution)/shard_map/ppermute | solution.py:308
  14.6 5.5 %collective-permute-start.2 = (f32[5,6,512]{2,1,0:T(8,128)S(1)}, f32[5,6,512]{2,1,0:T(8,128)S(1)}, u32[]{:S(2)}, u32[]{:S(2)}) collective-permute-start(f32[5,6,512]{2,1,0:T(8,128)S(1)} %pad_maximum_fusion.1), channel_id=1, source_target_pairs={{0,1},{1,2},{2,3},{3,4},{4,5},{5,6},{6,7},{7,8},{8,9},{9,10},{10,1... | collective-permute-start | bytes 184328 | tf_op jit(solution)/shard_map/ppermute | solution.py:294
  20.2 1.9 %collective-permute-start.3 = (f32[5,6,512]{2,1,0:T(8,128)S(1)}, f32[5,6,512]{2,1,0:T(8,128)S(1)}, u32[]{:S(2)}, u32[]{:S(2)}) collective-permute-start(f32[5,6,512]{2,1,0:T(8,128)S(1)} %pad_maximum_fusion.2), channel_id=1, source_target_pairs={{1,0},{2,1},{3,2},{4,3},{5,4},{6,5},{7,6},{8,7},{9,8},{10,9},{11,1... | collective-permute-start | bytes 184328 | tf_op jit(solution)/shard_map/ppermute | solution.py:299
  22.2 5.5 %collective-permute-done.3.row_after = f32[5,6,512]{2,1,0:T(8,128)S(1)} collective-permute-done((f32[5,6,512]{2,1,0:T(8,128)S(1)}, f32[5,6,512]{2,1,0:T(8,128)S(1)}, u32[]{:S(2)}, u32[]{:S(2)}) %collective-permute-start.3) | collective-permute-done | bytes 61472 | tf_op jit(solution)/shard_map/ppermute | solution.py:299
  27.7 1.7 %shard_map.47 = f32[40,256]{1,0:T(8,128)S(1)} custom-call(f32[5,4,8,512]{3,2,1,0:T(8,128)S(1)} %get-tuple-element.8.fine, f32[5,8,512]{2,1,0:T(8,128)S(1)} %get-tuple-element.14.before, f32[5,8,512]{2,1,0:T(8,128)S(1)} %get-tuple-element.13.after, f32[5,6,512]{2,1,0:T(8,128)S(1)} %collective-permute-done.2.row_before, ...), custom_call_target="tpu_custom_call" | custom-call | tf_op jit(solution)/shard_map/pallas_call | solution.py:283
  29.4 1.9 %collective-permute-start.5 = (f32[40,256]{1,0:T(8,128)S(1)}, f32[40,256]{1,0:T(8,128)S(1)}, u32[]{:S(2)}, u32[]{:S(2)}) collective-permute-start(f32[40,256]{1,0:T(8,128)S(1)} %shard_map.47), channel_id=1, source_target_pairs={{0,16},{16,0},{32,48},{48,32},{64,80},{80,64},{96,112},{112,96},{1... | collective-permute-start | bytes 122888 | tf_op jit(solution)/shard_map/ppermute | solution.py:305
  31.3 3.2 %collective-permute-start.4 = (f32[40,256]{1,0:T(8,128)S(1)}, f32[40,256]{1,0:T(8,128)S(1)}, u32[]{:S(2)}, u32[]{:S(2)}) collective-permute-start(f32[40,256]{1,0:T(8,128)S(1)} %shard_map.47), channel_id=1, source_target_pairs={{16,32},{32,16},{48,64},{64,48},{80,96},{96,80},{112,128},{128,112... | collective-permute-start | bytes 122888 | tf_op jit(solution)/shard_map/ppermute | solution.py:308
  34.6 5.4 %collective-permute-done.4 = f32[40,256]{1,0:T(8,128)S(1)} collective-permute-done((f32[40,256]{1,0:T(8,128)S(1)}, f32[40,256]{1,0:T(8,128)S(1)}, u32[]{:S(2)}, u32[]{:S(2)}) %collective-permute-start.4) | collective-permute-done | bytes 40992 | tf_op jit(solution)/shard_map/ppermute | solution.py:308
  40.1 1.9 %collective-permute-start.7 = (f32[60,256]{1,0:T(8,128)S(1)}, f32[60,256]{1,0:T(8,128)S(1)}, u32[]{:S(2)}, u32[]{:S(2)}) collective-permute-start(f32[60,256]{1,0:T(8,128)S(1)} %reshape.44), channel_id=1, source_target_pairs={{1,0},{2,1},{3,2},{4,3},{5,4},{6,5},{7,6},{8,7},{9,8},{10,9},{11,1... | collective-permute-start | bytes 184328 | tf_op jit(solution)/shard_map/ppermute | solution.py:299
  42.1 5.1 %collective-permute-start.6 = (f32[60,256]{1,0:T(8,128)S(1)}, f32[60,256]{1,0:T(8,128)S(1)}, u32[]{:S(2)}, u32[]{:S(2)}) collective-permute-start(f32[60,256]{1,0:T(8,128)S(1)} %reshape.42), channel_id=1, source_target_pairs={{0,1},{1,2},{2,3},{3,4},{4,5},{5,6},{6,7},{7,8},{8,9},{9,10},{10,1... | collective-permute-start | bytes 184328 | tf_op jit(solution)/shard_map/ppermute | solution.py:294
  47.6 1.6 %collective-permute-done.6 = f32[60,256]{1,0:T(8,128)S(1)} collective-permute-done((f32[60,256]{1,0:T(8,128)S(1)}, f32[60,256]{1,0:T(8,128)S(1)}, u32[]{:S(2)}, u32[]{:S(2)}) %collective-permute-start.6) | collective-permute-done | bytes 61472 | tf_op jit(solution)/shard_map/ppermute | solution.py:294
  50.6 3.4 %all-to-all-start = ((f32[8,10,128]{2,1,0:T(8,128)}), f32[8,10,128]{2,1,0:T(8,128)S(1)}, u32[]{:S(2)}, u32[]{:S(2)}) async-start(f32[8,10,128]{2,1,0:T(8,128)} %broadcast_in_dim.2), calls=%async_computation | async-start | bytes 131072 | tf_op jit(solution)/shard_map/all_to_all | solution.py:319
  53.9 5.5 %all-to-all-done = f32[8,10,128]{2,1,0:T(8,128)S(1)} async-done(((f32[8,10,128]{2,1,0:T(8,128)}), f32[8,10,128]{2,1,0:T(8,128)S(1)}, u32[]{:S(2)}, u32[]{:S(2)}) %all-to-all-start) | async-done | bytes 40992 | tf_op jit(solution)/shard_map/all_to_all | solution.py:319
  59.5 1.9 %collective-permute-start.8 = (f32[4,10,128]{2,1,0:T(8,128)S(1)}, f32[4,10,128]{2,1,0:T(8,128)S(1)}, u32[]{:S(2)}, u32[]{:S(2)}) collective-permute-start(f32[4,10,128]{2,1,0:T(8,128)S(1)} %slice_select_fusion), channel_id=1, source_target_pairs={{0,128},{16,144},{32,160},{48,176},{128,256},{144,272},{160,288},{... | collective-permute-start | bytes 61448 | tf_op jit(solution)/shard_map/ppermute | solution.py:330
  61.4 5.1 %collective-permute-done.8 = f32[4,10,128]{2,1,0:T(8,128)S(1)} collective-permute-done((f32[4,10,128]{2,1,0:T(8,128)S(1)}, f32[4,10,128]{2,1,0:T(8,128)S(1)}, u32[]{:S(2)}, u32[]{:S(2)}) %collective-permute-start.8) | collective-permute-done | bytes 20512 | tf_op jit(solution)/shard_map/ppermute | solution.py:330
  66.5 5.5 %collective-permute-start.9 = (f32[90,128]{1,0:T(8,128)S(1)}, f32[90,128]{1,0:T(8,128)S(1)}, u32[]{:S(2)}, u32[]{:S(2)}) collective-permute-start(f32[90,128]{1,0:T(8,128)S(1)} %reshape.46), channel_id=1, source_target_pairs={{0,1},{1,2},{2,3},{3,4},{4,5},{5,6},{6,7},{7,8},{8,9},{9,10},{10,1... | collective-permute-start | bytes 138248 | tf_op jit(solution)/shard_map/ppermute | solution.py:294
  72.0 1.9 %collective-permute-start.11 = (f32[90,128]{1,0:T(8,128)S(1)}, f32[90,128]{1,0:T(8,128)S(1)}, u32[]{:S(2)}, u32[]{:S(2)}) collective-permute-start(f32[90,128]{1,0:T(8,128)S(1)} %reshape.46), channel_id=1, source_target_pairs={{1,0},{2,1},{3,2},{4,3},{5,4},{6,5},{7,6},{8,7},{9,8},{10,9},{11,1... | collective-permute-start | bytes 138248 | tf_op jit(solution)/shard_map/ppermute | solution.py:299
  73.9 5.2 %collective-permute-start.10 = (f32[90,128]{1,0:T(8,128)S(1)}, f32[90,128]{1,0:T(8,128)S(1)}, u32[]{:S(2)}, u32[]{:S(2)}) collective-permute-start(f32[90,128]{1,0:T(8,128)S(1)} %collective-permute-done.9), channel_id=1, source_target_pairs={{0,1},{1,2},{2,3},{3,4},{4,5},{5,6},{6,7},{7,8},{8,9},{9,10},{10,1... | collective-permute-start | bytes 138248 | tf_op jit(solution)/shard_map/ppermute | solution.py:294
  79.3 1.9 %collective-permute-start.12 = (f32[90,128]{1,0:T(8,128)S(1)}, f32[90,128]{1,0:T(8,128)S(1)}, u32[]{:S(2)}, u32[]{:S(2)}) collective-permute-start(f32[90,128]{1,0:T(8,128)S(1)} %collective-permute-done.11), channel_id=1, source_target_pairs={{1,0},{2,1},{3,2},{4,3},{5,4},{6,5},{7,6},{8,7},{9,8},{10,9},{11,1... | collective-permute-start | bytes 138248 | tf_op jit(solution)/shard_map/ppermute | solution.py:299
  81.4 5.1 %collective-permute-done.12 = f32[90,128]{1,0:T(8,128)S(1)} collective-permute-done((f32[90,128]{1,0:T(8,128)S(1)}, f32[90,128]{1,0:T(8,128)S(1)}, u32[]{:S(2)}, u32[]{:S(2)}) %collective-permute-start.12) | collective-permute-done | bytes 46112 | tf_op jit(solution)/shard_map/ppermute | solution.py:299
  86.8 4.2 %shard_map.49 = f32[3,4,8,512]{3,2,1,0:T(8,128)} custom-call(f32[5,9,16,128]{3,2,1,0:T(8,128)S(1)} %pad.4.low, f32[5,6,8,256]{3,2,1,0:T(8,128)S(1)} %pad_maximum_fusion.mid, f32[5,4,8,512]{3,2,1,0:T(8,128)S(1)} %get-tuple-element.8.fine, f32[5,8,512]{2,1,0:T(8,128)S(1)} %get-tuple-element.14.before, f32[5,8,512]{2,1,0:T(8,128)S(1)} %get-tuple-element.13.after, ...), custom_call_target="tpu_custom_call" | custom-call | tf_op jit(solution)/shard_map/pallas_call | solution.py:283
  (53 shorter events, 5.4 us)
Async XLA Ops:
  0.0 0.9 %copy-start = (f32[3,4,8,512]{3,2,1,0:T(8,128)S(1)}, f32[3,4,8,512]{3,2,1,0:T(8,128)}, u32[]{:S(2)}) copy-start(f32[3,4,8,512]{3,2,1,0:T(8,128)} %load.1) | copy-start | bytes 589828
  0.9 0.8 copy-start.1
  1.8 0.8 copy-start.2
  2.6 0.8 copy-start.3
  3.5 6.8 %collective-permute-start.1 = (f32[5,8,512]{2,1,0:T(8,128)S(1)}, f32[5,8,512]{2,1,0:T(8,128)S(1)}, u32[]{:S(2)}, u32[]{:S(2)}) collective-permute-start(f32[5,8,512]{2,1,0:T(8,128)S(1)} %get-tuple-element.15), channel_id=1, source_target_pairs={{0,16},{16,0},{32,48},{48,32},{64,80},{80,64},{96,112},{112,96},{1... | collective-permute-start | bytes 245768 | tf_op jit(solution)/shard_map/ppermute | solution.py:305
  5.5 9.1 %collective-permute-start = (f32[5,8,512]{2,1,0:T(8,128)S(1)}, f32[5,8,512]{2,1,0:T(8,128)S(1)}, u32[]{:S(2)}, u32[]{:S(2)}) collective-permute-start(f32[5,8,512]{2,1,0:T(8,128)S(1)} %get-tuple-element.16), channel_id=1, source_target_pairs={{16,32},{32,16},{48,64},{64,48},{80,96},{96,80},{112,128},{128,112... | collective-permute-start | bytes 245768 | tf_op jit(solution)/shard_map/ppermute | solution.py:308
  14.6 7.5 %collective-permute-start.2 = (f32[5,6,512]{2,1,0:T(8,128)S(1)}, f32[5,6,512]{2,1,0:T(8,128)S(1)}, u32[]{:S(2)}, u32[]{:S(2)}) collective-permute-start(f32[5,6,512]{2,1,0:T(8,128)S(1)} %pad_maximum_fusion.1), channel_id=1, source_target_pairs={{0,1},{1,2},{2,3},{3,4},{4,5},{5,6},{6,7},{7,8},{8,9},{9,10},{10,1... | collective-permute-start | bytes 184328 | tf_op jit(solution)/shard_map/ppermute | solution.py:294
  20.2 7.5 %collective-permute-start.3 = (f32[5,6,512]{2,1,0:T(8,128)S(1)}, f32[5,6,512]{2,1,0:T(8,128)S(1)}, u32[]{:S(2)}, u32[]{:S(2)}) collective-permute-start(f32[5,6,512]{2,1,0:T(8,128)S(1)} %pad_maximum_fusion.2), channel_id=1, source_target_pairs={{1,0},{2,1},{3,2},{4,3},{5,4},{6,5},{7,6},{8,7},{9,8},{10,9},{11,1... | collective-permute-start | bytes 184328 | tf_op jit(solution)/shard_map/ppermute | solution.py:299
  29.4 5.2 %collective-permute-start.5 = (f32[40,256]{1,0:T(8,128)S(1)}, f32[40,256]{1,0:T(8,128)S(1)}, u32[]{:S(2)}, u32[]{:S(2)}) collective-permute-start(f32[40,256]{1,0:T(8,128)S(1)} %shard_map.47), channel_id=1, source_target_pairs={{0,16},{16,0},{32,48},{48,32},{64,80},{80,64},{96,112},{112,96},{1... | collective-permute-start | bytes 122888 | tf_op jit(solution)/shard_map/ppermute | solution.py:305
  31.3 8.6 %collective-permute-start.4 = (f32[40,256]{1,0:T(8,128)S(1)}, f32[40,256]{1,0:T(8,128)S(1)}, u32[]{:S(2)}, u32[]{:S(2)}) collective-permute-start(f32[40,256]{1,0:T(8,128)S(1)} %shard_map.47), channel_id=1, source_target_pairs={{16,32},{32,16},{48,64},{64,48},{80,96},{96,80},{112,128},{128,112... | collective-permute-start | bytes 122888 | tf_op jit(solution)/shard_map/ppermute | solution.py:308
  40.1 7.4 %collective-permute-start.7 = (f32[60,256]{1,0:T(8,128)S(1)}, f32[60,256]{1,0:T(8,128)S(1)}, u32[]{:S(2)}, u32[]{:S(2)}) collective-permute-start(f32[60,256]{1,0:T(8,128)S(1)} %reshape.44), channel_id=1, source_target_pairs={{1,0},{2,1},{3,2},{4,3},{5,4},{6,5},{7,6},{8,7},{9,8},{10,9},{11,1... | collective-permute-start | bytes 184328 | tf_op jit(solution)/shard_map/ppermute | solution.py:299
  42.1 7.0 %collective-permute-start.6 = (f32[60,256]{1,0:T(8,128)S(1)}, f32[60,256]{1,0:T(8,128)S(1)}, u32[]{:S(2)}, u32[]{:S(2)}) collective-permute-start(f32[60,256]{1,0:T(8,128)S(1)} %reshape.42), channel_id=1, source_target_pairs={{0,1},{1,2},{2,3},{3,4},{4,5},{5,6},{6,7},{7,8},{8,9},{9,10},{10,1... | collective-permute-start | bytes 184328 | tf_op jit(solution)/shard_map/ppermute | solution.py:294
  50.6 8.9 %all-to-all-start = ((f32[8,10,128]{2,1,0:T(8,128)}), f32[8,10,128]{2,1,0:T(8,128)S(1)}, u32[]{:S(2)}, u32[]{:S(2)}) async-start(f32[8,10,128]{2,1,0:T(8,128)} %broadcast_in_dim.2), calls=%async_computation | async-start | bytes 131072 | tf_op jit(solution)/shard_map/all_to_all | solution.py:319
  59.5 7.0 %collective-permute-start.8 = (f32[4,10,128]{2,1,0:T(8,128)S(1)}, f32[4,10,128]{2,1,0:T(8,128)S(1)}, u32[]{:S(2)}, u32[]{:S(2)}) collective-permute-start(f32[4,10,128]{2,1,0:T(8,128)S(1)} %slice_select_fusion), channel_id=1, source_target_pairs={{0,128},{16,144},{32,160},{48,176},{128,256},{144,272},{160,288},{... | collective-permute-start | bytes 61448 | tf_op jit(solution)/shard_map/ppermute | solution.py:330
  66.5 7.4 %collective-permute-start.9 = (f32[90,128]{1,0:T(8,128)S(1)}, f32[90,128]{1,0:T(8,128)S(1)}, u32[]{:S(2)}, u32[]{:S(2)}) collective-permute-start(f32[90,128]{1,0:T(8,128)S(1)} %reshape.46), channel_id=1, source_target_pairs={{0,1},{1,2},{2,3},{3,4},{4,5},{5,6},{6,7},{7,8},{8,9},{9,10},{10,1... | collective-permute-start | bytes 138248 | tf_op jit(solution)/shard_map/ppermute | solution.py:294
  72.0 7.2 %collective-permute-start.11 = (f32[90,128]{1,0:T(8,128)S(1)}, f32[90,128]{1,0:T(8,128)S(1)}, u32[]{:S(2)}, u32[]{:S(2)}) collective-permute-start(f32[90,128]{1,0:T(8,128)S(1)} %reshape.46), channel_id=1, source_target_pairs={{1,0},{2,1},{3,2},{4,3},{5,4},{6,5},{7,6},{8,7},{9,8},{10,9},{11,1... | collective-permute-start | bytes 138248 | tf_op jit(solution)/shard_map/ppermute | solution.py:299
  73.9 7.3 %collective-permute-start.10 = (f32[90,128]{1,0:T(8,128)S(1)}, f32[90,128]{1,0:T(8,128)S(1)}, u32[]{:S(2)}, u32[]{:S(2)}) collective-permute-start(f32[90,128]{1,0:T(8,128)S(1)} %collective-permute-done.9), channel_id=1, source_target_pairs={{0,1},{1,2},{2,3},{3,4},{4,5},{5,6},{6,7},{7,8},{8,9},{9,10},{10,1... | collective-permute-start | bytes 138248 | tf_op jit(solution)/shard_map/ppermute | solution.py:294
  79.3 7.2 %collective-permute-start.12 = (f32[90,128]{1,0:T(8,128)S(1)}, f32[90,128]{1,0:T(8,128)S(1)}, u32[]{:S(2)}, u32[]{:S(2)}) collective-permute-start(f32[90,128]{1,0:T(8,128)S(1)} %collective-permute-done.11), channel_id=1, source_target_pairs={{1,0},{2,1},{3,2},{4,3},{5,4},{6,5},{7,6},{8,7},{9,8},{10,9},{11,1... | collective-permute-start | bytes 138248 | tf_op jit(solution)/shard_map/ppermute | solution.py:299

commit v2 on v1

--- a/solution.py
+++ b/solution.py
@@ -121,8 +121,17 @@
     return free * 0.8 / (7.1 * stiff + 7.5)
 
 
-def prepare_kernel(density, fixed, loaded, load, fine, low_side, high_side):
-    for p in range(4):
+def prepare_kernel(density, fixed, loaded, load, fine, low_side, high_side, *scratch):
+    copies = [
+        pltpu.make_async_copy(source, scratch[k], scratch[4].at[k])
+        for k, source in enumerate((density, fixed, loaded, load))
+    ]
+    for copy in copies:
+        copy.start()
+    for copy in copies:
+        copy.wait()
+    density, fixed, loaded, load = scratch[:4]
+    for p in (0, 3, 1, 2):
         level = (density[p].astype(F32) + 1.0) * (1.0 / 256.0)
         stiff = 0.05 + level * level * level
         free = (1 - fixed[p]).astype(F32)
@@ -207,30 +216,38 @@
     out, source = iota(shape, 0), iota(shape, 1)
     left = (source // 8 == out // 2) & (source % 8 // 2 == 1 + out % 2)
     sums = exact_dot(left.astype(F32), short)
-    low[0:6] = sums[0:6]
-    low[6:8] = sums[6:8] * 0.125
-    low[8:10] = (sums[8:10] > 0.5).astype(F32)
+    row = iota(sums.shape, 0)
+    values = jnp.where(
+        row < 6, sums, jnp.where(row < 8, sums * 0.125, (sums > 0.5).astype(F32))
+    )
+    for k in range(low.shape[0]):
+        low[k] = values
 
 
 def finish_kernel(low, mid, fine, before, after, row_before, row_after, out):
-    s = [(low[3, p],) for p in range(9)]
-    gains = [gain(low[3, p], low[4, p]) for p in range(9)]
-    first = [[0.25 * gains[p] * low[c, p] for c in range(3)] for p in range(9)]
-    v = {p: [(c,) for c in first[p]] for p in range(9)}
+    parts = [slice(0, 8), slice(8, 16)]
+    s = [tuple(low[3, p, k] for k in parts) for p in range(9)]
+    gains = [tuple(gain(low[3, p, k], low[4, p, k]) for k in parts) for p in range(9)]
+    first = [
+        [tuple(0.25 * gains[p][k] * low[c, p, parts[k]] for k in range(2)) for c in range(3)]
+        for p in range(9)
+    ]
+    v = dict(enumerate(first))
     sums = stiff_sums(s, range(1, 8))
     for reach in (1, 2, 3):
         planes = range(reach, 9 - reach)
         image = stencil(v, s, sums, planes)
         v = {
             p: [
-                (v[p][c][0] + first[p][c] - gains[p] * image[p][c],) for c in range(3)
+                (v[p][c][0] + first[p][c][0] - gains[p][0] * image[p][c],)
+                for c in range(3)
             ]
             for p in planes
         }
     wide = jnp.concatenate([v[p][c][0] for c in range(3) for p in (3, 4, 5)], axis=0)
-    shape = (72, 144)
+    shape = (72, 72)
     to, source = iota(shape, 0), iota(shape, 1)
-    left = (source // 16 == to // 8) & (source % 16 == 3 + to % 8 // 2)
+    left = (source // 8 == to // 8) & (source % 8 == 2 + to % 8 // 2)
     raised = exact_dot(exact_dot(left.astype(F32), wide), spread_matrix(wide.shape[1]))
     first, s, free, gains = mid_fields(mid)
     v = []
@@ -278,100 +295,103 @@
             out[c, p - 1] = v[p][c][0] + tiles[p][c][0] - g * image[p][c]
 
 
-def call(kernel, shapes, *args):
+def call(kernel, shapes, *args, space=pltpu.VMEM, scratch=()):
     outs = [jax.ShapeDtypeStruct(shape, F32) for shape in shapes]
     return pl.pallas_call(
         kernel,
         out_shape=outs if len(outs) > 1 else outs[0],
-        in_specs=[VMEM] * len(args),
+        in_specs=[pl.BlockSpec(memory_space=space)] * len(args),
         out_specs=[VMEM] * len(outs) if len(outs) > 1 else VMEM,
+        scratch_shapes=list(scratch),
         compiler_params=PARAMS,
     )(*args)
 
 
-def up(value, axis):
+def inner_swap(value, axis):
+    return lax.ppermute(value, axis, [(i, i ^ 1) for i in range(lax.axis_size(axis))])
+
+
+def outer_swap(value, axis):
     n = lax.axis_size(axis)
-    return lax.ppermute(value, axis, [(i, i + 1) for i in range(n - 1)])
-
-
-def down(value, axis):
-    n = lax.axis_size(axis)
-    return lax.ppermute(value, axis, [(i + 1, i) for i in range(n - 1)])
+    return lax.ppermute(
+        value, axis, [(i, ((i + 1) ^ 1) - 1) for i in range(1, n - 1)]
+    )
 
 
 def both_sides(low, high, axis):
-    n = lax.axis_size(axis)
     even = lax.axis_index(axis) % 2 == 0
-    inner = lax.ppermute(
-        jnp.where(even, high, low), axis, [(i, i ^ 1) for i in range(n)]
-    )
-    outer = lax.ppermute(
-        jnp.where(even, low, high),
-        axis,
-        [(i, ((i + 1) ^ 1) - 1) for i in range(1, n - 1)],
-    )
+    outer = outer_swap(jnp.where(even, low, high), axis)
+    inner = inner_swap(jnp.where(even, high, low), axis)
     return jnp.where(even, outer, inner), jnp.where(even, inner, outer)
 
 
-def gather_x(low):
-    n = lax.axis_size("gx")
-    groups = [[8 * g + i for i in range(8)] for g in range(n // 8)]
-    row = lax.all_to_all(
-        jnp.broadcast_to(low[None], (8,) + low.shape),
-        "gx",
-        0,
-        0,
-        axis_index_groups=groups,
-    )
+def gather_low(low):
+    nx, ny = lax.axis_size("gx"), lax.axis_size("gy")
+    nz = low.shape[2]
+    groups = [
+        [(8 * g + i) * ny + 2 * h + j for i in range(8) for j in range(2)]
+        for g in range(nx // 8)
+        for h in range(ny // 2)
+    ]
+    row = lax.all_to_all(low, ("gx", "gy"), 0, 0, axis_index_groups=groups)
     place = lax.axis_index("gx") % 8
     first = place < 4
-    moves = [(j, j + 8) for j in range(n - 8) if j % 8 < 4]
-    moves += [(j, j - 8) for j in range(8, n) if j % 8 >= 4]
-    other = lax.ppermute(jnp.where(first, row[4:], row[:4]), "gx", moves)
+    moves = [(j, j + 8) for j in range(nx - 8) if j % 8 < 4]
+    moves += [(j, j - 8) for j in range(8, nx) if j % 8 >= 4]
+    other = lax.ppermute(jnp.where(first, row[8:], row[:8]), "gx", moves)
     planes = jnp.where(
         first, jnp.concatenate([other, row]), jnp.concatenate([row, other])
     )
-    return lax.dynamic_slice_in_dim(planes, place % 4, 9, 0)
+    pair = lax.dynamic_slice_in_dim(planes, place % 4 * 2, 18, 0)
+    even = lax.axis_index("gy") % 2 == 0
+    beside = outer_swap(pair.reshape(180, nz), "gy").reshape(9, 2, 10, nz)
+    beyond = jnp.where(even, beside[:, 1], beside[:, 0]).reshape(90, nz)
+    beyond = inner_swap(beyond, "gy").reshape(9, 1, 10, nz)
+    pair = pair.reshape(9, 2, 10, nz)
+    return jnp.where(
+        even,
+        jnp.concatenate([beside, pair, beyond], axis=1),
+        jnp.concatenate([beyond, pair, beside], axis=1),
+    )
 
 
 def per_device(density, fixed, loaded, load):
     nz = density.shape[2]
+    args = (density, fixed, loaded, load)
     fine, low_side, high_side = call(
         prepare_kernel,
         [(5, 4, 8, nz), (5, 8, nz), (5, 8, nz)],
-        density,
-        fixed,
-        loaded,
-        load,
+        *args,
+        space=pl.ANY,
+        scratch=[pltpu.VMEM(a.shape, a.dtype) for a in args]
+        + [pltpu.SemaphoreType.DMA((4,))],
     )
     before, after = both_sides(low_side, high_side, "gx")
 
     def edge(row):
-        return jnp.concatenate(
-            [before[:, None, row], fine[:, :, row], after[:, None, row]], axis=1
-        )
-
-    rims = (up(edge(7), "gy"), down(edge(0), "gy"))
+        planes = [before[:, None, row], fine[:, :, row], after[:, None, row]]
+        return jnp.concatenate(planes, axis=1).reshape(30, nz)
+
+    rims = [r.reshape(5, 6, nz) for r in both_sides(edge(0), edge(7), "gy")]
     fine_args = (fine, before, after, *rims)
     mid = call(fine_residual_kernel, [(40, nz // 2)], *fine_args)
 
     sides = both_sides(mid, mid, "gx")
     shape = (5, 2, 4, nz // 2)
     mid = jnp.concatenate([a.reshape(shape) for a in (sides[0], mid, sides[1])], axis=1)
-    rows_before = up(mid[:, :, 2:].reshape(60, nz // 2), "gy")
-    rows_after = down(mid[:, :, :2].reshape(60, nz // 2), "gy")
+    rows_before, rows_after = both_sides(
+        mid[:, :, :2].reshape(60, nz // 2), mid[:, :, 2:].reshape(60, nz // 2), "gy"
+    )
     shape = (5, 6, 2, nz // 2)
     mid = jnp.concatenate(
         [rows_before.reshape(shape), mid, rows_after.reshape(shape)], axis=2
     )
-    low = call(mid_residual_kernel, [(10, nz // 4)], mid)
-
-    low = gather_x(low).reshape(90, nz // 4)
-    near = up(low, "gy"), down(low, "gy")
-    far = [up(near[0], "gy"), near[0], low, near[1], down(near[1], "gy")]
-    low = jnp.stack(far).reshape(5, 9, 5, 2, nz // 4)
-    low = low.transpose(2, 1, 0, 3, 4).reshape(5, 9, 10, nz // 4)
-    low = jnp.pad(low, ((0, 0), (0, 0), (0, 6), (0, 0)))
+    low = call(mid_residual_kernel, [(16, 10, nz // 4)], mid)
+    low = gather_low(low).reshape(9, 5, 5, 2, nz // 4)
+    low = low.transpose(2, 0, 1, 3, 4).reshape(5, 9, 10, nz // 4)
+    low = jnp.concatenate(
+        [low[:, :, 1:], jnp.zeros((5, 9, 6, nz // 4), F32), low[:, :, :1]], axis=2
+    )
     return call(finish_kernel, [(3, 4, 8, nz)], low, mid, *fine_args)
 
 

time: 91.7 us -> 89.2 us (0.973)
  the two profiles are of different devices: /device:TPU:480 before, /device:TPU:160 now
where the time goes in v2:
time: 89.2 us; the launch traced here: 88.6 us
  starting transfers between devices  41.4 us (46%)
  waiting for transfers between devices  34 us (38%)
  Pallas kernels  7.56 us (8%)
  local copies, waits for them, and re-layouts  4.54 us (5%)
    ppermute x5, starting transfers between devices, inner_swap(): lax.ppermute(value, axis, [(i, i ^ 1) for i in range(lax.axis_size(axis))])  21.5 us
    ppermute x5, waiting for transfers between devices, outer_swap(): lax.ppermute(value, axis, [(i, (i + 1 ^ 1) - 1) for i in range(1, n - 1)])  17.7 us
    ppermute x5, starting transfers between devices, outer_swap(): lax.ppermute(value, axis, [(i, (i + 1 ^ 1) - 1) for i in range(1, n - 1)])  13.9 us
    pallas_call x4, Pallas kernels, call(): pl.pallas_call(kernel, out_shape=outs if len(outs) > 1 else outs[0], in_s...  7.56 us
    all_to_all x1, waiting for transfers between devices, gather_low(): row = lax.all_to_all(low, ('gx', 'gy'), 0, 0, axis_index_groups=groups)  6.57 us
    ppermute x1, waiting for transfers between devices, gather_low(): other = lax.ppermute(jnp.where(first, row[8:], row[:8]), 'gx', moves)  5.42 us
    ppermute x5, waiting for transfers between devices, inner_swap(): lax.ppermute(value, axis, [(i, i ^ 1) for i in range(lax.axis_size(axis))])  4.38 us
    all_to_all x1, starting transfers between devices, gather_low(): row = lax.all_to_all(low, ('gx', 'gy'), 0, 0, axis_index_groups=groups)  4.11 us
  transfers between devices with their start and end apart: 12, of which 9 were waited for; matrix products, arithmetic and copies ran while one was open for 1% of the time, Pallas kernels for 0%

profile of v2, /device:TPU:160, one launch (start us, length us, event | category | flops | bytes accessed | tf_op | source)
XLA Modules:
  0.0 88.6 jit_solution(9492527273533339211)
XLA Ops:
  0.0 0.9 %copy-done = f32[3,4,8,512]{3,2,1,0:T(8,128)S(1)} copy-done((f32[3,4,8,512]{3,2,1,0:T(8,128)S(1)}, f32[3,4,8,512]{3,2,1,0:T(8,128)}, u32[]{:S(2)}) %copy-start) | copy-done | bytes 196632
  4.0 1.9 %collective-permute-start.1 = (f32[5,8,512]{2,1,0:T(8,128)S(1)}, f32[5,8,512]{2,1,0:T(8,128)S(1)}, u32[]{:S(2)}, u32[]{:S(2)}) collective-permute-start(f32[5,8,512]{2,1,0:T(8,128)S(1)} %get-tuple-element.13), channel_id=1, source_target_pairs={{0,16},{16,0},{32,48},{48,32},{64,80},{80,64},{96,112},{112,96},{1... | collective-permute-start | bytes 245768 | tf_op jit(solution)/shard_map/ppermute | solution.py:311
  6.0 4.7 %collective-permute-start = (f32[5,8,512]{2,1,0:T(8,128)S(1)}, f32[5,8,512]{2,1,0:T(8,128)S(1)}, u32[]{:S(2)}, u32[]{:S(2)}) collective-permute-start(f32[5,8,512]{2,1,0:T(8,128)S(1)} %get-tuple-element.14), channel_id=1, source_target_pairs={{16,32},{32,16},{48,64},{64,48},{80,96},{96,80},{112,128},{128,112... | collective-permute-start | bytes 245768 | tf_op jit(solution)/shard_map/ppermute | solution.py:316
  11.0 4.1 %collective-permute-done = f32[5,8,512]{2,1,0:T(8,128)S(1)} collective-permute-done((f32[5,8,512]{2,1,0:T(8,128)S(1)}, f32[5,8,512]{2,1,0:T(8,128)S(1)}, u32[]{:S(2)}, u32[]{:S(2)}) %collective-permute-start) | collective-permute-done | bytes 81952 | tf_op jit(solution)/shard_map/ppermute | solution.py:316
  15.2 1.9 %collective-permute-start.2 = (f32[30,512]{1,0:T(8,128)S(1)}, f32[30,512]{1,0:T(8,128)S(1)}, u32[]{:S(2)}, u32[]{:S(2)}) collective-permute-start(f32[30,512]{1,0:T(8,128)S(1)} %select_n.174), channel_id=1, source_target_pairs={{1,2},{2,1},{3,4},{4,3},{5,6},{6,5},{7,8},{8,7},{9,10},{10,9},{11,... | collective-permute-start | bytes 184328 | tf_op jit(solution)/shard_map/ppermute | solution.py:316
  17.1 7.9 %collective-permute-start.3 = (f32[30,512]{1,0:T(8,128)S(1)}, f32[30,512]{1,0:T(8,128)S(1)}, u32[]{:S(2)}, u32[]{:S(2)}) collective-permute-start(f32[30,512]{1,0:T(8,128)S(1)} %select_n.176), channel_id=1, source_target_pairs={{0,1},{1,0},{2,3},{3,2},{4,5},{5,4},{6,7},{7,6},{8,9},{9,8},{10,11... | collective-permute-start | bytes 184328 | tf_op jit(solution)/shard_map/ppermute | solution.py:311
  25.0 2.2 %collective-permute-done.3 = f32[30,512]{1,0:T(8,128)S(1)} collective-permute-done((f32[30,512]{1,0:T(8,128)S(1)}, f32[30,512]{1,0:T(8,128)S(1)}, u32[]{:S(2)}, u32[]{:S(2)}) %collective-permute-start.3) | collective-permute-done | bytes 61472 | tf_op jit(solution)/shard_map/ppermute | solution.py:311
  27.3 1.7 %shard_map.47 = f32[40,256]{1,0:T(8,128)S(1)} custom-call(f32[5,4,8,512]{3,2,1,0:T(8,128)S(1)} %get-tuple-element.8.fine, f32[5,8,512]{2,1,0:T(8,128)S(1)} %get-tuple-element.12.before, f32[5,8,512]{2,1,0:T(8,128)S(1)} %get-tuple-element.11.after, f32[5,6,512]{2,1,0:T(8,128)S(1)} %reshape.62.row_before, f32[5,6,512]{2,1,0:T(8,128)S(1)} %reshape.63.row_after), custom_call_target="tpu_custom_call" | custom-call | tf_op jit(solution)/shard_map/pallas_call | solution.py:300
  28.9 1.9 %collective-permute-start.5 = (f32[40,256]{1,0:T(8,128)S(1)}, f32[40,256]{1,0:T(8,128)S(1)}, u32[]{:S(2)}, u32[]{:S(2)}) collective-permute-start(f32[40,256]{1,0:T(8,128)S(1)} %shard_map.47), channel_id=1, source_target_pairs={{0,16},{16,0},{32,48},{48,32},{64,80},{80,64},{96,112},{112,96},{1... | collective-permute-start | bytes 122888 | tf_op jit(solution)/shard_map/ppermute | solution.py:311
  30.9 3.5 %collective-permute-start.4 = (f32[40,256]{1,0:T(8,128)S(1)}, f32[40,256]{1,0:T(8,128)S(1)}, u32[]{:S(2)}, u32[]{:S(2)}) collective-permute-start(f32[40,256]{1,0:T(8,128)S(1)} %shard_map.47), channel_id=1, source_target_pairs={{16,32},{32,16},{48,64},{64,48},{80,96},{96,80},{112,128},{128,112... | collective-permute-start | bytes 122888 | tf_op jit(solution)/shard_map/ppermute | solution.py:316
  34.4 5.1 %collective-permute-done.4 = f32[40,256]{1,0:T(8,128)S(1)} collective-permute-done((f32[40,256]{1,0:T(8,128)S(1)}, f32[40,256]{1,0:T(8,128)S(1)}, u32[]{:S(2)}, u32[]{:S(2)}) %collective-permute-start.4) | collective-permute-done | bytes 40992 | tf_op jit(solution)/shard_map/ppermute | solution.py:316
  39.8 3.9 %collective-permute-start.7 = (f32[60,256]{1,0:T(8,128)S(1)}, f32[60,256]{1,0:T(8,128)S(1)}, u32[]{:S(2)}, u32[]{:S(2)}) collective-permute-start(f32[60,256]{1,0:T(8,128)S(1)} %select_n.184), channel_id=1, source_target_pairs={{0,1},{1,0},{2,3},{3,2},{4,5},{5,4},{6,7},{7,6},{8,9},{9,8},{10,11... | collective-permute-start | bytes 184328 | tf_op jit(solution)/shard_map/ppermute | solution.py:311
  43.7 1.9 %collective-permute-start.6 = (f32[60,256]{1,0:T(8,128)S(1)}, f32[60,256]{1,0:T(8,128)S(1)}, u32[]{:S(2)}, u32[]{:S(2)}) collective-permute-start(f32[60,256]{1,0:T(8,128)S(1)} %select_n.182), channel_id=1, source_target_pairs={{1,2},{2,1},{3,4},{4,3},{5,6},{6,5},{7,8},{8,7},{9,10},{10,9},{11,... | collective-permute-start | bytes 184328 | tf_op jit(solution)/shard_map/ppermute | solution.py:316
  45.9 3.9 %collective-permute-done.6 = f32[60,256]{1,0:T(8,128)S(1)} collective-permute-done((f32[60,256]{1,0:T(8,128)S(1)}, f32[60,256]{1,0:T(8,128)S(1)}, u32[]{:S(2)}, u32[]{:S(2)}) %collective-permute-start.6) | collective-permute-done | bytes 61472 | tf_op jit(solution)/shard_map/ppermute | solution.py:316
  50.0 1.3 %shard_map.48 = f32[16,10,128]{2,1,0:T(8,128)} custom-call(f32[5,6,8,256]{3,2,1,0:T(8,128)S(1)} %pad_maximum_fusion.1.mid), custom_call_target="tpu_custom_call" | custom-call | tf_op jit(solution)/shard_map/pallas_call | solution.py:300
  51.3 4.1 %all-to-all-start = ((f32[16,10,128]{2,1,0:T(8,128)}), f32[16,10,128]{2,1,0:T(8,128)S(1)}, u32[]{:S(2)}, u32[]{:S(2)}) async-start(f32[16,10,128]{2,1,0:T(8,128)} %shard_map.48), calls=%async_computation | async-start | bytes 262144 | tf_op jit(solution)/shard_map/all_to_all | solution.py:336
  55.5 6.6 %all-to-all-done = f32[16,10,128]{2,1,0:T(8,128)S(1)} async-done(((f32[16,10,128]{2,1,0:T(8,128)}), f32[16,10,128]{2,1,0:T(8,128)S(1)}, u32[]{:S(2)}, u32[]{:S(2)}) %all-to-all-start) | async-done | bytes 81952 | tf_op jit(solution)/shard_map/all_to_all | solution.py:336
  62.1 1.9 %collective-permute-start.8 = (f32[8,10,128]{2,1,0:T(8,128)S(1)}, f32[8,10,128]{2,1,0:T(8,128)S(1)}, u32[]{:S(2)}, u32[]{:S(2)}) collective-permute-start(f32[8,10,128]{2,1,0:T(8,128)S(1)} %slice_select_fusion.1), channel_id=1, source_target_pairs={{0,128},{16,144},{32,160},{48,176},{128,256},{144,272},{160,288},{... | collective-permute-start | bytes 122888 | tf_op jit(solution)/shard_map/ppermute | solution.py:341
  64.0 5.4 %collective-permute-done.8 = f32[8,10,128]{2,1,0:T(8,128)S(1)} collective-permute-done((f32[8,10,128]{2,1,0:T(8,128)S(1)}, f32[8,10,128]{2,1,0:T(8,128)S(1)}, u32[]{:S(2)}, u32[]{:S(2)}) %collective-permute-start.8) | collective-permute-done | bytes 40992 | tf_op jit(solution)/shard_map/ppermute | solution.py:341
  69.5 1.9 %collective-permute-start.9 = (f32[180,128]{1,0:T(8,128)S(1)}, f32[180,128]{1,0:T(8,128)S(1)}, u32[]{:S(2)}, u32[]{:S(2)}) collective-permute-start(f32[180,128]{1,0:T(8,128)S(1)} %reshape.69), channel_id=1, source_target_pairs={{1,2},{2,1},{3,4},{4,3},{5,6},{6,5},{7,8},{8,7},{9,10},{10,9},{11,... | collective-permute-start | bytes 276488 | tf_op jit(solution)/shard_map/ppermute | solution.py:316
  71.4 4.5 %collective-permute-done.9 = f32[180,128]{1,0:T(8,128)S(1)} collective-permute-done((f32[180,128]{1,0:T(8,128)S(1)}, f32[180,128]{1,0:T(8,128)S(1)}, u32[]{:S(2)}, u32[]{:S(2)}) %collective-permute-start.9) | collective-permute-done | bytes 92192 | tf_op jit(solution)/shard_map/ppermute | solution.py:316
  76.0 5.8 %collective-permute-start.10 = (f32[90,128]{1,0:T(8,128)S(1)}, f32[90,128]{1,0:T(8,128)S(1)}, u32[]{:S(2)}, u32[]{:S(2)}) collective-permute-start(f32[90,128]{1,0:T(8,128)S(1)} %select_n.193), channel_id=1, source_target_pairs={{0,1},{1,0},{2,3},{3,2},{4,5},{5,4},{6,7},{7,6},{8,9},{9,8},{10,11... | collective-permute-start | bytes 138248 | tf_op jit(solution)/shard_map/ppermute | solution.py:311
  82.1 1.9 %collective-permute-done.10 = f32[90,128]{1,0:T(8,128)S(1)} collective-permute-done((f32[90,128]{1,0:T(8,128)S(1)}, f32[90,128]{1,0:T(8,128)S(1)}, u32[]{:S(2)}, u32[]{:S(2)}) %collective-permute-start.10) | collective-permute-done | bytes 46112 | tf_op jit(solution)/shard_map/ppermute | solution.py:311
  84.5 4.1 %shard_map.49 = f32[3,4,8,512]{3,2,1,0:T(8,128)} custom-call(f32[5,9,16,128]{3,2,1,0:T(8,128)S(1)} %pad_maximum_fusion.low, f32[5,6,8,256]{3,2,1,0:T(8,128)S(1)} %pad_maximum_fusion.1.mid, f32[5,4,8,512]{3,2,1,0:T(8,128)S(1)} %get-tuple-element.8.fine, f32[5,8,512]{2,1,0:T(8,128)S(1)} %get-tuple-element.12.before, f32[5,8,512]{2,1,0:T(8,128)S(1)} %get-tuple-element.11.after, ...), custom_call_target="tpu_custom_call" | custom-call | tf_op jit(solution)/shard_map/pallas_call | solution.py:300
  (56 shorter events, 5.0 us)
Async XLA Ops:
  0.0 0.9 %copy-start = (f32[3,4,8,512]{3,2,1,0:T(8,128)S(1)}, f32[3,4,8,512]{3,2,1,0:T(8,128)}, u32[]{:S(2)}) copy-start(f32[3,4,8,512]{3,2,1,0:T(8,128)} %load.1) | copy-start | bytes 589828
  0.9 0.8 copy-start.1
  1.8 0.8 copy-start.2
  2.6 0.8 copy-start.3
  4.0 6.9 %collective-permute-start.1 = (f32[5,8,512]{2,1,0:T(8,128)S(1)}, f32[5,8,512]{2,1,0:T(8,128)S(1)}, u32[]{:S(2)}, u32[]{:S(2)}) collective-permute-start(f32[5,8,512]{2,1,0:T(8,128)S(1)} %get-tuple-element.13), channel_id=1, source_target_pairs={{0,16},{16,0},{32,48},{48,32},{64,80},{80,64},{96,112},{112,96},{1... | collective-permute-start | bytes 245768 | tf_op jit(solution)/shard_map/ppermute | solution.py:311
  6.0 9.1 %collective-permute-start = (f32[5,8,512]{2,1,0:T(8,128)S(1)}, f32[5,8,512]{2,1,0:T(8,128)S(1)}, u32[]{:S(2)}, u32[]{:S(2)}) collective-permute-start(f32[5,8,512]{2,1,0:T(8,128)S(1)} %get-tuple-element.14), channel_id=1, source_target_pairs={{16,32},{32,16},{48,64},{64,48},{80,96},{96,80},{112,128},{128,112... | collective-permute-start | bytes 245768 | tf_op jit(solution)/shard_map/ppermute | solution.py:316
  15.2 9.8 %collective-permute-start.2 = (f32[30,512]{1,0:T(8,128)S(1)}, f32[30,512]{1,0:T(8,128)S(1)}, u32[]{:S(2)}, u32[]{:S(2)}) collective-permute-start(f32[30,512]{1,0:T(8,128)S(1)} %select_n.174), channel_id=1, source_target_pairs={{1,2},{2,1},{3,4},{4,3},{5,6},{6,5},{7,8},{8,7},{9,10},{10,9},{11,... | collective-permute-start | bytes 184328 | tf_op jit(solution)/shard_map/ppermute | solution.py:316
  17.1 10.1 %collective-permute-start.3 = (f32[30,512]{1,0:T(8,128)S(1)}, f32[30,512]{1,0:T(8,128)S(1)}, u32[]{:S(2)}, u32[]{:S(2)}) collective-permute-start(f32[30,512]{1,0:T(8,128)S(1)} %select_n.176), channel_id=1, source_target_pairs={{0,1},{1,0},{2,3},{3,2},{4,5},{5,4},{6,7},{7,6},{8,9},{9,8},{10,11... | collective-permute-start | bytes 184328 | tf_op jit(solution)/shard_map/ppermute | solution.py:311
  28.9 5.5 %collective-permute-start.5 = (f32[40,256]{1,0:T(8,128)S(1)}, f32[40,256]{1,0:T(8,128)S(1)}, u32[]{:S(2)}, u32[]{:S(2)}) collective-permute-start(f32[40,256]{1,0:T(8,128)S(1)} %shard_map.47), channel_id=1, source_target_pairs={{0,16},{16,0},{32,48},{48,32},{64,80},{80,64},{96,112},{112,96},{1... | collective-permute-start | bytes 122888 | tf_op jit(solution)/shard_map/ppermute | solution.py:311
  30.9 8.6 %collective-permute-start.4 = (f32[40,256]{1,0:T(8,128)S(1)}, f32[40,256]{1,0:T(8,128)S(1)}, u32[]{:S(2)}, u32[]{:S(2)}) collective-permute-start(f32[40,256]{1,0:T(8,128)S(1)} %shard_map.47), channel_id=1, source_target_pairs={{16,32},{32,16},{48,64},{64,48},{80,96},{96,80},{112,128},{128,112... | collective-permute-start | bytes 122888 | tf_op jit(solution)/shard_map/ppermute | solution.py:316
  39.8 6.2 %collective-permute-start.7 = (f32[60,256]{1,0:T(8,128)S(1)}, f32[60,256]{1,0:T(8,128)S(1)}, u32[]{:S(2)}, u32[]{:S(2)}) collective-permute-start(f32[60,256]{1,0:T(8,128)S(1)} %select_n.184), channel_id=1, source_target_pairs={{0,1},{1,0},{2,3},{3,2},{4,5},{5,4},{6,7},{7,6},{8,9},{9,8},{10,11... | collective-permute-start | bytes 184328 | tf_op jit(solution)/shard_map/ppermute | solution.py:311
  43.7 6.2 %collective-permute-start.6 = (f32[60,256]{1,0:T(8,128)S(1)}, f32[60,256]{1,0:T(8,128)S(1)}, u32[]{:S(2)}, u32[]{:S(2)}) collective-permute-start(f32[60,256]{1,0:T(8,128)S(1)} %select_n.182), channel_id=1, source_target_pairs={{1,2},{2,1},{3,4},{4,3},{5,6},{6,5},{7,8},{8,7},{9,10},{10,9},{11,... | collective-permute-start | bytes 184328 | tf_op jit(solution)/shard_map/ppermute | solution.py:316
  51.3 10.7 %all-to-all-start = ((f32[16,10,128]{2,1,0:T(8,128)}), f32[16,10,128]{2,1,0:T(8,128)S(1)}, u32[]{:S(2)}, u32[]{:S(2)}) async-start(f32[16,10,128]{2,1,0:T(8,128)} %shard_map.48), calls=%async_computation | async-start | bytes 262144 | tf_op jit(solution)/shard_map/all_to_all | solution.py:336
  62.1 7.4 %collective-permute-start.8 = (f32[8,10,128]{2,1,0:T(8,128)S(1)}, f32[8,10,128]{2,1,0:T(8,128)S(1)}, u32[]{:S(2)}, u32[]{:S(2)}) collective-permute-start(f32[8,10,128]{2,1,0:T(8,128)S(1)} %slice_select_fusion.1), channel_id=1, source_target_pairs={{0,128},{16,144},{32,160},{48,176},{128,256},{144,272},{160,288},{... | collective-permute-start | bytes 122888 | tf_op jit(solution)/shard_map/ppermute | solution.py:341
  69.5 6.5 %collective-permute-start.9 = (f32[180,128]{1,0:T(8,128)S(1)}, f32[180,128]{1,0:T(8,128)S(1)}, u32[]{:S(2)}, u32[]{:S(2)}) collective-permute-start(f32[180,128]{1,0:T(8,128)S(1)} %reshape.69), channel_id=1, source_target_pairs={{1,2},{2,1},{3,4},{4,3},{5,6},{6,5},{7,8},{8,7},{9,10},{10,9},{11,... | collective-permute-start | bytes 276488 | tf_op jit(solution)/shard_map/ppermute | solution.py:316
  76.0 7.9 %collective-permute-start.10 = (f32[90,128]{1,0:T(8,128)S(1)}, f32[90,128]{1,0:T(8,128)S(1)}, u32[]{:S(2)}, u32[]{:S(2)}) collective-permute-start(f32[90,128]{1,0:T(8,128)S(1)} %select_n.193), channel_id=1, source_target_pairs={{0,1},{1,0},{2,3},{3,2},{4,5},{5,4},{6,7},{7,6},{8,9},{9,8},{10,11... | collective-permute-start | bytes 138248 | tf_op jit(solution)/shard_map/ppermute | solution.py:311

commit v3 on v2

--- a/solution.py
+++ b/solution.py
@@ -6,6 +6,9 @@
 from jax.sharding import PartitionSpec as P
 
 F32 = jnp.float32
+EXTRA = 8
+HBM = pl.BlockSpec(memory_space=pltpu.HBM)
+SMEM = pl.BlockSpec(memory_space=pltpu.SMEM)
 VMEM = pl.BlockSpec(memory_space=pltpu.VMEM)
 PARAMS = pltpu.CompilerParams(vmem_limit_bytes=48 * 1024 * 1024)
 
@@ -14,18 +17,33 @@
     return lax.broadcasted_iota(jnp.int32, shape, dim)
 
 
-def exact_dot(a, b):
-    return jnp.dot(a, b, precision=lax.Precision.HIGHEST, preferred_element_type=F32)
-
-
-def pool_matrix(n):
-    shape = (n, n // 2)
-    return (iota(shape, 0) // 2 == iota(shape, 1)).astype(F32)
-
-
-def spread_matrix(n):
-    shape = (n, 2 * n)
-    return (iota(shape, 0) == iota(shape, 1) // 2).astype(F32)
+def pick_rows(a, index):
+    return jnp.take_along_axis(a, index, axis=0)
+
+
+def lanes(a, k):
+    return a[:, 128 * k : 128 * (k + 1)]
+
+
+def spread_lanes(a):
+    half = iota((8, 128), 1) // 2
+    tiles = []
+    for k in range(a.shape[1] // 128):
+        for index in (half, half + 64):
+            tiles.append(jnp.take_along_axis(lanes(a, k), index, axis=1))
+    return jnp.concatenate(tiles, axis=1)
+
+
+def pool_lanes(a):
+    a = a + pltpu.roll(a, a.shape[1] - 1, 1)
+    lane = iota((8, 128), 1)
+    index = lane % 64 * 2
+    tiles = []
+    for k in range(0, a.shape[1] // 128, 2):
+        low = jnp.take_along_axis(lanes(a, k), index, axis=1)
+        high = jnp.take_along_axis(lanes(a, k + 1), index, axis=1)
+        tiles.append(jnp.where(lane < 64, low, high))
+    return jnp.concatenate(tiles, axis=1)
 
 
 def z_parts(tiles):
@@ -94,7 +112,7 @@
     return {p: 2.0 * terms[p] + (terms[p + 1] + terms[p - 1]) for p in planes}
 
 
-def stencil(v, s, sums, planes):
+def stencil(v, s, sums, planes, use=None):
     own, scaled = {}, {}
     result = {}
     for p in range(planes[0] - 1, planes[-1] + 2):
@@ -114,6 +132,8 @@
                 u, k = v[q][c][0], s[q][0]
                 here.append(8.1 * (k * u) + 0.125 * (u * sums[q] - (k * plain + heavy)))
             result[q] = here
+            if use is not None:
+                use(q, here)
     return result
 
 
@@ -121,28 +141,47 @@
     return free * 0.8 / (7.1 * stiff + 7.5)
 
 
-def prepare_kernel(density, fixed, loaded, load, fine, low_side, high_side, *scratch):
+def run_copies(pairs, sems):
     copies = [
-        pltpu.make_async_copy(source, scratch[k], scratch[4].at[k])
-        for k, source in enumerate((density, fixed, loaded, load))
+        pltpu.make_async_copy(source, target, sems.at[k])
+        for k, (source, target) in enumerate(pairs)
     ]
     for copy in copies:
         copy.start()
     for copy in copies:
         copy.wait()
-    density, fixed, loaded, load = scratch[:4]
-    for p in (0, 3, 1, 2):
-        level = (density[p].astype(F32) + 1.0) * (1.0 / 256.0)
-        stiff = 0.05 + level * level * level
-        free = (1 - fixed[p]).astype(F32)
-        factor = gain(stiff, free) * loaded[p].astype(F32)
-        values = [factor * load[c, p] for c in range(3)] + [stiff, free]
-        for f in range(5):
-            fine[f, p] = values[f]
-            if p == 0:
-                low_side[f] = values[f]
-            if p == 3:
-                high_side[f] = values[f]
+
+
+def start_values(density, fixed, loaded, load):
+    level = (density.astype(F32) + 1.0) * (1.0 / 256.0)
+    stiff = 0.05 + level * level * level
+    free = (1 - fixed).astype(F32)
+    factor = gain(stiff, free) * loaded.astype(F32)
+    return [factor * c for c in load] + [stiff, free]
+
+
+def edge_kernel(even, density, fixed, loaded, load, outer, *scratch):
+    plane = jnp.where(even[0] == 1, 0, 3)
+    sources = [a.at[plane] for a in (density, fixed, loaded)] + [load.at[:, plane]]
+    run_copies(zip(sources, scratch[:4]), scratch[4])
+    d, x, m, f = scratch[:4]
+    values = start_values(d[...], x[...], m[...], [f[c] for c in range(3)])
+    for k in range(5):
+        outer[k] = values[k]
+
+
+def prepare_kernel(even, density, fixed, loaded, load, fine, inner, *scratch):
+    run_copies(zip((density, fixed, loaded, load), scratch[:4]), scratch[4])
+    d, x, m, f = scratch[:4]
+    is_even = even[0] == 1
+    kept = {}
+    for p in range(4):
+        values = start_values(d[p], x[p], m[p], [f[c, p] for c in range(3)])
+        for k in range(5):
+            fine[k, p] = values[k]
+        kept[p] = values
+    for k in range(5):
+        inner[k] = jnp.where(is_even, kept[3][k], kept[0][k])
 
 
 def fine_tiles(fine, before, after, row_before, row_after):
@@ -174,17 +213,19 @@
             rows[c].append(free * (back * v[p][c][0] - image[p][c]))
         rows[3].append(stiff)
         rows[4].append(free)
-    pairs = []
+    row = iota((8, rows[0][0].shape[1]), 0)
+    index = row % 4 * 2
     for f in range(5):
-        pairs += [rows[f][0] + rows[f][1], rows[f][2] + rows[f][3]]
-    wide = jnp.concatenate(pairs, axis=0)
-    short = exact_dot(wide, pool_matrix(wide.shape[1]))
-    shape = (40, 80)
-    left = (iota(shape, 0) == iota(shape, 1) // 2).astype(F32)
-    sums = exact_dot(left, short)
-    mid[0:24] = sums[0:24]
-    mid[24:32] = sums[24:32] * 0.125
-    mid[32:40] = (sums[32:40] > 0.5).astype(F32)
+        halves = []
+        for x in (0, 2):
+            both = rows[f][x] + rows[f][x + 1]
+            halves.append(pick_rows(both + pltpu.roll(both, 7, 0), index))
+        total = pool_lanes(jnp.where(row < 4, halves[0], halves[1]))
+        if f == 3:
+            total = total * 0.125
+        if f == 4:
+            total = (total > 0.5).astype(F32)
+        mid[8 * f : 8 * f + 8] = total
 
 
 def mid_fields(mid):
@@ -210,21 +251,23 @@
         )
     pairs.append(s[2][0] + s[3][0])
     pairs.append(free[2] + free[3])
-    wide = jnp.concatenate(pairs, axis=0)
-    short = exact_dot(wide, pool_matrix(wide.shape[1]))
-    shape = (10, 40)
-    out, source = iota(shape, 0), iota(shape, 1)
-    left = (source // 8 == out // 2) & (source % 8 // 2 == 1 + out % 2)
-    sums = exact_dot(left.astype(F32), short)
-    row = iota(sums.shape, 0)
-    values = jnp.where(
-        row < 6, sums, jnp.where(row < 8, sums * 0.125, (sums > 0.5).astype(F32))
-    )
+    sums = [pool_lanes(a + pltpu.roll(a, 7, 0)) for a in pairs]
+    sums[3] = sums[3] * 0.125
+    sums[4] = (sums[4] > 0.5).astype(F32)
+    row = iota(sums[0].shape, 0)
+    index = 2 + row % 2 * 2
+    packed = pick_rows(sums[0], index)
+    for f in range(1, 4):
+        packed = jnp.where(row // 2 == f, pick_rows(sums[f], index), packed)
+    last = pick_rows(sums[4], index)[0:2]
     for k in range(low.shape[0]):
-        low[k] = values
-
-
-def finish_kernel(low, mid, fine, before, after, row_before, row_after, out):
+        low[k, 0:8] = packed
+        low[k, 8:10] = last
+
+
+def finish_kernel(
+    low, mid, fine, before, after, row_before, row_after, out, held, sems
+):
     parts = [slice(0, 8), slice(8, 16)]
     s = [tuple(low[3, p, k] for k in parts) for p in range(9)]
     gains = [tuple(gain(low[3, p, k], low[4, p, k]) for k in parts) for p in range(9)]
@@ -244,64 +287,64 @@
             ]
             for p in planes
         }
-    wide = jnp.concatenate([v[p][c][0] for c in range(3) for p in (3, 4, 5)], axis=0)
-    shape = (72, 72)
-    to, source = iota(shape, 0), iota(shape, 1)
-    left = (source // 8 == to // 8) & (source % 8 == 2 + to % 8 // 2)
-    raised = exact_dot(exact_dot(left.astype(F32), wide), spread_matrix(wide.shape[1]))
+    row = iota((8, low.shape[3]), 0)
+    raised = [
+        [spread_lanes(pick_rows(v[p][c][0], 2 + row // 2)) for p in (3, 4, 5)]
+        for c in range(3)
+    ]
     first, s, free, gains = mid_fields(mid)
     v = []
     for p in range(6):
         here = []
         for c in range(3):
-            at = (c * 3 + p // 2) * 8
-            here.append((first[p][c][0] + free[p] * raised[at : at + 8],))
+            here.append((first[p][c][0] + free[p] * raised[c][p // 2],))
         v.append(here)
     planes = range(1, 5)
     image = stencil(v, s, stiff_sums(s, planes), planes)
-    wide = jnp.concatenate(
-        [
-            v[p][c][0] + first[p][c][0] - gains[p] * image[p][c]
-            for c in range(3)
-            for p in planes
-        ],
-        axis=0,
-    )
-    shape = (192, 96)
-    to, source = iota(shape, 0), iota(shape, 1)
-    inner = to % 16
-    row = jnp.where(inner < 8, 2 + inner // 2, jnp.where(inner == 8, 6, 1))
-    left = (source // 8 == to // 16) & (source % 8 == row)
-    raised = exact_dot(exact_dot(left.astype(F32), wide), spread_matrix(wide.shape[1]))
+    row = iota((8, mid.shape[3]), 0)
+    picks = (2 + row // 2, jnp.where(row == 0, 6, 1))
+    raised = []
+    for c in range(3):
+        raised.append([])
+        for p in planes:
+            a = v[p][c][0] + first[p][c][0] - gains[p] * image[p][c]
+            raised[c].append([spread_lanes(pick_rows(a, index)) for index in picks])
     tiles = fine_tiles(fine, before, after, row_before, row_after)
     s = [t[3] for t in tiles]
     v = []
     for p in range(6):
         here = []
         for c in range(3):
-            at = (c * 4 + (p + 1) // 2) * 16
+            up = raised[c][(p + 1) // 2]
             here.append(
-                tuple(
-                    tiles[p][c][k]
-                    + tiles[p][4][k] * raised[at + 8 * k : at + 8 * k + 8]
-                    for k in range(2)
-                )
+                tuple(tiles[p][c][k] + tiles[p][4][k] * up[k] for k in range(2))
             )
         v.append(here)
-    image = stencil(v, s, stiff_sums(s, planes), planes)
-    for p in planes:
+    sums = stiff_sums(s, planes)
+    copies = []
+
+    def finish(p, image):
         g = gain(s[p][0], tiles[p][4][0])
         for c in range(3):
-            out[c, p - 1] = v[p][c][0] + tiles[p][c][0] - g * image[p][c]
-
-
-def call(kernel, shapes, *args, space=pltpu.VMEM, scratch=()):
-    outs = [jax.ShapeDtypeStruct(shape, F32) for shape in shapes]
+            held[c, p - 1] = v[p][c][0] + tiles[p][c][0] - g * image[c]
+        copies.append(
+            pltpu.make_async_copy(held.at[:, p - 1], out.at[:, p - 1], sems.at[p - 1])
+        )
+        copies[-1].start()
+
+    stencil(v, s, sums, planes, finish)
+    for copy in copies:
+        copy.wait()
+
+
+def call(kernel, shapes, *args, ins=None, outs=None, scratch=()):
+    results = [jax.ShapeDtypeStruct(shape, F32) for shape in shapes]
+    outs = outs or [VMEM] * len(results)
     return pl.pallas_call(
         kernel,
-        out_shape=outs if len(outs) > 1 else outs[0],
-        in_specs=[pl.BlockSpec(memory_space=space)] * len(args),
-        out_specs=[VMEM] * len(outs) if len(outs) > 1 else VMEM,
+        out_shape=results if len(results) > 1 else results[0],
+        in_specs=ins or [VMEM] * len(args),
+        out_specs=outs if len(results) > 1 else outs[0],
         scratch_shapes=list(scratch),
         compiler_params=PARAMS,
     )(*args)
@@ -320,7 +363,9 @@
 
 def both_sides(low, high, axis):
     even = lax.axis_index(axis) % 2 == 0
-    outer = outer_swap(jnp.where(even, low, high), axis)
+    wide = jnp.where(even, low, high)
+    rows = low.shape[0]
+    outer = outer_swap(jnp.concatenate([wide, wide[:EXTRA]]), axis)[:rows]
     inner = inner_swap(jnp.where(even, high, low), axis)
     return jnp.where(even, outer, inner), jnp.where(even, inner, outer)
 
@@ -357,16 +402,28 @@
 
 def per_device(density, fixed, loaded, load):
     nz = density.shape[2]
-    args = (density, fixed, loaded, load)
-    fine, low_side, high_side = call(
+    even = lax.axis_index("gx") % 2 == 0
+    args = (even.astype(jnp.int32).reshape(1), density, fixed, loaded, load)
+    ins = [SMEM] + [HBM] * 4
+    sems = pltpu.SemaphoreType.DMA((4,))
+    outer = call(
+        edge_kernel,
+        [(5, 8, nz)],
+        *args,
+        ins=ins,
+        scratch=[pltpu.VMEM((8, nz), a.dtype) for a in args[1:4]]
+        + [pltpu.VMEM((3, 8, nz), F32), sems],
+    )
+    outer = outer_swap(outer, "gx")
+    fine, inner = call(
         prepare_kernel,
-        [(5, 4, 8, nz), (5, 8, nz), (5, 8, nz)],
+        [(5, 4, 8, nz), (5, 8, nz)],
         *args,
-        space=pl.ANY,
-        scratch=[pltpu.VMEM(a.shape, a.dtype) for a in args]
-        + [pltpu.SemaphoreType.DMA((4,))],
-    )
-    before, after = both_sides(low_side, high_side, "gx")
+        ins=ins,
+        scratch=[pltpu.VMEM(a.shape, a.dtype) for a in args[1:]] + [sems],
+    )
+    inner = inner_swap(inner, "gx")
+    before, after = jnp.where(even, outer, inner), jnp.where(even, inner, outer)
 
     def edge(row):
         planes = [before[:, None, row], fine[:, :, row], after[:, None, row]]
@@ -392,7 +449,15 @@
     low = jnp.concatenate(
         [low[:, :, 1:], jnp.zeros((5, 9, 6, nz // 4), F32), low[:, :, :1]], axis=2
     )
-    return call(finish_kernel, [(3, 4, 8, nz)], low, mid, *fine_args)
+    return call(
+        finish_kernel,
+        [(3, 4, 8, nz)],
+        low,
+        mid,
+        *fine_args,
+        outs=[HBM],
+        scratch=[pltpu.VMEM((3, 4, 8, nz), F32), sems],
+    )
 
 
 def solution(mesh):

time: 89.2 us -> 83 us (0.930)
  waiting for transfers between devices: 34 us -> 28.1 us
  Pallas kernels: 7.56 us -> 5.68 us
  starting transfers between devices: 41.4 us -> 43 us
    ppermute x5, waiting for transfers between devices: 17.7 us -> 8.75 us  [outer_swap(): lax.ppermute(value, axis, [(i, (i + 1 ^ 1) - 1) for i in range(1, n - 1)])]
    ppermute x5, waiting for transfers between devices: 4.38 us -> 7.48 us  [inner_swap(): lax.ppermute(value, axis, [(i, i ^ 1) for i in range(lax.axis_size(axis))])]
    ppermute x5, starting transfers between devices: 21.5 us -> 24.2 us  [inner_swap(): lax.ppermute(value, axis, [(i, i ^ 1) for i in range(lax.axis_size(axis))])]
    pallas_call x4 -> x5, Pallas kernels: 7.56 us -> 5.68 us  [call(): pl.pallas_call(kernel, out_shape=results if len(results) > 1 else results...]
  transfers between devices with their start and end apart: 12 -> 12, of which waited for: 9 -> 9; matrix products, arithmetic and copies ran while one was open for 1% -> 1% of each run, Pallas kernels for 0% -> 1%
where the time goes in v3:
time: 83 us; the launch traced here: 82.4 us
  starting transfers between devices  43 us (52%)
  waiting for transfers between devices  28.1 us (34%)
  Pallas kernels  5.68 us (7%)
  local copies, waits for them, and re-layouts  4.55 us (5%)
    ppermute x5, starting transfers between devices, inner_swap(): lax.ppermute(value, axis, [(i, i ^ 1) for i in range(lax.axis_size(axis))])  24.2 us
    ppermute x5, starting transfers between devices, outer_swap(): lax.ppermute(value, axis, [(i, (i + 1 ^ 1) - 1) for i in range(1, n - 1)])  13.4 us
    ppermute x5, waiting for transfers between devices, outer_swap(): lax.ppermute(value, axis, [(i, (i + 1 ^ 1) - 1) for i in range(1, n - 1)])  8.75 us
    ppermute x5, waiting for transfers between devices, inner_swap(): lax.ppermute(value, axis, [(i, i ^ 1) for i in range(lax.axis_size(axis))])  7.48 us
    all_to_all x1, waiting for transfers between devices, gather_low(): row = lax.all_to_all(low, ('gx', 'gy'), 0, 0, axis_index_groups=groups)  6.51 us
    pallas_call x5, Pallas kernels, call(): pl.pallas_call(kernel, out_shape=results if len(results) > 1 else results...  5.68 us
    ppermute x1, waiting for transfers between devices, gather_low(): other = lax.ppermute(jnp.where(first, row[8:], row[:8]), 'gx', moves)  5.42 us
    all_to_all x1, starting transfers between devices, gather_low(): row = lax.all_to_all(low, ('gx', 'gy'), 0, 0, axis_index_groups=groups)  3.51 us
  transfers between devices with their start and end apart: 12, of which 9 were waited for; matrix products, arithmetic and copies ran while one was open for 1% of the time, Pallas kernels for 1%

profile of v3, /device:TPU:160, one launch (start us, length us, event | category | flops | bytes accessed | tf_op | source)
XLA Modules:
  0.0 82.4 jit_solution(4713626986350178837)
XLA Ops:
  3.6 4.0 %collective-permute-start = (f32[5,8,512]{2,1,0:T(8,128)S(1)}, f32[5,8,512]{2,1,0:T(8,128)S(1)}, u32[]{:S(2)}, u32[]{:S(2)}) collective-permute-start(f32[5,8,512]{2,1,0:T(8,128)S(1)} %shard_map.47), channel_id=1, source_target_pairs={{16,32},{32,16},{48,64},{64,48},{80,96},{96,80},{112,128},{128,112... | collective-permute-start | bytes 245768 | tf_op jit(solution)/shard_map/ppermute | solution.py:359
  8.2 1.9 %collective-permute-start.1 = (f32[5,8,512]{2,1,0:T(8,128)S(1)}, f32[5,8,512]{2,1,0:T(8,128)S(1)}, u32[]{:S(2)}, u32[]{:S(2)}) collective-permute-start(f32[5,8,512]{2,1,0:T(8,128)S(1)} %get-tuple-element.8), channel_id=1, source_target_pairs={{0,16},{16,0},{32,48},{48,32},{64,80},{80,64},{96,112},{112,96},{1... | collective-permute-start | bytes 245768 | tf_op jit(solution)/shard_map/ppermute | solution.py:354
  10.4 2.2 %collective-permute-done = f32[5,8,512]{2,1,0:T(8,128)S(1)} collective-permute-done((f32[5,8,512]{2,1,0:T(8,128)S(1)}, f32[5,8,512]{2,1,0:T(8,128)S(1)}, u32[]{:S(2)}, u32[]{:S(2)}) %collective-permute-start) | collective-permute-done | bytes 81952 | tf_op jit(solution)/shard_map/ppermute | solution.py:359
  12.8 1.9 %collective-permute-start.2 = (f32[38,512]{1,0:T(8,128)S(1)}, f32[38,512]{1,0:T(8,128)S(1)}, u32[]{:S(2)}, u32[]{:S(2)}) collective-permute-start(f32[38,512]{1,0:T(8,128)S(1)} %pad_maximum_fusion.4), channel_id=1, source_target_pairs={{1,2},{2,1},{3,4},{4,3},{5,6},{6,5},{7,8},{8,7},{9,10},{10,9},{11,... | collective-permute-start | bytes 233480 | tf_op jit(solution)/shard_map/ppermute | solution.py:359
  14.8 7.9 %collective-permute-start.3 = (f32[30,512]{1,0:T(8,128)S(1)}, f32[30,512]{1,0:T(8,128)S(1)}, u32[]{:S(2)}, u32[]{:S(2)}) collective-permute-start(f32[30,512]{1,0:T(8,128)S(1)} %select_n.166), channel_id=1, source_target_pairs={{0,1},{1,0},{2,3},{3,2},{4,5},{5,4},{6,7},{7,6},{8,9},{9,8},{10,11... | collective-permute-start | bytes 184328 | tf_op jit(solution)/shard_map/ppermute | solution.py:354
  22.6 2.2 %collective-permute-done.3 = f32[30,512]{1,0:T(8,128)S(1)} collective-permute-done((f32[30,512]{1,0:T(8,128)S(1)}, f32[30,512]{1,0:T(8,128)S(1)}, u32[]{:S(2)}, u32[]{:S(2)}) %collective-permute-start.3) | collective-permute-done | bytes 61472 | tf_op jit(solution)/shard_map/ppermute | solution.py:354
  24.9 1.1 %shard_map.48 = f32[40,256]{1,0:T(8,128)S(1)} custom-call(f32[5,4,8,512]{3,2,1,0:T(8,128)S(1)} %get-tuple-element.7.fine, f32[5,8,512]{2,1,0:T(8,128)S(1)} %get-tuple-element.10.before, f32[5,8,512]{2,1,0:T(8,128)S(1)} %get-tuple-element.9.after, f32[5,6,512]{2,1,0:T(8,128)S(1)} %reshape.69.row_before, f32[5,6,512]{2,1,0:T(8,128)S(1)} %reshape.70.row_after), custom_call_target="tpu_custom_call" | custom-call | tf_op jit(solution)/shard_map/pallas_call | solution.py:343
  26.0 3.6 %collective-permute-start.4 = (f32[48,256]{1,0:T(8,128)S(1)}, f32[48,256]{1,0:T(8,128)S(1)}, u32[]{:S(2)}, u32[]{:S(2)}) collective-permute-start(f32[48,256]{1,0:T(8,128)S(1)} %pad_maximum_fusion.6), channel_id=1, source_target_pairs={{16,32},{32,16},{48,64},{64,48},{80,96},{96,80},{112,128},{128,112... | collective-permute-start | bytes 147464 | tf_op jit(solution)/shard_map/ppermute | solution.py:359
  29.7 1.9 %collective-permute-start.5 = (f32[40,256]{1,0:T(8,128)S(1)}, f32[40,256]{1,0:T(8,128)S(1)}, u32[]{:S(2)}, u32[]{:S(2)}) collective-permute-start(f32[40,256]{1,0:T(8,128)S(1)} %shard_map.48), channel_id=1, source_target_pairs={{0,16},{16,0},{32,48},{48,32},{64,80},{80,64},{96,112},{112,96},{1... | collective-permute-start | bytes 122888 | tf_op jit(solution)/shard_map/ppermute | solution.py:354
  31.6 1.2 %collective-permute-done.5 = f32[40,256]{1,0:T(8,128)S(1)} collective-permute-done((f32[40,256]{1,0:T(8,128)S(1)}, f32[40,256]{1,0:T(8,128)S(1)}, u32[]{:S(2)}, u32[]{:S(2)}) %collective-permute-start.5) | collective-permute-done | bytes 40992 | tf_op jit(solution)/shard_map/ppermute | solution.py:354
  32.8 2.0 %collective-permute-done.4 = f32[48,256]{1,0:T(8,128)S(1)} collective-permute-done((f32[48,256]{1,0:T(8,128)S(1)}, f32[48,256]{1,0:T(8,128)S(1)}, u32[]{:S(2)}, u32[]{:S(2)}) %collective-permute-start.4) | collective-permute-done | bytes 49184 | tf_op jit(solution)/shard_map/ppermute | solution.py:359
  35.0 1.9 %collective-permute-start.6 = (f32[68,256]{1,0:T(8,128)S(1)}, f32[68,256]{1,0:T(8,128)S(1)}, u32[]{:S(2)}, u32[]{:S(2)}) collective-permute-start(f32[68,256]{1,0:T(8,128)S(1)} %pad_maximum_fusion.5), channel_id=1, source_target_pairs={{1,2},{2,1},{3,4},{4,3},{5,6},{6,5},{7,8},{8,7},{9,10},{10,9},{11,... | collective-permute-start | bytes 208904 | tf_op jit(solution)/shard_map/ppermute | solution.py:359
  37.0 6.6 %collective-permute-start.7 = (f32[60,256]{1,0:T(8,128)S(1)}, f32[60,256]{1,0:T(8,128)S(1)}, u32[]{:S(2)}, u32[]{:S(2)}) collective-permute-start(f32[60,256]{1,0:T(8,128)S(1)} %select_n.174), channel_id=1, source_target_pairs={{0,1},{1,0},{2,3},{3,2},{4,5},{5,4},{6,7},{7,6},{8,9},{9,8},{10,11... | collective-permute-start | bytes 184328 | tf_op jit(solution)/shard_map/ppermute | solution.py:354
  43.6 2.2 %collective-permute-done.7 = f32[60,256]{1,0:T(8,128)S(1)} collective-permute-done((f32[60,256]{1,0:T(8,128)S(1)}, f32[60,256]{1,0:T(8,128)S(1)}, u32[]{:S(2)}, u32[]{:S(2)}) %collective-permute-start.7) | collective-permute-done | bytes 61472 | tf_op jit(solution)/shard_map/ppermute | solution.py:354
  46.1 1.1 %shard_map.49 = f32[16,10,128]{2,1,0:T(8,128)} custom-call(f32[5,6,8,256]{3,2,1,0:T(8,128)S(1)} %pad_maximum_fusion.1.mid), custom_call_target="tpu_custom_call" | custom-call | tf_op jit(solution)/shard_map/pallas_call | solution.py:343
  47.1 3.5 %all-to-all-start = ((f32[16,10,128]{2,1,0:T(8,128)}), f32[16,10,128]{2,1,0:T(8,128)S(1)}, u32[]{:S(2)}, u32[]{:S(2)}) async-start(f32[16,10,128]{2,1,0:T(8,128)} %shard_map.49), calls=%async_computation | async-start | bytes 262144 | tf_op jit(solution)/shard_map/all_to_all | solution.py:381
  50.7 6.5 %all-to-all-done = f32[16,10,128]{2,1,0:T(8,128)S(1)} async-done(((f32[16,10,128]{2,1,0:T(8,128)}), f32[16,10,128]{2,1,0:T(8,128)S(1)}, u32[]{:S(2)}, u32[]{:S(2)}) %all-to-all-start) | async-done | bytes 81952 | tf_op jit(solution)/shard_map/all_to_all | solution.py:381
  57.2 1.9 %collective-permute-start.8 = (f32[8,10,128]{2,1,0:T(8,128)S(1)}, f32[8,10,128]{2,1,0:T(8,128)S(1)}, u32[]{:S(2)}, u32[]{:S(2)}) collective-permute-start(f32[8,10,128]{2,1,0:T(8,128)S(1)} %slice_select_fusion.1), channel_id=1, source_target_pairs={{0,128},{16,144},{32,160},{48,176},{128,256},{144,272},{160,288},{... | collective-permute-start | bytes 122888 | tf_op jit(solution)/shard_map/ppermute | solution.py:386
  59.1 5.4 %collective-permute-done.8 = f32[8,10,128]{2,1,0:T(8,128)S(1)} collective-permute-done((f32[8,10,128]{2,1,0:T(8,128)S(1)}, f32[8,10,128]{2,1,0:T(8,128)S(1)}, u32[]{:S(2)}, u32[]{:S(2)}) %collective-permute-start.8) | collective-permute-done | bytes 40992 | tf_op jit(solution)/shard_map/ppermute | solution.py:386
  64.6 1.9 %collective-permute-start.9 = (f32[180,128]{1,0:T(8,128)S(1)}, f32[180,128]{1,0:T(8,128)S(1)}, u32[]{:S(2)}, u32[]{:S(2)}) collective-permute-start(f32[180,128]{1,0:T(8,128)S(1)} %reshape.76), channel_id=1, source_target_pairs={{1,2},{2,1},{3,4},{4,3},{5,6},{6,5},{7,8},{8,7},{9,10},{10,9},{11,... | collective-permute-start | bytes 276488 | tf_op jit(solution)/shard_map/ppermute | solution.py:359
  66.6 4.5 %collective-permute-done.9 = f32[180,128]{1,0:T(8,128)S(1)} collective-permute-done((f32[180,128]{1,0:T(8,128)S(1)}, f32[180,128]{1,0:T(8,128)S(1)}, u32[]{:S(2)}, u32[]{:S(2)}) %collective-permute-start.9) | collective-permute-done | bytes 92192 | tf_op jit(solution)/shard_map/ppermute | solution.py:359
  71.1 5.8 %collective-permute-start.10 = (f32[90,128]{1,0:T(8,128)S(1)}, f32[90,128]{1,0:T(8,128)S(1)}, u32[]{:S(2)}, u32[]{:S(2)}) collective-permute-start(f32[90,128]{1,0:T(8,128)S(1)} %select_n.183), channel_id=1, source_target_pairs={{0,1},{1,0},{2,3},{3,2},{4,5},{5,4},{6,7},{7,6},{8,9},{9,8},{10,11... | collective-permute-start | bytes 138248 | tf_op jit(solution)/shard_map/ppermute | solution.py:354
  77.2 1.9 %collective-permute-done.10 = f32[90,128]{1,0:T(8,128)S(1)} collective-permute-done((f32[90,128]{1,0:T(8,128)S(1)}, f32[90,128]{1,0:T(8,128)S(1)}, u32[]{:S(2)}, u32[]{:S(2)}) %collective-permute-start.10) | collective-permute-done | bytes 46112 | tf_op jit(solution)/shard_map/ppermute | solution.py:354
  79.6 2.8 %shard_map.50 = f32[3,4,8,512]{3,2,1,0:T(8,128)} custom-call(f32[5,9,16,128]{3,2,1,0:T(8,128)S(1)} %pad_maximum_fusion.low, f32[5,6,8,256]{3,2,1,0:T(8,128)S(1)} %pad_maximum_fusion.1.mid, f32[5,4,8,512]{3,2,1,0:T(8,128)S(1)} %get-tuple-element.7.fine, f32[5,8,512]{2,1,0:T(8,128)S(1)} %get-tuple-element.10.before, f32[5,8,512]{2,1,0:T(8,128)S(1)} %get-tuple-element.9.after, ...), custom_call_target="tpu_custom_call" | custom-call | tf_op jit(solution)/shard_map/pallas_call | solution.py:343
  (62 shorter events, 5.8 us)
Async XLA Ops:
  0.0 0.9 %copy-start = (f32[3,4,8,512]{3,2,1,0:T(8,128)S(1)}, f32[3,4,8,512]{3,2,1,0:T(8,128)}, u32[]{:S(2)}) copy-start(f32[3,4,8,512]{3,2,1,0:T(8,128)} %load.3) | copy-start | bytes 589828
  0.9 0.8 %copy-start.1 = (s32[4,8,512]{2,1,0:T(8,128)S(1)}, s32[4,8,512]{2,1,0:T(8,128)}, u32[]{:S(2)}) copy-start(s32[4,8,512]{2,1,0:T(8,128)} %density.3) | copy-start | bytes 196612
  1.8 0.8 %copy-start.2 = (s32[4,8,512]{2,1,0:T(8,128)S(1)}, s32[4,8,512]{2,1,0:T(8,128)}, u32[]{:S(2)}) copy-start(s32[4,8,512]{2,1,0:T(8,128)} %fixed.3) | copy-start | bytes 196612
  2.6 0.8 %copy-start.3 = (s32[4,8,512]{2,1,0:T(8,128)S(1)}, s32[4,8,512]{2,1,0:T(8,128)}, u32[]{:S(2)}) copy-start(s32[4,8,512]{2,1,0:T(8,128)} %loaded.3) | copy-start | bytes 196612
  3.6 9.1 %collective-permute-start = (f32[5,8,512]{2,1,0:T(8,128)S(1)}, f32[5,8,512]{2,1,0:T(8,128)S(1)}, u32[]{:S(2)}, u32[]{:S(2)}) collective-permute-start(f32[5,8,512]{2,1,0:T(8,128)S(1)} %shard_map.47), channel_id=1, source_target_pairs={{16,32},{32,16},{48,64},{64,48},{80,96},{96,80},{112,128},{128,112... | collective-permute-start | bytes 245768 | tf_op jit(solution)/shard_map/ppermute | solution.py:359
  8.2 4.5 %collective-permute-start.1 = (f32[5,8,512]{2,1,0:T(8,128)S(1)}, f32[5,8,512]{2,1,0:T(8,128)S(1)}, u32[]{:S(2)}, u32[]{:S(2)}) collective-permute-start(f32[5,8,512]{2,1,0:T(8,128)S(1)} %get-tuple-element.8), channel_id=1, source_target_pairs={{0,16},{16,0},{32,48},{48,32},{64,80},{80,64},{96,112},{112,96},{1... | collective-permute-start | bytes 245768 | tf_op jit(solution)/shard_map/ppermute | solution.py:354
  12.8 12.0 %collective-permute-start.2 = (f32[38,512]{1,0:T(8,128)S(1)}, f32[38,512]{1,0:T(8,128)S(1)}, u32[]{:S(2)}, u32[]{:S(2)}) collective-permute-start(f32[38,512]{1,0:T(8,128)S(1)} %pad_maximum_fusion.4), channel_id=1, source_target_pairs={{1,2},{2,1},{3,4},{4,3},{5,6},{6,5},{7,8},{8,7},{9,10},{10,9},{11,... | collective-permute-start | bytes 233480 | tf_op jit(solution)/shard_map/ppermute | solution.py:359
  14.8 10.1 %collective-permute-start.3 = (f32[30,512]{1,0:T(8,128)S(1)}, f32[30,512]{1,0:T(8,128)S(1)}, u32[]{:S(2)}, u32[]{:S(2)}) collective-permute-start(f32[30,512]{1,0:T(8,128)S(1)} %select_n.166), channel_id=1, source_target_pairs={{0,1},{1,0},{2,3},{3,2},{4,5},{5,4},{6,7},{7,6},{8,9},{9,8},{10,11... | collective-permute-start | bytes 184328 | tf_op jit(solution)/shard_map/ppermute | solution.py:354
  26.0 8.7 %collective-permute-start.4 = (f32[48,256]{1,0:T(8,128)S(1)}, f32[48,256]{1,0:T(8,128)S(1)}, u32[]{:S(2)}, u32[]{:S(2)}) collective-permute-start(f32[48,256]{1,0:T(8,128)S(1)} %pad_maximum_fusion.6), channel_id=1, source_target_pairs={{16,32},{32,16},{48,64},{64,48},{80,96},{96,80},{112,128},{128,112... | collective-permute-start | bytes 147464 | tf_op jit(solution)/shard_map/ppermute | solution.py:359
  29.7 3.1 %collective-permute-start.5 = (f32[40,256]{1,0:T(8,128)S(1)}, f32[40,256]{1,0:T(8,128)S(1)}, u32[]{:S(2)}, u32[]{:S(2)}) collective-permute-start(f32[40,256]{1,0:T(8,128)S(1)} %shard_map.48), channel_id=1, source_target_pairs={{0,16},{16,0},{32,48},{48,32},{64,80},{80,64},{96,112},{112,96},{1... | collective-permute-start | bytes 122888 | tf_op jit(solution)/shard_map/ppermute | solution.py:354
  35.0 10.9 %collective-permute-start.6 = (f32[68,256]{1,0:T(8,128)S(1)}, f32[68,256]{1,0:T(8,128)S(1)}, u32[]{:S(2)}, u32[]{:S(2)}) collective-permute-start(f32[68,256]{1,0:T(8,128)S(1)} %pad_maximum_fusion.5), channel_id=1, source_target_pairs={{1,2},{2,1},{3,4},{4,3},{5,6},{6,5},{7,8},{8,7},{9,10},{10,9},{11,... | collective-permute-start | bytes 208904 | tf_op jit(solution)/shard_map/ppermute | solution.py:359
  37.0 8.9 %collective-permute-start.7 = (f32[60,256]{1,0:T(8,128)S(1)}, f32[60,256]{1,0:T(8,128)S(1)}, u32[]{:S(2)}, u32[]{:S(2)}) collective-permute-start(f32[60,256]{1,0:T(8,128)S(1)} %select_n.174), channel_id=1, source_target_pairs={{0,1},{1,0},{2,3},{3,2},{4,5},{5,4},{6,7},{7,6},{8,9},{9,8},{10,11... | collective-permute-start | bytes 184328 | tf_op jit(solution)/shard_map/ppermute | solution.py:354
  47.1 10.0 %all-to-all-start = ((f32[16,10,128]{2,1,0:T(8,128)}), f32[16,10,128]{2,1,0:T(8,128)S(1)}, u32[]{:S(2)}, u32[]{:S(2)}) async-start(f32[16,10,128]{2,1,0:T(8,128)} %shard_map.49), calls=%async_computation | async-start | bytes 262144 | tf_op jit(solution)/shard_map/all_to_all | solution.py:381
  57.2 7.4 %collective-permute-start.8 = (f32[8,10,128]{2,1,0:T(8,128)S(1)}, f32[8,10,128]{2,1,0:T(8,128)S(1)}, u32[]{:S(2)}, u32[]{:S(2)}) collective-permute-start(f32[8,10,128]{2,1,0:T(8,128)S(1)} %slice_select_fusion.1), channel_id=1, source_target_pairs={{0,128},{16,144},{32,160},{48,176},{128,256},{144,272},{160,288},{... | collective-permute-start | bytes 122888 | tf_op jit(solution)/shard_map/ppermute | solution.py:386
  64.6 6.5 %collective-permute-start.9 = (f32[180,128]{1,0:T(8,128)S(1)}, f32[180,128]{1,0:T(8,128)S(1)}, u32[]{:S(2)}, u32[]{:S(2)}) collective-permute-start(f32[180,128]{1,0:T(8,128)S(1)} %reshape.76), channel_id=1, source_target_pairs={{1,2},{2,1},{3,4},{4,3},{5,6},{6,5},{7,8},{8,7},{9,10},{10,9},{11,... | collective-permute-start | bytes 276488 | tf_op jit(solution)/shard_map/ppermute | solution.py:359
  71.1 7.9 %collective-permute-start.10 = (f32[90,128]{1,0:T(8,128)S(1)}, f32[90,128]{1,0:T(8,128)S(1)}, u32[]{:S(2)}, u32[]{:S(2)}) collective-permute-start(f32[90,128]{1,0:T(8,128)S(1)} %select_n.183), channel_id=1, source_target_pairs={{0,1},{1,0},{2,3},{3,2},{4,5},{5,4},{6,7},{7,6},{8,9},{9,8},{10,11... | collective-permute-start | bytes 138248 | tf_op jit(solution)/shard_map/ppermute | solution.py:354

commit v4 on v3

--- a/solution.py
+++ b/solution.py
@@ -10,7 +10,6 @@
 HBM = pl.BlockSpec(memory_space=pltpu.HBM)
 SMEM = pl.BlockSpec(memory_space=pltpu.SMEM)
 VMEM = pl.BlockSpec(memory_space=pltpu.VMEM)
-PARAMS = pltpu.CompilerParams(vmem_limit_bytes=48 * 1024 * 1024)
 
 
 def iota(shape, dim):
@@ -337,7 +336,7 @@
         copy.wait()
 
 
-def call(kernel, shapes, *args, ins=None, outs=None, scratch=()):
+def call(kernel, shapes, *args, ins=None, outs=None, scratch=(), limit=48):
     results = [jax.ShapeDtypeStruct(shape, F32) for shape in shapes]
     outs = outs or [VMEM] * len(results)
     return pl.pallas_call(
@@ -346,7 +345,7 @@
         in_specs=ins or [VMEM] * len(args),
         out_specs=outs if len(results) > 1 else outs[0],
         scratch_shapes=list(scratch),
-        compiler_params=PARAMS,
+        compiler_params=pltpu.CompilerParams(vmem_limit_bytes=limit << 20),
     )(*args)
 
 
@@ -390,8 +389,9 @@
     pair = lax.dynamic_slice_in_dim(planes, place % 4 * 2, 18, 0)
     even = lax.axis_index("gy") % 2 == 0
     beside = outer_swap(pair.reshape(180, nz), "gy").reshape(9, 2, 10, nz)
-    beyond = jnp.where(even, beside[:, 1], beside[:, 0]).reshape(90, nz)
-    beyond = inner_swap(beyond, "gy").reshape(9, 1, 10, nz)
+    own = jnp.where(even, pair[0::2], pair[1::2]).reshape(90, nz)
+    moves = [(j + 2, j) if j % 2 == 0 else (j, j + 2) for j in range(ny - 2)]
+    beyond = lax.ppermute(own, "gy", moves).reshape(9, 1, 10, nz)
     pair = pair.reshape(9, 2, 10, nz)
     return jnp.where(
         even,
@@ -413,6 +413,7 @@
         ins=ins,
         scratch=[pltpu.VMEM((8, nz), a.dtype) for a in args[1:4]]
         + [pltpu.VMEM((3, 8, nz), F32), sems],
+        limit=60,
     )
     outer = outer_swap(outer, "gx")
     fine, inner = call(

time: 83 us -> 80.2 us (0.966)
  the two profiles are of different devices: /device:TPU:160 before, /device:TPU:88 now
where the time goes in v4:
time: 80.2 us; the launch traced here: 79.7 us
  starting transfers between devices  48.6 us (61%)
  waiting for transfers between devices  21.7 us (27%)
  Pallas kernels  7.15 us (9%)
  local copies, waits for them, and re-layouts  1.11 us (1%)
    ppermute x5, starting transfers between devices, outer_swap(): lax.ppermute(value, axis, [(i, (i + 1 ^ 1) - 1) for i in range(1, n - 1)])  23.2 us
    ppermute x4, waiting for transfers between devices, inner_swap(): lax.ppermute(value, axis, [(i, i ^ 1) for i in range(lax.axis_size(axis))])  9.63 us
    ppermute x4, starting transfers between devices, inner_swap(): lax.ppermute(value, axis, [(i, i ^ 1) for i in range(lax.axis_size(axis))])  7.68 us
    ppermute x1, starting transfers between devices, gather_low(): beyond = lax.ppermute(own, 'gy', moves).reshape(9, 1, 10, nz)  7.3 us
    pallas_call x5, Pallas kernels, call(): pl.pallas_call(kernel, out_shape=results if len(results) > 1 else results...  7.15 us
    all_to_all x1, starting transfers between devices, gather_low(): row = lax.all_to_all(low, ('gx', 'gy'), 0, 0, axis_index_groups=groups)  7.02 us
    all_to_all x1, waiting for transfers between devices, gather_low(): row = lax.all_to_all(low, ('gx', 'gy'), 0, 0, axis_index_groups=groups)  5.49 us
    ppermute x1, starting transfers between devices, gather_low(): other = lax.ppermute(jnp.where(first, row[8:], row[:8]), 'gx', moves)  3.46 us
  transfers between devices with their start and end apart: 12, of which 8 were waited for; matrix products, arithmetic and copies ran while one was open for 1% of the time, Pallas kernels for 1%

profile of v4, /device:TPU:88, one launch (start us, length us, event | category | flops | bytes accessed | tf_op | source)
XLA Modules:
  0.0 79.7 jit_solution(11113581647700120664)
XLA Ops:
  0.0 1.6 %shard_map.47 = f32[5,8,512]{2,1,0:T(8,128)} custom-call(s32[1]{0:T(128)} %bitcast.even, s32[4,8,512]{2,1,0:T(8,128)} %density.3, s32[4,8,512]{2,1,0:T(8,128)} %fixed.3, s32[4,8,512]{2,1,0:T(8,128)} %loaded.3, f32[3,4,8,512]{3,2,1,0:T(8,128)} %load.3), custom_call_target="tpu_custom_call" | custom-call | tf_op jit(solution)/shard_map/pallas_call | solution.py:342
  1.6 4.0 %collective-permute-start = (f32[5,8,512]{2,1,0:T(8,128)}, f32[5,8,512]{2,1,0:T(8,128)S(1)}, u32[]{:S(2)}, u32[]{:S(2)}) collective-permute-start(f32[5,8,512]{2,1,0:T(8,128)} %shard_map.47), channel_id=1, source_target_pairs={{16,32},{32,16},{48,64},{64,48},{80,96},{96,80},{112,128},{128,112... | collective-permute-start | bytes 245768 | tf_op jit(solution)/shard_map/ppermute | solution.py:358
  6.3 1.9 %collective-permute-start.1 = (f32[5,8,512]{2,1,0:T(8,128)S(1)}, f32[5,8,512]{2,1,0:T(8,128)S(1)}, u32[]{:S(2)}, u32[]{:S(2)}) collective-permute-start(f32[5,8,512]{2,1,0:T(8,128)S(1)} %get-tuple-element.8), channel_id=1, source_target_pairs={{0,16},{16,0},{32,48},{48,32},{64,80},{80,64},{96,112},{112,96},{1... | collective-permute-start | bytes 245768 | tf_op jit(solution)/shard_map/ppermute | solution.py:353
  8.5 1.2 %collective-permute-done = f32[5,8,512]{2,1,0:T(8,128)S(1)} collective-permute-done((f32[5,8,512]{2,1,0:T(8,128)}, f32[5,8,512]{2,1,0:T(8,128)S(1)}, u32[]{:S(2)}, u32[]{:S(2)}) %collective-permute-start) | collective-permute-done | bytes 81952 | tf_op jit(solution)/shard_map/ppermute | solution.py:358
  9.9 4.3 %collective-permute-start.2 = (f32[38,512]{1,0:T(8,128)S(1)}, f32[38,512]{1,0:T(8,128)S(1)}, u32[]{:S(2)}, u32[]{:S(2)}) collective-permute-start(f32[38,512]{1,0:T(8,128)S(1)} %pad_maximum_fusion.4), channel_id=1, source_target_pairs={{1,2},{2,1},{3,4},{4,3},{5,6},{6,5},{7,8},{8,7},{9,10},{10,9},{11,... | collective-permute-start | bytes 233480 | tf_op jit(solution)/shard_map/ppermute | solution.py:358
  14.2 1.9 %collective-permute-start.3 = (f32[30,512]{1,0:T(8,128)S(1)}, f32[30,512]{1,0:T(8,128)S(1)}, u32[]{:S(2)}, u32[]{:S(2)}) collective-permute-start(f32[30,512]{1,0:T(8,128)S(1)} %select_n.162), channel_id=1, source_target_pairs={{0,1},{1,0},{2,3},{3,2},{4,5},{5,4},{6,7},{7,6},{8,9},{9,8},{10,11... | collective-permute-start | bytes 184328 | tf_op jit(solution)/shard_map/ppermute | solution.py:353
  16.1 4.2 %collective-permute-done.3 = f32[30,512]{1,0:T(8,128)S(1)} collective-permute-done((f32[30,512]{1,0:T(8,128)S(1)}, f32[30,512]{1,0:T(8,128)S(1)}, u32[]{:S(2)}, u32[]{:S(2)}) %collective-permute-start.3) | collective-permute-done | bytes 61472 | tf_op jit(solution)/shard_map/ppermute | solution.py:353
  20.4 1.1 %shard_map.48 = f32[40,256]{1,0:T(8,128)S(1)} custom-call(f32[5,4,8,512]{3,2,1,0:T(8,128)S(1)} %get-tuple-element.7.fine, f32[5,8,512]{2,1,0:T(8,128)S(1)} %get-tuple-element.10.before, f32[5,8,512]{2,1,0:T(8,128)S(1)} %get-tuple-element.9.after, f32[5,6,512]{2,1,0:T(8,128)S(1)} %reshape.65.row_before, f32[5,6,512]{2,1,0:T(8,128)S(1)} %reshape.66.row_after), custom_call_target="tpu_custom_call" | custom-call | tf_op jit(solution)/shard_map/pallas_call | solution.py:342
  21.5 3.2 %collective-permute-start.4 = (f32[48,256]{1,0:T(8,128)S(1)}, f32[48,256]{1,0:T(8,128)S(1)}, u32[]{:S(2)}, u32[]{:S(2)}) collective-permute-start(f32[48,256]{1,0:T(8,128)S(1)} %pad_maximum_fusion.6), channel_id=1, source_target_pairs={{16,32},{32,16},{48,64},{64,48},{80,96},{96,80},{112,128},{128,112... | collective-permute-start | bytes 147464 | tf_op jit(solution)/shard_map/ppermute | solution.py:358
  24.7 1.9 %collective-permute-start.5 = (f32[40,256]{1,0:T(8,128)S(1)}, f32[40,256]{1,0:T(8,128)S(1)}, u32[]{:S(2)}, u32[]{:S(2)}) collective-permute-start(f32[40,256]{1,0:T(8,128)S(1)} %shard_map.48), channel_id=1, source_target_pairs={{0,16},{16,0},{32,48},{48,32},{64,80},{80,64},{96,112},{112,96},{1... | collective-permute-start | bytes 122888 | tf_op jit(solution)/shard_map/ppermute | solution.py:353
  26.7 1.2 %collective-permute-done.5 = f32[40,256]{1,0:T(8,128)S(1)} collective-permute-done((f32[40,256]{1,0:T(8,128)S(1)}, f32[40,256]{1,0:T(8,128)S(1)}, u32[]{:S(2)}, u32[]{:S(2)}) %collective-permute-start.5) | collective-permute-done | bytes 40992 | tf_op jit(solution)/shard_map/ppermute | solution.py:353
  27.9 1.2 %collective-permute-done.4 = f32[48,256]{1,0:T(8,128)S(1)} collective-permute-done((f32[48,256]{1,0:T(8,128)S(1)}, f32[48,256]{1,0:T(8,128)S(1)}, u32[]{:S(2)}, u32[]{:S(2)}) %collective-permute-start.4) | collective-permute-done | bytes 49184 | tf_op jit(solution)/shard_map/ppermute | solution.py:358
  29.3 5.8 %collective-permute-start.6 = (f32[68,256]{1,0:T(8,128)S(1)}, f32[68,256]{1,0:T(8,128)S(1)}, u32[]{:S(2)}, u32[]{:S(2)}) collective-permute-start(f32[68,256]{1,0:T(8,128)S(1)} %pad_maximum_fusion.5), channel_id=1, source_target_pairs={{1,2},{2,1},{3,4},{4,3},{5,6},{6,5},{7,8},{8,7},{9,10},{10,9},{11,... | collective-permute-start | bytes 208904 | tf_op jit(solution)/shard_map/ppermute | solution.py:358
  35.2 1.9 %collective-permute-start.7 = (f32[60,256]{1,0:T(8,128)S(1)}, f32[60,256]{1,0:T(8,128)S(1)}, u32[]{:S(2)}, u32[]{:S(2)}) collective-permute-start(f32[60,256]{1,0:T(8,128)S(1)} %select_n.170), channel_id=1, source_target_pairs={{0,1},{1,0},{2,3},{3,2},{4,5},{5,4},{6,7},{7,6},{8,9},{9,8},{10,11... | collective-permute-start | bytes 184328 | tf_op jit(solution)/shard_map/ppermute | solution.py:353
  37.1 4.2 %collective-permute-done.7 = f32[60,256]{1,0:T(8,128)S(1)} collective-permute-done((f32[60,256]{1,0:T(8,128)S(1)}, f32[60,256]{1,0:T(8,128)S(1)}, u32[]{:S(2)}, u32[]{:S(2)}) %collective-permute-start.7) | collective-permute-done | bytes 61472 | tf_op jit(solution)/shard_map/ppermute | solution.py:353
  41.5 1.1 %shard_map.49 = f32[16,10,128]{2,1,0:T(8,128)} custom-call(f32[5,6,8,256]{3,2,1,0:T(8,128)S(1)} %pad_maximum_fusion.1.mid), custom_call_target="tpu_custom_call" | custom-call | tf_op jit(solution)/shard_map/pallas_call | solution.py:342
  42.6 7.0 %all-to-all-start = ((f32[16,10,128]{2,1,0:T(8,128)}), f32[16,10,128]{2,1,0:T(8,128)S(1)}, u32[]{:S(2)}, u32[]{:S(2)}) async-start(f32[16,10,128]{2,1,0:T(8,128)} %shard_map.49), calls=%async_computation | async-start | bytes 262144 | tf_op jit(solution)/shard_map/all_to_all | solution.py:380
  49.6 5.5 %all-to-all-done = f32[16,10,128]{2,1,0:T(8,128)S(1)} async-done(((f32[16,10,128]{2,1,0:T(8,128)}), f32[16,10,128]{2,1,0:T(8,128)S(1)}, u32[]{:S(2)}, u32[]{:S(2)}) %all-to-all-start) | async-done | bytes 81952 | tf_op jit(solution)/shard_map/all_to_all | solution.py:380
  55.1 3.5 %collective-permute-start.8 = (f32[8,10,128]{2,1,0:T(8,128)S(1)}, f32[8,10,128]{2,1,0:T(8,128)S(1)}, u32[]{:S(2)}, u32[]{:S(2)}) collective-permute-start(f32[8,10,128]{2,1,0:T(8,128)S(1)} %slice_select_fusion.1), channel_id=1, source_target_pairs={{0,128},{16,144},{32,160},{48,176},{128,256},{144,272},{160,288},{... | collective-permute-start | bytes 122888 | tf_op jit(solution)/shard_map/ppermute | solution.py:385
  58.6 2.7 %collective-permute-done.8 = f32[8,10,128]{2,1,0:T(8,128)S(1)} collective-permute-done((f32[8,10,128]{2,1,0:T(8,128)S(1)}, f32[8,10,128]{2,1,0:T(8,128)S(1)}, u32[]{:S(2)}, u32[]{:S(2)}) %collective-permute-start.8) | collective-permute-done | bytes 40992 | tf_op jit(solution)/shard_map/ppermute | solution.py:385
  61.4 5.8 %collective-permute-start.9 = (f32[180,128]{1,0:T(8,128)S(1)}, f32[180,128]{1,0:T(8,128)S(1)}, u32[]{:S(2)}, u32[]{:S(2)}) collective-permute-start(f32[180,128]{1,0:T(8,128)S(1)} %reshape.72), channel_id=1, source_target_pairs={{1,2},{2,1},{3,4},{4,3},{5,6},{6,5},{7,8},{8,7},{9,10},{10,9},{11,... | collective-permute-start | bytes 276488 | tf_op jit(solution)/shard_map/ppermute | solution.py:358
  67.2 7.3 %collective-permute-start.10 = (f32[90,128]{1,0:T(8,128)S(1)}, f32[90,128]{1,0:T(8,128)S(1)}, u32[]{:S(2)}, u32[]{:S(2)}) collective-permute-start(f32[90,128]{1,0:T(8,128)S(1)} %reshape.73), channel_id=1, source_target_pairs={{2,0},{1,3},{4,2},{3,5},{6,4},{5,7},{8,6},{7,9},{10,8},{9,11},{12,... | collective-permute-start | bytes 138248 | tf_op jit(solution)/shard_map/ppermute | solution.py:394
  74.7 1.6 %collective-permute-done.10 = f32[90,128]{1,0:T(8,128)S(1)} collective-permute-done((f32[90,128]{1,0:T(8,128)S(1)}, f32[90,128]{1,0:T(8,128)S(1)}, u32[]{:S(2)}, u32[]{:S(2)}) %collective-permute-start.10) | collective-permute-done | bytes 46112 | tf_op jit(solution)/shard_map/ppermute | solution.py:394
  76.9 2.8 %shard_map.50 = f32[3,4,8,512]{3,2,1,0:T(8,128)} custom-call(f32[5,9,16,128]{3,2,1,0:T(8,128)S(1)} %pad_maximum_fusion.low, f32[5,6,8,256]{3,2,1,0:T(8,128)S(1)} %pad_maximum_fusion.1.mid, f32[5,4,8,512]{3,2,1,0:T(8,128)S(1)} %get-tuple-element.7.fine, f32[5,8,512]{2,1,0:T(8,128)S(1)} %get-tuple-element.10.before, f32[5,8,512]{2,1,0:T(8,128)S(1)} %get-tuple-element.9.after, ...), custom_call_target="tpu_custom_call" | custom-call | tf_op jit(solution)/shard_map/pallas_call | solution.py:342
  (61 shorter events, 2.3 us)
Async XLA Ops:
  0.0 5.6 %copy-start = (f32[3,4,8,512]{3,2,1,0:T(8,128)S(1)}, f32[3,4,8,512]{3,2,1,0:T(8,128)}, u32[]{:S(2)}) copy-start(f32[3,4,8,512]{3,2,1,0:T(8,128)} %load.3) | copy-start | bytes 589828
  0.0 5.6 %copy-start.1 = (s32[4,8,512]{2,1,0:T(8,128)S(1)}, s32[4,8,512]{2,1,0:T(8,128)}, u32[]{:S(2)}) copy-start(s32[4,8,512]{2,1,0:T(8,128)} %density.3) | copy-start | bytes 196612
  0.0 5.6 %copy-start.2 = (s32[4,8,512]{2,1,0:T(8,128)S(1)}, s32[4,8,512]{2,1,0:T(8,128)}, u32[]{:S(2)}) copy-start(s32[4,8,512]{2,1,0:T(8,128)} %fixed.3) | copy-start | bytes 196612
  0.0 5.6 %copy-start.3 = (s32[4,8,512]{2,1,0:T(8,128)S(1)}, s32[4,8,512]{2,1,0:T(8,128)}, u32[]{:S(2)}) copy-start(s32[4,8,512]{2,1,0:T(8,128)} %loaded.3) | copy-start | bytes 196612
  1.6 8.1 %collective-permute-start = (f32[5,8,512]{2,1,0:T(8,128)}, f32[5,8,512]{2,1,0:T(8,128)S(1)}, u32[]{:S(2)}, u32[]{:S(2)}) collective-permute-start(f32[5,8,512]{2,1,0:T(8,128)} %shard_map.47), channel_id=1, source_target_pairs={{16,32},{32,16},{48,64},{64,48},{80,96},{96,80},{112,128},{128,112... | collective-permute-start | bytes 245768 | tf_op jit(solution)/shard_map/ppermute | solution.py:358
  6.3 3.4 %collective-permute-start.1 = (f32[5,8,512]{2,1,0:T(8,128)S(1)}, f32[5,8,512]{2,1,0:T(8,128)S(1)}, u32[]{:S(2)}, u32[]{:S(2)}) collective-permute-start(f32[5,8,512]{2,1,0:T(8,128)S(1)} %get-tuple-element.8), channel_id=1, source_target_pairs={{0,16},{16,0},{32,48},{48,32},{64,80},{80,64},{96,112},{112,96},{1... | collective-permute-start | bytes 245768 | tf_op jit(solution)/shard_map/ppermute | solution.py:353
  9.9 10.5 %collective-permute-start.2 = (f32[38,512]{1,0:T(8,128)S(1)}, f32[38,512]{1,0:T(8,128)S(1)}, u32[]{:S(2)}, u32[]{:S(2)}) collective-permute-start(f32[38,512]{1,0:T(8,128)S(1)} %pad_maximum_fusion.4), channel_id=1, source_target_pairs={{1,2},{2,1},{3,4},{4,3},{5,6},{6,5},{7,8},{8,7},{9,10},{10,9},{11,... | collective-permute-start | bytes 233480 | tf_op jit(solution)/shard_map/ppermute | solution.py:358
  14.2 6.2 %collective-permute-start.3 = (f32[30,512]{1,0:T(8,128)S(1)}, f32[30,512]{1,0:T(8,128)S(1)}, u32[]{:S(2)}, u32[]{:S(2)}) collective-permute-start(f32[30,512]{1,0:T(8,128)S(1)} %select_n.162), channel_id=1, source_target_pairs={{0,1},{1,0},{2,3},{3,2},{4,5},{5,4},{6,7},{7,6},{8,9},{9,8},{10,11... | collective-permute-start | bytes 184328 | tf_op jit(solution)/shard_map/ppermute | solution.py:353
  21.5 7.5 %collective-permute-start.4 = (f32[48,256]{1,0:T(8,128)S(1)}, f32[48,256]{1,0:T(8,128)S(1)}, u32[]{:S(2)}, u32[]{:S(2)}) collective-permute-start(f32[48,256]{1,0:T(8,128)S(1)} %pad_maximum_fusion.6), channel_id=1, source_target_pairs={{16,32},{32,16},{48,64},{64,48},{80,96},{96,80},{112,128},{128,112... | collective-permute-start | bytes 147464 | tf_op jit(solution)/shard_map/ppermute | solution.py:358
  24.7 3.1 %collective-permute-start.5 = (f32[40,256]{1,0:T(8,128)S(1)}, f32[40,256]{1,0:T(8,128)S(1)}, u32[]{:S(2)}, u32[]{:S(2)}) collective-permute-start(f32[40,256]{1,0:T(8,128)S(1)} %shard_map.48), channel_id=1, source_target_pairs={{0,16},{16,0},{32,48},{48,32},{64,80},{80,64},{96,112},{112,96},{1... | collective-permute-start | bytes 122888 | tf_op jit(solution)/shard_map/ppermute | solution.py:353
  29.3 12.1 %collective-permute-start.6 = (f32[68,256]{1,0:T(8,128)S(1)}, f32[68,256]{1,0:T(8,128)S(1)}, u32[]{:S(2)}, u32[]{:S(2)}) collective-permute-start(f32[68,256]{1,0:T(8,128)S(1)} %pad_maximum_fusion.5), channel_id=1, source_target_pairs={{1,2},{2,1},{3,4},{4,3},{5,6},{6,5},{7,8},{8,7},{9,10},{10,9},{11,... | collective-permute-start | bytes 208904 | tf_op jit(solution)/shard_map/ppermute | solution.py:358
  35.2 6.2 %collective-permute-start.7 = (f32[60,256]{1,0:T(8,128)S(1)}, f32[60,256]{1,0:T(8,128)S(1)}, u32[]{:S(2)}, u32[]{:S(2)}) collective-permute-start(f32[60,256]{1,0:T(8,128)S(1)} %select_n.170), channel_id=1, source_target_pairs={{0,1},{1,0},{2,3},{3,2},{4,5},{5,4},{6,7},{7,6},{8,9},{9,8},{10,11... | collective-permute-start | bytes 184328 | tf_op jit(solution)/shard_map/ppermute | solution.py:353
  42.6 12.5 %all-to-all-start = ((f32[16,10,128]{2,1,0:T(8,128)}), f32[16,10,128]{2,1,0:T(8,128)S(1)}, u32[]{:S(2)}, u32[]{:S(2)}) async-start(f32[16,10,128]{2,1,0:T(8,128)} %shard_map.49), calls=%async_computation | async-start | bytes 262144 | tf_op jit(solution)/shard_map/all_to_all | solution.py:380
  55.1 6.2 %collective-permute-start.8 = (f32[8,10,128]{2,1,0:T(8,128)S(1)}, f32[8,10,128]{2,1,0:T(8,128)S(1)}, u32[]{:S(2)}, u32[]{:S(2)}) collective-permute-start(f32[8,10,128]{2,1,0:T(8,128)S(1)} %slice_select_fusion.1), channel_id=1, source_target_pairs={{0,128},{16,144},{32,160},{48,176},{128,256},{144,272},{160,288},{... | collective-permute-start | bytes 122888 | tf_op jit(solution)/shard_map/ppermute | solution.py:385
  61.4 14.9 %collective-permute-start.9 = (f32[180,128]{1,0:T(8,128)S(1)}, f32[180,128]{1,0:T(8,128)S(1)}, u32[]{:S(2)}, u32[]{:S(2)}) collective-permute-start(f32[180,128]{1,0:T(8,128)S(1)} %reshape.72), channel_id=1, source_target_pairs={{1,2},{2,1},{3,4},{4,3},{5,6},{6,5},{7,8},{8,7},{9,10},{10,9},{11,... | collective-permute-start | bytes 276488 | tf_op jit(solution)/shard_map/ppermute | solution.py:358
  67.2 9.0 %collective-permute-start.10 = (f32[90,128]{1,0:T(8,128)S(1)}, f32[90,128]{1,0:T(8,128)S(1)}, u32[]{:S(2)}, u32[]{:S(2)}) collective-permute-start(f32[90,128]{1,0:T(8,128)S(1)} %reshape.73), channel_id=1, source_target_pairs={{2,0},{1,3},{4,2},{3,5},{6,4},{5,7},{8,6},{7,9},{10,8},{9,11},{12,... | collective-permute-start | bytes 138248 | tf_op jit(solution)/shard_map/ppermute | solution.py:394

commit v5 on v4

--- a/solution.py
+++ b/solution.py
@@ -227,26 +227,27 @@
         mid[8 * f : 8 * f + 8] = total
 
 
-def mid_fields(mid):
+def mid_fields(mids):
     v, s, free, gains = [], [], [], []
     for p in range(6):
-        stiff, open_ = mid[3, p], mid[4, p]
+        mid = mids[p // 2].at[:, p % 2]
+        stiff, open_ = mid[3], mid[4]
         g = gain(stiff, open_)
-        v.append([(0.5 * g * mid[c, p],) for c in range(3)])
+        v.append([(0.5 * g * mid[c],) for c in range(3)])
         s.append((stiff,))
         free.append(open_)
         gains.append(g)
     return v, s, free, gains
 
 
-def mid_residual_kernel(mid, low):
-    v, s, free, _ = mid_fields(mid)
+def mid_residual_kernel(before, mid, after, low):
+    v, s, free, _ = mid_fields((before, mid, after))
     planes = range(2, 4)
     image = stencil(v, s, stiff_sums(s, planes), planes)
     pairs = []
     for c in range(3):
         pairs.append(
-            sum(free[p] * (mid[c, p] - 2.0 * image[p][c]) for p in planes)
+            sum(free[p] * (mid[c, p - 2] - 2.0 * image[p][c]) for p in planes)
         )
     pairs.append(s[2][0] + s[3][0])
     pairs.append(free[2] + free[3])
@@ -265,7 +266,18 @@
 
 
 def finish_kernel(
-    low, mid, fine, before, after, row_before, row_after, out, held, sems
+    low,
+    mid_before,
+    mid,
+    mid_after,
+    fine,
+    before,
+    after,
+    row_before,
+    row_after,
+    out,
+    held,
+    sems,
 ):
     parts = [slice(0, 8), slice(8, 16)]
     s = [tuple(low[3, p, k] for k in parts) for p in range(9)]
@@ -291,7 +303,7 @@
         [spread_lanes(pick_rows(v[p][c][0], 2 + row // 2)) for p in (3, 4, 5)]
         for c in range(3)
     ]
-    first, s, free, gains = mid_fields(mid)
+    first, s, free, gains = mid_fields((mid_before, mid, mid_after))
     v = []
     for p in range(6):
         here = []
@@ -360,12 +372,19 @@
     )
 
 
-def both_sides(low, high, axis):
+def shifts(low, high, axis):
+    n = lax.axis_size(axis)
+    rows = low.shape[0]
+    low = jnp.concatenate([low, low[:EXTRA]])
+    after = lax.ppermute(low, axis, [(i + 1, i) for i in range(n - 1)])[:rows]
+    before = lax.ppermute(high, axis, [(i, i + 1) for i in range(n - 1)])
+    return before, after
+
+
+def swaps(value, axis):
     even = lax.axis_index(axis) % 2 == 0
-    wide = jnp.where(even, low, high)
-    rows = low.shape[0]
-    outer = outer_swap(jnp.concatenate([wide, wide[:EXTRA]]), axis)[:rows]
-    inner = inner_swap(jnp.where(even, high, low), axis)
+    outer = outer_swap(jnp.concatenate([value, value[:EXTRA]]), axis)[: value.shape[0]]
+    inner = inner_swap(value, axis)
     return jnp.where(even, outer, inner), jnp.where(even, inner, outer)
 
 
@@ -430,21 +449,19 @@
         planes = [before[:, None, row], fine[:, :, row], after[:, None, row]]
         return jnp.concatenate(planes, axis=1).reshape(30, nz)
 
-    rims = [r.reshape(5, 6, nz) for r in both_sides(edge(0), edge(7), "gy")]
+    rims = [r.reshape(5, 6, nz) for r in shifts(edge(0), edge(7), "gy")]
     fine_args = (fine, before, after, *rims)
     mid = call(fine_residual_kernel, [(40, nz // 2)], *fine_args)
 
-    sides = both_sides(mid, mid, "gx")
-    shape = (5, 2, 4, nz // 2)
-    mid = jnp.concatenate([a.reshape(shape) for a in (sides[0], mid, sides[1])], axis=1)
-    rows_before, rows_after = both_sides(
-        mid[:, :, :2].reshape(60, nz // 2), mid[:, :, 2:].reshape(60, nz // 2), "gy"
-    )
-    shape = (5, 6, 2, nz // 2)
-    mid = jnp.concatenate(
-        [rows_before.reshape(shape), mid, rows_after.reshape(shape)], axis=2
-    )
-    low = call(mid_residual_kernel, [(16, 10, nz // 4)], mid)
+    mid = mid.reshape(5, 2, 4, nz // 2)
+    rows = shifts(
+        mid[:, :, :2].reshape(20, nz // 2), mid[:, :, 2:].reshape(20, nz // 2), "gy"
+    )
+    rows = [r.reshape(5, 2, 2, nz // 2) for r in rows]
+    mid = jnp.concatenate([rows[0], mid, rows[1]], axis=2).reshape(80, nz // 2)
+    sides = swaps(mid, "gx")
+    mids = [a.reshape(5, 2, 8, nz // 2) for a in (sides[0], mid, sides[1])]
+    low = call(mid_residual_kernel, [(16, 10, nz // 4)], *mids)
     low = gather_low(low).reshape(9, 5, 5, 2, nz // 4)
     low = low.transpose(2, 0, 1, 3, 4).reshape(5, 9, 10, nz // 4)
     low = jnp.concatenate(
@@ -454,7 +471,7 @@
         finish_kernel,
         [(3, 4, 8, nz)],
         low,
-        mid,
+        *mids,
         *fine_args,
         outs=[HBM],
         scratch=[pltpu.VMEM((3, 4, 8, nz), F32), sems],

time: 80.2 us -> 76.1 us (0.949)
  the two profiles are of different devices: /device:TPU:88 before, /device:TPU:224 now
where the time goes in v5:
time: 76.1 us; the launch traced here: 75.6 us
  starting transfers between devices  44 us (58%)
  waiting for transfers between devices  22.7 us (30%)
  Pallas kernels  7.15 us (9%)
  local copies, waits for them, and re-layouts  0.81 us (1%)
    ppermute x3, starting transfers between devices, outer_swap(): lax.ppermute(value, axis, [(i, (i + 1 ^ 1) - 1) for i in range(1, n - 1)])  13.6 us
    ppermute x2, starting transfers between devices, shifts(): before = lax.ppermute(high, axis, [(i, i + 1) for i in range(n - 1)])  11 us
    pallas_call x5, Pallas kernels, call(): pl.pallas_call(kernel, out_shape=results if len(results) > 1 else results...  7.15 us
    ppermute x1, starting transfers between devices, gather_low(): beyond = lax.ppermute(own, 'gy', moves).reshape(9, 1, 10, nz)  6.46 us
    ppermute x3, waiting for transfers between devices, outer_swap(): lax.ppermute(value, axis, [(i, (i + 1 ^ 1) - 1) for i in range(1, n - 1)])  5.67 us
    ppermute x1, waiting for transfers between devices, gather_low(): other = lax.ppermute(jnp.where(first, row[8:], row[:8]), 'gx', moves)  5.41 us
    all_to_all x1, waiting for transfers between devices, gather_low(): row = lax.all_to_all(low, ('gx', 'gy'), 0, 0, axis_index_groups=groups)  5.37 us
    ppermute x2, starting transfers between devices, inner_swap(): lax.ppermute(value, axis, [(i, i ^ 1) for i in range(lax.axis_size(axis))])  3.84 us
  transfers between devices with their start and end apart: 12, of which 8 were waited for; matrix products, arithmetic and copies ran while one was open for 0% of the time, Pallas kernels for 1%

profile of v5, /device:TPU:224, one launch (start us, length us, event | category | flops | bytes accessed | tf_op | source)
XLA Modules:
  0.0 75.6 jit_solution(10813306308776977224)
XLA Ops:
  0.0 1.6 %shard_map.47 = f32[5,8,512]{2,1,0:T(8,128)} custom-call(s32[1]{0:T(128)} %bitcast.even, s32[4,8,512]{2,1,0:T(8,128)} %density.3, s32[4,8,512]{2,1,0:T(8,128)} %fixed.3, s32[4,8,512]{2,1,0:T(8,128)} %loaded.3, f32[3,4,8,512]{3,2,1,0:T(8,128)} %load.3), custom_call_target="tpu_custom_call" | custom-call | tf_op jit(solution)/shard_map/pallas_call | solution.py:354
  1.6 4.0 %collective-permute-start = (f32[5,8,512]{2,1,0:T(8,128)}, f32[5,8,512]{2,1,0:T(8,128)S(1)}, u32[]{:S(2)}, u32[]{:S(2)}) collective-permute-start(f32[5,8,512]{2,1,0:T(8,128)} %shard_map.47), channel_id=1, source_target_pairs={{16,32},{32,16},{48,64},{64,48},{80,96},{96,80},{112,128},{128,112... | collective-permute-start | bytes 245768 | tf_op jit(solution)/shard_map/ppermute | solution.py:370
  6.3 1.9 %collective-permute-start.1 = (f32[5,8,512]{2,1,0:T(8,128)S(1)}, f32[5,8,512]{2,1,0:T(8,128)S(1)}, u32[]{:S(2)}, u32[]{:S(2)}) collective-permute-start(f32[5,8,512]{2,1,0:T(8,128)S(1)} %get-tuple-element.8), channel_id=1, source_target_pairs={{0,16},{16,0},{32,48},{48,32},{64,80},{80,64},{96,112},{112,96},{1... | collective-permute-start | bytes 245768 | tf_op jit(solution)/shard_map/ppermute | solution.py:365
  8.3 2.6 %collective-permute-done = f32[5,8,512]{2,1,0:T(8,128)S(1)} collective-permute-done((f32[5,8,512]{2,1,0:T(8,128)}, f32[5,8,512]{2,1,0:T(8,128)S(1)}, u32[]{:S(2)}, u32[]{:S(2)}) %collective-permute-start) | collective-permute-done | bytes 81952 | tf_op jit(solution)/shard_map/ppermute | solution.py:370
  11.1 1.9 %collective-permute-start.3 = (f32[38,512]{1,0:T(8,128)S(1)}, f32[38,512]{1,0:T(8,128)S(1)}, u32[]{:S(2)}, u32[]{:S(2)}) collective-permute-start(f32[38,512]{1,0:T(8,128)S(1)} %pad_maximum_fusion.4), channel_id=1, source_target_pairs={{1,0},{2,1},{3,2},{4,3},{5,4},{6,5},{7,6},{8,7},{9,8},{10,9},{11,1... | collective-permute-start | bytes 233480 | tf_op jit(solution)/shard_map/ppermute | solution.py:379
  13.0 5.5 %collective-permute-start.2 = (f32[30,512]{1,0:T(8,128)S(1)}, f32[30,512]{1,0:T(8,128)S(1)}, u32[]{:S(2)}, u32[]{:S(2)}) collective-permute-start(f32[30,512]{1,0:T(8,128)S(1)} %reshape.69), channel_id=1, source_target_pairs={{0,1},{1,2},{2,3},{3,4},{4,5},{5,6},{6,7},{7,8},{8,9},{9,10},{10,1... | collective-permute-start | bytes 184328 | tf_op jit(solution)/shard_map/ppermute | solution.py:380
  18.5 1.9 %collective-permute-done.2 = f32[30,512]{1,0:T(8,128)S(1)} collective-permute-done((f32[30,512]{1,0:T(8,128)S(1)}, f32[30,512]{1,0:T(8,128)S(1)}, u32[]{:S(2)}, u32[]{:S(2)}) %collective-permute-start.2) | collective-permute-done | bytes 61472 | tf_op jit(solution)/shard_map/ppermute | solution.py:380
  20.5 1.1 %shard_map.48 = f32[40,256]{1,0:T(8,128)S(1)} custom-call(f32[5,4,8,512]{3,2,1,0:T(8,128)S(1)} %get-tuple-element.7.fine, f32[5,8,512]{2,1,0:T(8,128)S(1)} %get-tuple-element.14.before, f32[5,8,512]{2,1,0:T(8,128)S(1)} %get-tuple-element.13.after, f32[5,6,512]{2,1,0:T(8,128)S(1)} %reshape.70.row_before, f32[5,6,512]{2,1,0:T(8,128)S(1)} %reshape.72.row_after), custom_call_target="tpu_custom_call" | custom-call | tf_op jit(solution)/shard_map/pallas_call | solution.py:354
  21.7 1.9 %collective-permute-start.5 = (f32[28,256]{1,0:T(8,128)S(1)}, f32[28,256]{1,0:T(8,128)S(1)}, u32[]{:S(2)}, u32[]{:S(2)}) collective-permute-start(f32[28,256]{1,0:T(8,128)S(1)} %pad_maximum_fusion.6), channel_id=1, source_target_pairs={{1,0},{2,1},{3,2},{4,3},{5,4},{6,5},{7,6},{8,7},{9,8},{10,9},{11,1... | collective-permute-start | bytes 86024 | tf_op jit(solution)/shard_map/ppermute | solution.py:379
  23.6 5.5 %collective-permute-start.4 = (f32[20,256]{1,0:T(8,128)S(1)}, f32[20,256]{1,0:T(8,128)S(1)}, u32[]{:S(2)}, u32[]{:S(2)}) collective-permute-start(f32[20,256]{1,0:T(8,128)S(1)} %reshape.74), channel_id=1, source_target_pairs={{0,1},{1,2},{2,3},{3,4},{4,5},{5,6},{6,7},{7,8},{8,9},{9,10},{10,1... | collective-permute-start | bytes 61448 | tf_op jit(solution)/shard_map/ppermute | solution.py:380
  29.1 1.5 %collective-permute-done.4 = f32[20,256]{1,0:T(8,128)S(1)} collective-permute-done((f32[20,256]{1,0:T(8,128)S(1)}, f32[20,256]{1,0:T(8,128)S(1)}, u32[]{:S(2)}, u32[]{:S(2)}) %collective-permute-start.4) | collective-permute-done | bytes 20512 | tf_op jit(solution)/shard_map/ppermute | solution.py:380
  30.8 2.9 %collective-permute-start.6 = (f32[88,256]{1,0:T(8,128)S(1)}, f32[88,256]{1,0:T(8,128)S(1)}, u32[]{:S(2)}, u32[]{:S(2)}) collective-permute-start(f32[88,256]{1,0:T(8,128)S(1)} %pad_maximum_fusion.1), channel_id=1, source_target_pairs={{16,32},{32,16},{48,64},{64,48},{80,96},{96,80},{112,128},{128,112... | collective-permute-start | bytes 270344 | tf_op jit(solution)/shard_map/ppermute | solution.py:370
  33.7 1.9 %collective-permute-start.7 = (f32[80,256]{1,0:T(8,128)S(1)}, f32[80,256]{1,0:T(8,128)S(1)}, u32[]{:S(2)}, u32[]{:S(2)}) collective-permute-start(f32[80,256]{1,0:T(8,128)S(1)} %bitcast.13), channel_id=1, source_target_pairs={{0,16},{16,0},{32,48},{48,32},{64,80},{80,64},{96,112},{112,96},{1... | collective-permute-start | bytes 245768 | tf_op jit(solution)/shard_map/ppermute | solution.py:365
  35.6 1.2 %collective-permute-done.7 = f32[80,256]{1,0:T(8,128)S(1)} collective-permute-done((f32[80,256]{1,0:T(8,128)S(1)}, f32[80,256]{1,0:T(8,128)S(1)}, u32[]{:S(2)}, u32[]{:S(2)}) %collective-permute-start.7) | collective-permute-done | bytes 81952 | tf_op jit(solution)/shard_map/ppermute | solution.py:365
  36.9 3.0 %collective-permute-done.6 = f32[88,256]{1,0:T(8,128)S(1)} collective-permute-done((f32[88,256]{1,0:T(8,128)S(1)}, f32[88,256]{1,0:T(8,128)S(1)}, u32[]{:S(2)}, u32[]{:S(2)}) %collective-permute-start.6) | collective-permute-done | bytes 90144 | tf_op jit(solution)/shard_map/ppermute | solution.py:370
  39.9 1.1 %shard_map.49 = f32[16,10,128]{2,1,0:T(8,128)} custom-call(f32[5,2,8,256]{3,2,1,0:T(8,128)S(1)} %bitcast.16, f32[5,2,8,256]{3,2,1,0:T(8,128)S(1)} %pad_maximum_fusion.5.mid, f32[5,2,8,256]{3,2,1,0:T(8,128)S(1)} %bitcast.14), custom_call_target="tpu_custom_call" | custom-call | tf_op jit(solution)/shard_map/pallas_call | solution.py:354
  41.0 3.4 %all-to-all-start = ((f32[16,10,128]{2,1,0:T(8,128)}), f32[16,10,128]{2,1,0:T(8,128)S(1)}, u32[]{:S(2)}, u32[]{:S(2)}) async-start(f32[16,10,128]{2,1,0:T(8,128)} %shard_map.49), calls=%async_computation | async-start | bytes 262144 | tf_op jit(solution)/shard_map/all_to_all | solution.py:399
  44.4 5.4 %all-to-all-done = f32[16,10,128]{2,1,0:T(8,128)S(1)} async-done(((f32[16,10,128]{2,1,0:T(8,128)}), f32[16,10,128]{2,1,0:T(8,128)S(1)}, u32[]{:S(2)}, u32[]{:S(2)}) %all-to-all-start) | async-done | bytes 81952 | tf_op jit(solution)/shard_map/all_to_all | solution.py:399
  49.8 1.9 %collective-permute-start.8 = (f32[8,10,128]{2,1,0:T(8,128)S(1)}, f32[8,10,128]{2,1,0:T(8,128)S(1)}, u32[]{:S(2)}, u32[]{:S(2)}) collective-permute-start(f32[8,10,128]{2,1,0:T(8,128)S(1)} %slice_select_fusion.3), channel_id=1, source_target_pairs={{0,128},{16,144},{32,160},{48,176},{128,256},{144,272},{160,288},{... | collective-permute-start | bytes 122888 | tf_op jit(solution)/shard_map/ppermute | solution.py:404
  51.8 5.4 %collective-permute-done.8 = f32[8,10,128]{2,1,0:T(8,128)S(1)} collective-permute-done((f32[8,10,128]{2,1,0:T(8,128)S(1)}, f32[8,10,128]{2,1,0:T(8,128)S(1)}, u32[]{:S(2)}, u32[]{:S(2)}) %collective-permute-start.8) | collective-permute-done | bytes 40992 | tf_op jit(solution)/shard_map/ppermute | solution.py:404
  57.3 6.7 %collective-permute-start.9 = (f32[180,128]{1,0:T(8,128)S(1)}, f32[180,128]{1,0:T(8,128)S(1)}, u32[]{:S(2)}, u32[]{:S(2)}) collective-permute-start(f32[180,128]{1,0:T(8,128)S(1)} %reshape.81), channel_id=1, source_target_pairs={{1,2},{2,1},{3,4},{4,3},{5,6},{6,5},{7,8},{8,7},{9,10},{10,9},{11,... | collective-permute-start | bytes 276488 | tf_op jit(solution)/shard_map/ppermute | solution.py:370
  64.0 6.5 %collective-permute-start.10 = (f32[90,128]{1,0:T(8,128)S(1)}, f32[90,128]{1,0:T(8,128)S(1)}, u32[]{:S(2)}, u32[]{:S(2)}) collective-permute-start(f32[90,128]{1,0:T(8,128)S(1)} %reshape.82), channel_id=1, source_target_pairs={{2,0},{1,3},{4,2},{3,5},{6,4},{5,7},{8,6},{7,9},{10,8},{9,11},{12,... | collective-permute-start | bytes 138248 | tf_op jit(solution)/shard_map/ppermute | solution.py:413
  70.6 1.6 %collective-permute-done.10 = f32[90,128]{1,0:T(8,128)S(1)} collective-permute-done((f32[90,128]{1,0:T(8,128)S(1)}, f32[90,128]{1,0:T(8,128)S(1)}, u32[]{:S(2)}, u32[]{:S(2)}) %collective-permute-start.10) | collective-permute-done | bytes 46112 | tf_op jit(solution)/shard_map/ppermute | solution.py:413
  72.8 2.8 %shard_map.50 = f32[3,4,8,512]{3,2,1,0:T(8,128)} custom-call(f32[5,9,16,128]{3,2,1,0:T(8,128)S(1)} %pad_maximum_fusion.low, f32[5,2,8,256]{3,2,1,0:T(8,128)S(1)} %bitcast.17, f32[5,2,8,256]{3,2,1,0:T(8,128)S(1)} %pad_maximum_fusion.5.mid, f32[5,2,8,256]{3,2,1,0:T(8,128)S(1)} %bitcast.15, f32[5,4,8,512]{3,2,1,0:T(8,128)S(1)} %get-tuple-element.7.fine, ...), custom_call_target="tpu_custom_call" | custom-call | tf_op jit(solution)/shard_map/pallas_call | solution.py:354
  (56 shorter events, 1.9 us)
Async XLA Ops:
  0.0 5.6 %copy-start = (f32[3,4,8,512]{3,2,1,0:T(8,128)S(1)}, f32[3,4,8,512]{3,2,1,0:T(8,128)}, u32[]{:S(2)}) copy-start(f32[3,4,8,512]{3,2,1,0:T(8,128)} %load.3) | copy-start | bytes 589828
  0.0 5.6 %copy-start.1 = (s32[4,8,512]{2,1,0:T(8,128)S(1)}, s32[4,8,512]{2,1,0:T(8,128)}, u32[]{:S(2)}) copy-start(s32[4,8,512]{2,1,0:T(8,128)} %density.3) | copy-start | bytes 196612
  0.0 5.6 %copy-start.2 = (s32[4,8,512]{2,1,0:T(8,128)S(1)}, s32[4,8,512]{2,1,0:T(8,128)}, u32[]{:S(2)}) copy-start(s32[4,8,512]{2,1,0:T(8,128)} %fixed.3) | copy-start | bytes 196612
  0.0 5.6 %copy-start.3 = (s32[4,8,512]{2,1,0:T(8,128)S(1)}, s32[4,8,512]{2,1,0:T(8,128)}, u32[]{:S(2)}) copy-start(s32[4,8,512]{2,1,0:T(8,128)} %loaded.3) | copy-start | bytes 196612
  1.6 9.3 %collective-permute-start = (f32[5,8,512]{2,1,0:T(8,128)}, f32[5,8,512]{2,1,0:T(8,128)S(1)}, u32[]{:S(2)}, u32[]{:S(2)}) collective-permute-start(f32[5,8,512]{2,1,0:T(8,128)} %shard_map.47), channel_id=1, source_target_pairs={{16,32},{32,16},{48,64},{64,48},{80,96},{96,80},{112,128},{128,112... | collective-permute-start | bytes 245768 | tf_op jit(solution)/shard_map/ppermute | solution.py:370
  6.3 4.6 %collective-permute-start.1 = (f32[5,8,512]{2,1,0:T(8,128)S(1)}, f32[5,8,512]{2,1,0:T(8,128)S(1)}, u32[]{:S(2)}, u32[]{:S(2)}) collective-permute-start(f32[5,8,512]{2,1,0:T(8,128)S(1)} %get-tuple-element.8), channel_id=1, source_target_pairs={{0,16},{16,0},{32,48},{48,32},{64,80},{80,64},{96,112},{112,96},{1... | collective-permute-start | bytes 245768 | tf_op jit(solution)/shard_map/ppermute | solution.py:365
  11.1 9.4 %collective-permute-start.3 = (f32[38,512]{1,0:T(8,128)S(1)}, f32[38,512]{1,0:T(8,128)S(1)}, u32[]{:S(2)}, u32[]{:S(2)}) collective-permute-start(f32[38,512]{1,0:T(8,128)S(1)} %pad_maximum_fusion.4), channel_id=1, source_target_pairs={{1,0},{2,1},{3,2},{4,3},{5,4},{6,5},{7,6},{8,7},{9,8},{10,9},{11,1... | collective-permute-start | bytes 233480 | tf_op jit(solution)/shard_map/ppermute | solution.py:379
  13.0 7.4 %collective-permute-start.2 = (f32[30,512]{1,0:T(8,128)S(1)}, f32[30,512]{1,0:T(8,128)S(1)}, u32[]{:S(2)}, u32[]{:S(2)}) collective-permute-start(f32[30,512]{1,0:T(8,128)S(1)} %reshape.69), channel_id=1, source_target_pairs={{0,1},{1,2},{2,3},{3,4},{4,5},{5,6},{6,7},{7,8},{8,9},{9,10},{10,1... | collective-permute-start | bytes 184328 | tf_op jit(solution)/shard_map/ppermute | solution.py:380
  21.7 9.0 %collective-permute-start.5 = (f32[28,256]{1,0:T(8,128)S(1)}, f32[28,256]{1,0:T(8,128)S(1)}, u32[]{:S(2)}, u32[]{:S(2)}) collective-permute-start(f32[28,256]{1,0:T(8,128)S(1)} %pad_maximum_fusion.6), channel_id=1, source_target_pairs={{1,0},{2,1},{3,2},{4,3},{5,4},{6,5},{7,6},{8,7},{9,8},{10,9},{11,1... | collective-permute-start | bytes 86024 | tf_op jit(solution)/shard_map/ppermute | solution.py:379
  23.6 7.0 %collective-permute-start.4 = (f32[20,256]{1,0:T(8,128)S(1)}, f32[20,256]{1,0:T(8,128)S(1)}, u32[]{:S(2)}, u32[]{:S(2)}) collective-permute-start(f32[20,256]{1,0:T(8,128)S(1)} %reshape.74), channel_id=1, source_target_pairs={{0,1},{1,2},{2,3},{3,4},{4,5},{5,6},{6,7},{7,8},{8,9},{9,10},{10,1... | collective-permute-start | bytes 61448 | tf_op jit(solution)/shard_map/ppermute | solution.py:380
  30.8 9.2 %collective-permute-start.6 = (f32[88,256]{1,0:T(8,128)S(1)}, f32[88,256]{1,0:T(8,128)S(1)}, u32[]{:S(2)}, u32[]{:S(2)}) collective-permute-start(f32[88,256]{1,0:T(8,128)S(1)} %pad_maximum_fusion.1), channel_id=1, source_target_pairs={{16,32},{32,16},{48,64},{64,48},{80,96},{96,80},{112,128},{128,112... | collective-permute-start | bytes 270344 | tf_op jit(solution)/shard_map/ppermute | solution.py:370
  33.7 3.2 %collective-permute-start.7 = (f32[80,256]{1,0:T(8,128)S(1)}, f32[80,256]{1,0:T(8,128)S(1)}, u32[]{:S(2)}, u32[]{:S(2)}) collective-permute-start(f32[80,256]{1,0:T(8,128)S(1)} %bitcast.13), channel_id=1, source_target_pairs={{0,16},{16,0},{32,48},{48,32},{64,80},{80,64},{96,112},{112,96},{1... | collective-permute-start | bytes 245768 | tf_op jit(solution)/shard_map/ppermute | solution.py:365
  41.0 8.8 %all-to-all-start = ((f32[16,10,128]{2,1,0:T(8,128)}), f32[16,10,128]{2,1,0:T(8,128)S(1)}, u32[]{:S(2)}, u32[]{:S(2)}) async-start(f32[16,10,128]{2,1,0:T(8,128)} %shard_map.49), calls=%async_computation | async-start | bytes 262144 | tf_op jit(solution)/shard_map/all_to_all | solution.py:399
  49.8 7.4 %collective-permute-start.8 = (f32[8,10,128]{2,1,0:T(8,128)S(1)}, f32[8,10,128]{2,1,0:T(8,128)S(1)}, u32[]{:S(2)}, u32[]{:S(2)}) collective-permute-start(f32[8,10,128]{2,1,0:T(8,128)S(1)} %slice_select_fusion.3), channel_id=1, source_target_pairs={{0,128},{16,144},{32,160},{48,176},{128,256},{144,272},{160,288},{... | collective-permute-start | bytes 122888 | tf_op jit(solution)/shard_map/ppermute | solution.py:404
  57.3 14.9 %collective-permute-start.9 = (f32[180,128]{1,0:T(8,128)S(1)}, f32[180,128]{1,0:T(8,128)S(1)}, u32[]{:S(2)}, u32[]{:S(2)}) collective-permute-start(f32[180,128]{1,0:T(8,128)S(1)} %reshape.81), channel_id=1, source_target_pairs={{1,2},{2,1},{3,4},{4,3},{5,6},{6,5},{7,8},{8,7},{9,10},{10,9},{11,... | collective-permute-start | bytes 276488 | tf_op jit(solution)/shard_map/ppermute | solution.py:370
  64.0 8.2 %collective-permute-start.10 = (f32[90,128]{1,0:T(8,128)S(1)}, f32[90,128]{1,0:T(8,128)S(1)}, u32[]{:S(2)}, u32[]{:S(2)}) collective-permute-start(f32[90,128]{1,0:T(8,128)S(1)} %reshape.82), channel_id=1, source_target_pairs={{2,0},{1,3},{4,2},{3,5},{6,4},{5,7},{8,6},{7,9},{10,8},{9,11},{12,... | collective-permute-start | bytes 138248 | tf_op jit(solution)/shard_map/ppermute | solution.py:413

commit v6 on v5

--- a/solution.py
+++ b/solution.py
@@ -63,8 +63,9 @@
     if len(tiles) == 1:
         return pltpu.roll(a, n - 1, 0), pltpu.roll(a, 1, 0)
     row = iota(a.shape, 0)
-    after = pltpu.roll(jnp.where(row == 0, tiles[1], a), n - 1, 0)
-    before = pltpu.roll(jnp.where(row == n - 1, tiles[1], a), 1, 0)
+    rim = tiles[1] if n == 8 else jnp.concatenate([tiles[1]] * 2, axis=0)
+    after = pltpu.roll(jnp.where(row == 0, rim, a), n - 1, 0)
+    before = pltpu.roll(jnp.where(row == n - 1, rim, a), 1, 0)
     return after, before
 
 
@@ -159,47 +160,94 @@
     return [factor * c for c in load] + [stiff, free]
 
 
-def edge_kernel(even, density, fixed, loaded, load, outer, *scratch):
-    plane = jnp.where(even[0] == 1, 0, 3)
-    sources = [a.at[plane] for a in (density, fixed, loaded)] + [load.at[:, plane]]
-    run_copies(zip(sources, scratch[:4]), scratch[4])
-    d, x, m, f = scratch[:4]
-    values = start_values(d[...], x[...], m[...], [f[c] for c in range(3)])
-    for k in range(5):
-        outer[k] = values[k]
-
-
-def prepare_kernel(even, density, fixed, loaded, load, fine, inner, *scratch):
+def rows_kernel(density, fixed, loaded, load, low, high, *scratch):
     run_copies(zip((density, fixed, loaded, load), scratch[:4]), scratch[4])
     d, x, m, f = scratch[:4]
-    is_even = even[0] == 1
-    kept = {}
+    low[0:8] = jnp.zeros((8, low.shape[1]), F32)
+    high[96:104] = jnp.zeros((8, low.shape[1]), F32)
+    for p in range(4):
+        values = start_values(d[p], x[p], m[p], [f[c, p] for c in range(3)])
+        for k in range(5):
+            at = 5 * (4 * k + p)
+            low[8 + at : 13 + at] = values[k][0:5]
+            high[at : at + 5] = values[k][3:8]
+
+
+def fine_kernel(density, fixed, loaded, load, fine, *scratch):
+    run_copies(zip((density, fixed, loaded, load), scratch[:4]), scratch[4])
+    d, x, m, f = scratch[:4]
     for p in range(4):
         values = start_values(d[p], x[p], m[p], [f[c, p] for c in range(3)])
         for k in range(5):
             fine[k, p] = values[k]
-        kept[p] = values
+
+
+def rim_tile(after, before):
+    row = iota((8, after.shape[1]), 0)
+    return jnp.where(row == 0, after, before)
+
+
+def own_rows(fine, low, high, k, p):
+    at = 5 * (4 * k + p)
+    row = iota((8, fine.shape[3]), 0)
+    turned = pltpu.roll(fine[k, p], 4, 0)
+    first = jnp.where(row < 4, high[at + 1 : at + 9], turned)
+    last = jnp.where(row < 4, turned, low[at + 4 : at + 12])
+    rim = rim_tile(low[at + 12 : at + 13], high[at : at + 1])
+    return jnp.concatenate([first, last], axis=0), rim
+
+
+def side_rows(side, k):
+    at = 80 + 2 * k
+    rim = rim_tile(side[at + 1 : at + 2], side[at : at + 1])
+    return side[16 * k : 16 * k + 16], rim
+
+
+def sides_kernel(even, fine, low, high, outer, inner):
+    is_even = even[0] == 1
     for k in range(5):
-        inner[k] = jnp.where(is_even, kept[3][k], kept[0][k])
-
-
-def fine_tiles(fine, before, after, row_before, row_after):
-    row = iota((8, fine.shape[3]), 0)
+        first, last = [own_rows(fine, low, high, k, p)[0] for p in (0, 3)]
+        outer[16 * k : 16 * k + 16] = jnp.where(is_even, first, last)
+        inner[16 * k : 16 * k + 16] = jnp.where(is_even, last, first)
+        ends = []
+        for p in (0, 3):
+            at = 5 * (4 * k + p)
+            ends.append((high[at : at + 1], low[at + 12 : at + 13]))
+        for j in range(2):
+            first, last = ends[0][j], ends[1][j]
+            at = 80 + 2 * k + j
+            outer[at : at + 1] = jnp.where(is_even, first, last)
+            inner[at : at + 1] = jnp.where(is_even, last, first)
+    outer[90:104] = jnp.zeros((14, low.shape[1]), F32)
+    inner[90:96] = jnp.zeros((6, low.shape[1]), F32)
+
+
+def fine_tiles(fine, low, high, before, after):
     result = []
     for p in range(6):
         here = []
-        for f in range(5):
-            main = before[f] if p == 0 else after[f] if p == 5 else fine[f, p - 1]
-            rim = jnp.where(
-                row == 0, row_after[f, pl.ds(p, 1), :], row_before[f, pl.ds(p, 1), :]
-            )
+        for k in range(5):
+            if p in (0, 5):
+                side, at = before if p == 0 else after, 16 * k
+                main = side[at + 4 : at + 12]
+                rim = rim_tile(side[at + 12 : at + 13], side[at + 3 : at + 4])
+            else:
+                at = 5 * (4 * k + p - 1)
+                main = fine[k, p - 1]
+                rim = rim_tile(low[at + 8 : at + 9], high[at + 4 : at + 5])
             here.append((main, rim))
         result.append(here)
     return result
 
 
-def fine_residual_kernel(fine, before, after, row_before, row_after, mid):
-    tiles = fine_tiles(fine, before, after, row_before, row_after)
+def fine_residual_kernel(fine, low, high, before, after, mid):
+    tiles = []
+    for p in range(6):
+        if p in (0, 5):
+            side = before if p == 0 else after
+            tiles.append([side_rows(side, k) for k in range(5)])
+        else:
+            tiles.append([own_rows(fine, low, high, k, p - 1) for k in range(5)])
     v = [t[:3] for t in tiles]
     s = [t[3] for t in tiles]
     planes = range(1, 5)
@@ -212,19 +260,20 @@
             rows[c].append(free * (back * v[p][c][0] - image[p][c]))
         rows[3].append(stiff)
         rows[4].append(free)
-    row = iota((8, rows[0][0].shape[1]), 0)
+    row = iota((8, fine.shape[3]), 0)
     index = row % 4 * 2
     for f in range(5):
-        halves = []
         for x in (0, 2):
             both = rows[f][x] + rows[f][x + 1]
-            halves.append(pick_rows(both + pltpu.roll(both, 7, 0), index))
-        total = pool_lanes(jnp.where(row < 4, halves[0], halves[1]))
-        if f == 3:
-            total = total * 0.125
-        if f == 4:
-            total = (total > 0.5).astype(F32)
-        mid[8 * f : 8 * f + 8] = total
+            both = both + pltpu.roll(both, 15, 0)
+            halves = [pick_rows(both[at : at + 8], index) for at in (0, 8)]
+            total = pool_lanes(jnp.where(row < 4, halves[0], halves[1]))
+            if f == 3:
+                total = total * 0.125
+            if f == 4:
+                total = (total > 0.5).astype(F32)
+            at = 16 * f + 4 * x
+            mid[at : at + 8] = total
 
 
 def mid_fields(mids):
@@ -271,10 +320,10 @@
     mid,
     mid_after,
     fine,
+    row_after,
+    row_before,
     before,
     after,
-    row_before,
-    row_after,
     out,
     held,
     sems,
@@ -320,7 +369,7 @@
         for p in planes:
             a = v[p][c][0] + first[p][c][0] - gains[p] * image[p][c]
             raised[c].append([spread_lanes(pick_rows(a, index)) for index in picks])
-    tiles = fine_tiles(fine, before, after, row_before, row_after)
+    tiles = fine_tiles(fine, row_after, row_before, before, after)
     s = [t[3] for t in tiles]
     v = []
     for p in range(6):
@@ -370,15 +419,6 @@
     return lax.ppermute(
         value, axis, [(i, ((i + 1) ^ 1) - 1) for i in range(1, n - 1)]
     )
-
-
-def shifts(low, high, axis):
-    n = lax.axis_size(axis)
-    rows = low.shape[0]
-    low = jnp.concatenate([low, low[:EXTRA]])
-    after = lax.ppermute(low, axis, [(i + 1, i) for i in range(n - 1)])[:rows]
-    before = lax.ppermute(high, axis, [(i, i + 1) for i in range(n - 1)])
-    return before, after
 
 
 def swaps(value, axis):
@@ -421,44 +461,34 @@
 
 def per_device(density, fixed, loaded, load):
     nz = density.shape[2]
+    args = (density, fixed, loaded, load)
+    sems = pltpu.SemaphoreType.DMA((4,))
+    inputs = dict(
+        ins=[HBM] * 4, scratch=[pltpu.VMEM(a.shape, a.dtype) for a in args] + [sems]
+    )
+    low_rows, high_rows = call(
+        rows_kernel, [(108, nz), (104, nz)], *args, limit=60, **inputs
+    )
+    n = lax.axis_size("gy")
+    row_after = lax.ppermute(low_rows, "gy", [(i + 1, i) for i in range(n - 1)])
+    row_before = lax.ppermute(high_rows, "gy", [(i, i + 1) for i in range(n - 1)])
+    fine = call(fine_kernel, [(5, 4, 8, nz)], *args, **inputs)
+
     even = lax.axis_index("gx") % 2 == 0
-    args = (even.astype(jnp.int32).reshape(1), density, fixed, loaded, load)
-    ins = [SMEM] + [HBM] * 4
-    sems = pltpu.SemaphoreType.DMA((4,))
-    outer = call(
-        edge_kernel,
-        [(5, 8, nz)],
-        *args,
-        ins=ins,
-        scratch=[pltpu.VMEM((8, nz), a.dtype) for a in args[1:4]]
-        + [pltpu.VMEM((3, 8, nz), F32), sems],
-        limit=60,
-    )
-    outer = outer_swap(outer, "gx")
-    fine, inner = call(
-        prepare_kernel,
-        [(5, 4, 8, nz), (5, 8, nz)],
-        *args,
-        ins=ins,
-        scratch=[pltpu.VMEM(a.shape, a.dtype) for a in args[1:]] + [sems],
-    )
-    inner = inner_swap(inner, "gx")
+    outer, inner = call(
+        sides_kernel,
+        [(104, nz), (96, nz)],
+        even.astype(jnp.int32).reshape(1),
+        fine,
+        row_after,
+        row_before,
+        ins=[SMEM] + [VMEM] * 3,
+    )
+    outer, inner = outer_swap(outer, "gx")[:96], inner_swap(inner, "gx")
     before, after = jnp.where(even, outer, inner), jnp.where(even, inner, outer)
-
-    def edge(row):
-        planes = [before[:, None, row], fine[:, :, row], after[:, None, row]]
-        return jnp.concatenate(planes, axis=1).reshape(30, nz)
-
-    rims = [r.reshape(5, 6, nz) for r in shifts(edge(0), edge(7), "gy")]
-    fine_args = (fine, before, after, *rims)
-    mid = call(fine_residual_kernel, [(40, nz // 2)], *fine_args)
-
-    mid = mid.reshape(5, 2, 4, nz // 2)
-    rows = shifts(
-        mid[:, :, :2].reshape(20, nz // 2), mid[:, :, 2:].reshape(20, nz // 2), "gy"
-    )
-    rows = [r.reshape(5, 2, 2, nz // 2) for r in rows]
-    mid = jnp.concatenate([rows[0], mid, rows[1]], axis=2).reshape(80, nz // 2)
+    fine_args = (fine, row_after, row_before, before, after)
+    mid = call(fine_residual_kernel, [(80, nz // 2)], *fine_args)
+
     sides = swaps(mid, "gx")
     mids = [a.reshape(5, 2, 8, nz // 2) for a in (sides[0], mid, sides[1])]
     low = call(mid_residual_kernel, [(16, 10, nz // 4)], *mids)

time: 76.1 us -> 72.3 us (0.950)
  starting transfers between devices: 44 us -> 36.3 us
  waiting for transfers between devices: 22.7 us -> 25.7 us
  Pallas kernels: 7.15 us -> 8.69 us
    ppermute x4 -> x2, starting transfers between devices: 14.8 us -> 7.41 us  [the longest x1 5.49 us: per_device(): lax.ppermute(high_rows, 'gy', [(i, i + 1) for i in range(n - 1)])]
    pallas_call x5 -> x6, Pallas kernels: 7.15 us -> 8.69 us  [call(): pl.pallas_call(kernel, out_shape=results if len(results) > 1 else results...]
    ppermute x3, waiting for transfers between devices: 5.67 us -> 6.87 us  [outer_swap(): lax.ppermute(value, axis, [(i, (i + 1 ^ 1) - 1) for i in range(1, n - 1)])]
    ppermute x2, waiting for transfers between devices: 1.25 us -> 2.29 us  [inner_swap(): lax.ppermute(value, axis, [(i, i ^ 1) for i in range(lax.axis_size(axis))])]
    ppermute x4 -> x2, waiting for transfers between devices: 3.39 us -> 4.14 us  [the longest x1 4.14 us: per_device(): lax.ppermute(high_rows, 'gy', [(i, i + 1) for i in range(n - 1)])]
  transfers between devices with their start and end apart: 12 -> 10, of which waited for: 8 -> 8; matrix products, arithmetic and copies ran while one was open for 0% -> 0% of each run, Pallas kernels for 1% -> 1%
where the time goes in v6:
time: 72.3 us; the launch traced here: 71.9 us
  starting transfers between devices  36.3 us (50%)
  waiting for transfers between devices  25.7 us (36%)
  Pallas kernels  8.69 us (12%)
    ppermute x3, starting transfers between devices, outer_swap(): lax.ppermute(value, axis, [(i, (i + 1 ^ 1) - 1) for i in range(1, n - 1)])  13 us
    pallas_call x6, Pallas kernels, call(): pl.pallas_call(kernel, out_shape=results if len(results) > 1 else results...  8.69 us
    ppermute x3, waiting for transfers between devices, outer_swap(): lax.ppermute(value, axis, [(i, (i + 1 ^ 1) - 1) for i in range(1, n - 1)])  6.87 us
    ppermute x1, starting transfers between devices, gather_low(): beyond = lax.ppermute(own, 'gy', moves).reshape(9, 1, 10, nz)  6.39 us
    ppermute x1, starting transfers between devices, per_device(): lax.ppermute(high_rows, 'gy', [(i, i + 1) for i in range(n - 1)])  5.49 us
    ppermute x1, waiting for transfers between devices, gather_low(): other = lax.ppermute(jnp.where(first, row[8:], row[:8]), 'gx', moves)  5.41 us
    all_to_all x1, waiting for transfers between devices, gather_low(): row = lax.all_to_all(low, ('gx', 'gy'), 0, 0, axis_index_groups=groups)  5.37 us
    ppermute x2, starting transfers between devices, inner_swap(): lax.ppermute(value, axis, [(i, i ^ 1) for i in range(lax.axis_size(axis))])  4.22 us
  transfers between devices with their start and end apart: 10, of which 8 were waited for; matrix products, arithmetic and copies ran while one was open for 0% of the time, Pallas kernels for 1%

profile of v6, /device:TPU:224, one launch (start us, length us, event | category | flops | bytes accessed | tf_op | source)
XLA Modules:
  0.0 71.9 jit_solution(5843386474327186352)
XLA Ops:
  0.0 2.0 %shard_map.47 = (f32[108,512]{1,0:T(8,128)}, f32[104,512]{1,0:T(8,128)}) custom-call(s32[4,8,512]{2,1,0:T(8,128)} %density.3, s32[4,8,512]{2,1,0:T(8,128)} %fixed.3, s32[4,8,512]{2,1,0:T(8,128)} %loaded.3, f32[3,4,8,512]{3,2,1,0:T(8,128)} %load.3), custom_call_target="tpu_custom_call" | custom-call | tf_op jit(solution)/shard_map/pallas_call | solution.py:403
  2.0 1.9 %collective-permute-start = (f32[108,512]{1,0:T(8,128)}, f32[108,512]{1,0:T(8,128)S(1)}, u32[]{:S(2)}, u32[]{:S(2)}) collective-permute-start(f32[108,512]{1,0:T(8,128)} %get-tuple-element.9), channel_id=1, source_target_pairs={{1,0},{2,1},{3,2},{4,3},{5,4},{6,5},{7,6},{8,7},{9,8},{10,9},{11,1... | collective-permute-start | bytes 663560 | tf_op jit(solution)/shard_map/ppermute | solution.py:473
  3.9 5.5 %collective-permute-start.1 = (f32[104,512]{1,0:T(8,128)}, f32[104,512]{1,0:T(8,128)S(1)}, u32[]{:S(2)}, u32[]{:S(2)}) collective-permute-start(f32[104,512]{1,0:T(8,128)} %get-tuple-element.10), channel_id=1, source_target_pairs={{0,1},{1,2},{2,3},{3,4},{4,5},{5,6},{6,7},{7,8},{8,9},{9,10},{10,1... | collective-permute-start | bytes 638984 | tf_op jit(solution)/shard_map/ppermute | solution.py:474
  9.5 0.6 shard_map.46.fine
  10.1 4.1 %collective-permute-done.1.high.row_before = f32[104,512]{1,0:T(8,128)S(1)} collective-permute-done((f32[104,512]{1,0:T(8,128)}, f32[104,512]{1,0:T(8,128)S(1)}, u32[]{:S(2)}, u32[]{:S(2)}) %collective-permute-start.1) | collective-permute-done | bytes 213024 | tf_op jit(solution)/shard_map/ppermute | solution.py:474
  14.3 3.1 %collective-permute-start.2 = (f32[104,512]{1,0:T(8,128)S(1)}, f32[104,512]{1,0:T(8,128)S(1)}, u32[]{:S(2)}, u32[]{:S(2)}) collective-permute-start(f32[104,512]{1,0:T(8,128)S(1)} %get-tuple-element.11), channel_id=1, source_target_pairs={{16,32},{32,16},{48,64},{64,48},{80,96},{96,80},{112,128},{128,112... | collective-permute-start | bytes 638984 | tf_op jit(solution)/shard_map/ppermute | solution.py:419
  17.4 2.3 %collective-permute-start.3 = (f32[96,512]{1,0:T(8,128)S(1)}, f32[96,512]{1,0:T(8,128)S(1)}, u32[]{:S(2)}, u32[]{:S(2)}) collective-permute-start(f32[96,512]{1,0:T(8,128)S(1)} %get-tuple-element.12), channel_id=1, source_target_pairs={{0,16},{16,0},{32,48},{48,32},{64,80},{80,64},{96,112},{112,96},{1... | collective-permute-start | bytes 589832 | tf_op jit(solution)/shard_map/ppermute | solution.py:414
  19.7 1.0 %collective-permute-done.3 = f32[96,512]{1,0:T(8,128)S(1)} collective-permute-done((f32[96,512]{1,0:T(8,128)S(1)}, f32[96,512]{1,0:T(8,128)S(1)}, u32[]{:S(2)}, u32[]{:S(2)}) %collective-permute-start.3) | collective-permute-done | bytes 196640 | tf_op jit(solution)/shard_map/ppermute | solution.py:414
  20.8 4.0 %collective-permute-done.2 = f32[104,512]{1,0:T(8,128)S(1)} collective-permute-done((f32[104,512]{1,0:T(8,128)S(1)}, f32[104,512]{1,0:T(8,128)S(1)}, u32[]{:S(2)}, u32[]{:S(2)}) %collective-permute-start.2) | collective-permute-done | bytes 213024 | tf_op jit(solution)/shard_map/ppermute | solution.py:419
  24.8 2.2 %shard_map.49 = f32[80,256]{1,0:T(8,128)S(1)} custom-call(f32[5,4,8,512]{3,2,1,0:T(8,128)S(1)} %shard_map.46.fine, f32[108,512]{1,0:T(8,128)S(1)} %collective-permute-done.low.row_after, f32[104,512]{1,0:T(8,128)S(1)} %collective-permute-done.1.high.row_before, f32[96,512]{1,0:T(8,128)S(1)} %get-tuple-element.14.before, f32[96,512]{1,0:T(8,128)S(1)} %get-tuple-element.13.after), custom_call_target="tpu_custom_call" | custom-call | tf_op jit(solution)/shard_map/pallas_call | solution.py:403
  27.0 3.1 %collective-permute-start.4 = (f32[88,256]{1,0:T(8,128)S(1)}, f32[88,256]{1,0:T(8,128)S(1)}, u32[]{:S(2)}, u32[]{:S(2)}) collective-permute-start(f32[88,256]{1,0:T(8,128)S(1)} %pad_maximum_fusion.1), channel_id=1, source_target_pairs={{16,32},{32,16},{48,64},{64,48},{80,96},{96,80},{112,128},{128,112... | collective-permute-start | bytes 270344 | tf_op jit(solution)/shard_map/ppermute | solution.py:419
  30.1 1.9 %collective-permute-start.5 = (f32[80,256]{1,0:T(8,128)S(1)}, f32[80,256]{1,0:T(8,128)S(1)}, u32[]{:S(2)}, u32[]{:S(2)}) collective-permute-start(f32[80,256]{1,0:T(8,128)S(1)} %shard_map.49), channel_id=1, source_target_pairs={{0,16},{16,0},{32,48},{48,32},{64,80},{80,64},{96,112},{112,96},{1... | collective-permute-start | bytes 245768 | tf_op jit(solution)/shard_map/ppermute | solution.py:414
  32.1 1.2 %collective-permute-done.5 = f32[80,256]{1,0:T(8,128)S(1)} collective-permute-done((f32[80,256]{1,0:T(8,128)S(1)}, f32[80,256]{1,0:T(8,128)S(1)}, u32[]{:S(2)}, u32[]{:S(2)}) %collective-permute-start.5) | collective-permute-done | bytes 81952 | tf_op jit(solution)/shard_map/ppermute | solution.py:414
  33.3 2.9 %collective-permute-done.4 = f32[88,256]{1,0:T(8,128)S(1)} collective-permute-done((f32[88,256]{1,0:T(8,128)S(1)}, f32[88,256]{1,0:T(8,128)S(1)}, u32[]{:S(2)}, u32[]{:S(2)}) %collective-permute-start.4) | collective-permute-done | bytes 90144 | tf_op jit(solution)/shard_map/ppermute | solution.py:419
  36.2 1.1 %shard_map.50 = f32[16,10,128]{2,1,0:T(8,128)} custom-call(f32[5,2,8,256]{3,2,1,0:T(8,128)S(1)} %bitcast.11, f32[5,2,8,256]{3,2,1,0:T(8,128)S(1)} %bitcast.7, f32[5,2,8,256]{3,2,1,0:T(8,128)S(1)} %bitcast.9), custom_call_target="tpu_custom_call" | custom-call | tf_op jit(solution)/shard_map/pallas_call | solution.py:403
  37.3 3.4 %all-to-all-start = ((f32[16,10,128]{2,1,0:T(8,128)}), f32[16,10,128]{2,1,0:T(8,128)S(1)}, u32[]{:S(2)}, u32[]{:S(2)}) async-start(f32[16,10,128]{2,1,0:T(8,128)} %shard_map.50), calls=%async_computation | async-start | bytes 262144 | tf_op jit(solution)/shard_map/all_to_all | solution.py:439
  40.7 5.4 %all-to-all-done = f32[16,10,128]{2,1,0:T(8,128)S(1)} async-done(((f32[16,10,128]{2,1,0:T(8,128)}), f32[16,10,128]{2,1,0:T(8,128)S(1)}, u32[]{:S(2)}, u32[]{:S(2)}) %all-to-all-start) | async-done | bytes 81952 | tf_op jit(solution)/shard_map/all_to_all | solution.py:439
  46.1 1.9 %collective-permute-start.6 = (f32[8,10,128]{2,1,0:T(8,128)S(1)}, f32[8,10,128]{2,1,0:T(8,128)S(1)}, u32[]{:S(2)}, u32[]{:S(2)}) collective-permute-start(f32[8,10,128]{2,1,0:T(8,128)S(1)} %slice_select_fusion.5), channel_id=1, source_target_pairs={{0,128},{16,144},{32,160},{48,176},{128,256},{144,272},{160,288},{... | collective-permute-start | bytes 122888 | tf_op jit(solution)/shard_map/ppermute | solution.py:444
  48.0 5.4 %collective-permute-done.6 = f32[8,10,128]{2,1,0:T(8,128)S(1)} collective-permute-done((f32[8,10,128]{2,1,0:T(8,128)S(1)}, f32[8,10,128]{2,1,0:T(8,128)S(1)}, u32[]{:S(2)}, u32[]{:S(2)}) %collective-permute-start.6) | collective-permute-done | bytes 40992 | tf_op jit(solution)/shard_map/ppermute | solution.py:444
  53.5 6.7 %collective-permute-start.7 = (f32[180,128]{1,0:T(8,128)S(1)}, f32[180,128]{1,0:T(8,128)S(1)}, u32[]{:S(2)}, u32[]{:S(2)}) collective-permute-start(f32[180,128]{1,0:T(8,128)S(1)} %reshape.44), channel_id=1, source_target_pairs={{1,2},{2,1},{3,4},{4,3},{5,6},{6,5},{7,8},{8,7},{9,10},{10,9},{11,... | collective-permute-start | bytes 276488 | tf_op jit(solution)/shard_map/ppermute | solution.py:419
  60.3 6.4 %collective-permute-start.8 = (f32[90,128]{1,0:T(8,128)S(1)}, f32[90,128]{1,0:T(8,128)S(1)}, u32[]{:S(2)}, u32[]{:S(2)}) collective-permute-start(f32[90,128]{1,0:T(8,128)S(1)} %reshape.45), channel_id=1, source_target_pairs={{2,0},{1,3},{4,2},{3,5},{6,4},{5,7},{8,6},{7,9},{10,8},{9,11},{12,... | collective-permute-start | bytes 138248 | tf_op jit(solution)/shard_map/ppermute | solution.py:453
  66.9 1.6 %collective-permute-done.8 = f32[90,128]{1,0:T(8,128)S(1)} collective-permute-done((f32[90,128]{1,0:T(8,128)S(1)}, f32[90,128]{1,0:T(8,128)S(1)}, u32[]{:S(2)}, u32[]{:S(2)}) %collective-permute-start.8) | collective-permute-done | bytes 46112 | tf_op jit(solution)/shard_map/ppermute | solution.py:453
  68.7 0.2 reshape.46
  69.1 2.8 %shard_map.51 = f32[3,4,8,512]{3,2,1,0:T(8,128)} custom-call(f32[5,9,16,128]{3,2,1,0:T(8,128)S(1)} %pad_maximum_fusion.low, f32[5,2,8,256]{3,2,1,0:T(8,128)S(1)} %bitcast.12, f32[5,2,8,256]{3,2,1,0:T(8,128)S(1)} %bitcast.8, f32[5,2,8,256]{3,2,1,0:T(8,128)S(1)} %bitcast.10, f32[5,4,8,512]{3,2,1,0:T(8,128)S(1)} %shard_map.46.fine, ...), custom_call_target="tpu_custom_call" | custom-call | tf_op jit(solution)/shard_map/pallas_call | solution.py:403
  (30 shorter events, 0.8 us)
Async XLA Ops:
  0.0 9.4 %copy-start = (f32[3,4,8,512]{3,2,1,0:T(8,128)S(1)}, f32[3,4,8,512]{3,2,1,0:T(8,128)}, u32[]{:S(2)}) copy-start(f32[3,4,8,512]{3,2,1,0:T(8,128)} %load.3) | copy-start | bytes 589828
  0.0 9.4 %copy-start.1 = (s32[4,8,512]{2,1,0:T(8,128)S(1)}, s32[4,8,512]{2,1,0:T(8,128)}, u32[]{:S(2)}) copy-start(s32[4,8,512]{2,1,0:T(8,128)} %density.3) | copy-start | bytes 196612
  0.0 9.4 %copy-start.2 = (s32[4,8,512]{2,1,0:T(8,128)S(1)}, s32[4,8,512]{2,1,0:T(8,128)}, u32[]{:S(2)}) copy-start(s32[4,8,512]{2,1,0:T(8,128)} %fixed.3) | copy-start | bytes 196612
  0.0 9.4 %copy-start.3 = (s32[4,8,512]{2,1,0:T(8,128)S(1)}, s32[4,8,512]{2,1,0:T(8,128)}, u32[]{:S(2)}) copy-start(s32[4,8,512]{2,1,0:T(8,128)} %loaded.3) | copy-start | bytes 196612
  2.0 12.2 %collective-permute-start = (f32[108,512]{1,0:T(8,128)}, f32[108,512]{1,0:T(8,128)S(1)}, u32[]{:S(2)}, u32[]{:S(2)}) collective-permute-start(f32[108,512]{1,0:T(8,128)} %get-tuple-element.9), channel_id=1, source_target_pairs={{1,0},{2,1},{3,2},{4,3},{5,4},{6,5},{7,6},{8,7},{9,8},{10,9},{11,1... | collective-permute-start | bytes 663560 | tf_op jit(solution)/shard_map/ppermute | solution.py:473
  3.9 10.3 %collective-permute-start.1 = (f32[104,512]{1,0:T(8,128)}, f32[104,512]{1,0:T(8,128)S(1)}, u32[]{:S(2)}, u32[]{:S(2)}) collective-permute-start(f32[104,512]{1,0:T(8,128)} %get-tuple-element.10), channel_id=1, source_target_pairs={{0,1},{1,2},{2,3},{3,4},{4,5},{5,6},{6,7},{7,8},{8,9},{9,10},{10,1... | collective-permute-start | bytes 638984 | tf_op jit(solution)/shard_map/ppermute | solution.py:474
  14.3 10.5 %collective-permute-start.2 = (f32[104,512]{1,0:T(8,128)S(1)}, f32[104,512]{1,0:T(8,128)S(1)}, u32[]{:S(2)}, u32[]{:S(2)}) collective-permute-start(f32[104,512]{1,0:T(8,128)S(1)} %get-tuple-element.11), channel_id=1, source_target_pairs={{16,32},{32,16},{48,64},{64,48},{80,96},{96,80},{112,128},{128,112... | collective-permute-start | bytes 638984 | tf_op jit(solution)/shard_map/ppermute | solution.py:419
  17.4 3.4 %collective-permute-start.3 = (f32[96,512]{1,0:T(8,128)S(1)}, f32[96,512]{1,0:T(8,128)S(1)}, u32[]{:S(2)}, u32[]{:S(2)}) collective-permute-start(f32[96,512]{1,0:T(8,128)S(1)} %get-tuple-element.12), channel_id=1, source_target_pairs={{0,16},{16,0},{32,48},{48,32},{64,80},{80,64},{96,112},{112,96},{1... | collective-permute-start | bytes 589832 | tf_op jit(solution)/shard_map/ppermute | solution.py:414
  27.0 9.2 %collective-permute-start.4 = (f32[88,256]{1,0:T(8,128)S(1)}, f32[88,256]{1,0:T(8,128)S(1)}, u32[]{:S(2)}, u32[]{:S(2)}) collective-permute-start(f32[88,256]{1,0:T(8,128)S(1)} %pad_maximum_fusion.1), channel_id=1, source_target_pairs={{16,32},{32,16},{48,64},{64,48},{80,96},{96,80},{112,128},{128,112... | collective-permute-start | bytes 270344 | tf_op jit(solution)/shard_map/ppermute | solution.py:419
  30.1 3.2 %collective-permute-start.5 = (f32[80,256]{1,0:T(8,128)S(1)}, f32[80,256]{1,0:T(8,128)S(1)}, u32[]{:S(2)}, u32[]{:S(2)}) collective-permute-start(f32[80,256]{1,0:T(8,128)S(1)} %shard_map.49), channel_id=1, source_target_pairs={{0,16},{16,0},{32,48},{48,32},{64,80},{80,64},{96,112},{112,96},{1... | collective-permute-start | bytes 245768 | tf_op jit(solution)/shard_map/ppermute | solution.py:414
  37.3 8.8 %all-to-all-start = ((f32[16,10,128]{2,1,0:T(8,128)}), f32[16,10,128]{2,1,0:T(8,128)S(1)}, u32[]{:S(2)}, u32[]{:S(2)}) async-start(f32[16,10,128]{2,1,0:T(8,128)} %shard_map.50), calls=%async_computation | async-start | bytes 262144 | tf_op jit(solution)/shard_map/all_to_all | solution.py:439
  46.1 7.4 %collective-permute-start.6 = (f32[8,10,128]{2,1,0:T(8,128)S(1)}, f32[8,10,128]{2,1,0:T(8,128)S(1)}, u32[]{:S(2)}, u32[]{:S(2)}) collective-permute-start(f32[8,10,128]{2,1,0:T(8,128)S(1)} %slice_select_fusion.5), channel_id=1, source_target_pairs={{0,128},{16,144},{32,160},{48,176},{128,256},{144,272},{160,288},{... | collective-permute-start | bytes 122888 | tf_op jit(solution)/shard_map/ppermute | solution.py:444
  53.5 14.9 %collective-permute-start.7 = (f32[180,128]{1,0:T(8,128)S(1)}, f32[180,128]{1,0:T(8,128)S(1)}, u32[]{:S(2)}, u32[]{:S(2)}) collective-permute-start(f32[180,128]{1,0:T(8,128)S(1)} %reshape.44), channel_id=1, source_target_pairs={{1,2},{2,1},{3,4},{4,3},{5,6},{6,5},{7,8},{8,7},{9,10},{10,9},{11,... | collective-permute-start | bytes 276488 | tf_op jit(solution)/shard_map/ppermute | solution.py:419
  60.3 8.1 %collective-permute-start.8 = (f32[90,128]{1,0:T(8,128)S(1)}, f32[90,128]{1,0:T(8,128)S(1)}, u32[]{:S(2)}, u32[]{:S(2)}) collective-permute-start(f32[90,128]{1,0:T(8,128)S(1)} %reshape.45), channel_id=1, source_target_pairs={{2,0},{1,3},{4,2},{3,5},{6,4},{5,7},{8,6},{7,9},{10,8},{9,11},{12,... | collective-permute-start | bytes 138248 | tf_op jit(solution)/shard_map/ppermute | solution.py:453

commit v7 on v6

--- a/solution.py
+++ b/solution.py
@@ -49,9 +49,14 @@
     t, d = [], []
     for a in tiles:
         n = a.shape[1]
-        lane = iota(a.shape, 1)
-        after = jnp.where(lane == n - 1, 0.0, pltpu.roll(a, n - 1, 1))
-        before = jnp.where(lane == 0, 0.0, pltpu.roll(a, 1, 1))
+        after, before = pltpu.roll(a, n - 1, 1), pltpu.roll(a, 1, 1)
+        lane = iota((a.shape[0], 128), 1)
+        last = jnp.where(lane == 127, 0.0, after[:, n - 128 :])
+        first = jnp.where(lane == 0, 0.0, before[:, :128])
+        if n > 128:
+            last = jnp.concatenate([after[:, : n - 128], last], axis=1)
+            first = jnp.concatenate([first, before[:, 128:]], axis=1)
+        after, before = last, first
         t.append((after + before) + 2.0 * a)
         d.append(after - before)
     return tuple(t), tuple(d)
@@ -314,6 +319,18 @@
         low[k, 8:10] = last
 
 
+def low_tiles(low, p, f):
+    at = 2 if f == 4 else 0
+    row = iota((8, low.shape[3]), 0)
+    index = 2 * f - at + (row + 1) % 2
+    picks = [pick_rows(low[p, b, at : at + 8], index) for b in range(5)]
+    main = picks[0]
+    for b in range(1, 5):
+        main = jnp.where(row >= 2 * b - 1, picks[b], main)
+    after = low[p, 4, 2 * f + 1 : 2 * f + 2]
+    return main, rim_tile(after, low[p, 0, 2 * f : 2 * f + 1])
+
+
 def finish_kernel(
     low,
     mid_before,
@@ -328,11 +345,11 @@
     held,
     sems,
 ):
-    parts = [slice(0, 8), slice(8, 16)]
-    s = [tuple(low[3, p, k] for k in parts) for p in range(9)]
-    gains = [tuple(gain(low[3, p, k], low[4, p, k]) for k in parts) for p in range(9)]
+    fields = [[low_tiles(low, p, f) for f in range(5)] for p in range(9)]
+    s = [f[3] for f in fields]
+    gains = [tuple(gain(f[3][k], f[4][k]) for k in range(2)) for f in fields]
     first = [
-        [tuple(0.25 * gains[p][k] * low[c, p, parts[k]] for k in range(2)) for c in range(3)]
+        [tuple(0.25 * gains[p][k] * fields[p][c][k] for k in range(2)) for c in range(3)]
         for p in range(9)
     ]
     v = dict(enumerate(first))
@@ -441,7 +458,8 @@
     first = place < 4
     moves = [(j, j + 8) for j in range(nx - 8) if j % 8 < 4]
     moves += [(j, j - 8) for j in range(8, nx) if j % 8 >= 4]
-    other = lax.ppermute(jnp.where(first, row[8:], row[:8]), "gx", moves)
+    half = jnp.where(first, row[8:], row[:8]).reshape(80, nz)
+    other = lax.ppermute(half, "gx", moves).reshape(8, 10, nz)
     planes = jnp.where(
         first, jnp.concatenate([other, row]), jnp.concatenate([row, other])
     )
@@ -492,11 +510,7 @@
     sides = swaps(mid, "gx")
     mids = [a.reshape(5, 2, 8, nz // 2) for a in (sides[0], mid, sides[1])]
     low = call(mid_residual_kernel, [(16, 10, nz // 4)], *mids)
-    low = gather_low(low).reshape(9, 5, 5, 2, nz // 4)
-    low = low.transpose(2, 0, 1, 3, 4).reshape(5, 9, 10, nz // 4)
-    low = jnp.concatenate(
-        [low[:, :, 1:], jnp.zeros((5, 9, 6, nz // 4), F32), low[:, :, :1]], axis=2
-    )
+    low = gather_low(low)
     return call(
         finish_kernel,
         [(3, 4, 8, nz)],

time: 72.3 us -> 71.5 us (0.989)
  no operation moved by 1% of the time
where the time goes in v7:
time: 71.5 us; the launch traced here: 71.1 us
  starting transfers between devices  36.3 us (51%)
  waiting for transfers between devices  25.5 us (36%)
  Pallas kernels  8.7 us (12%)
    ppermute x3, starting transfers between devices, outer_swap(): lax.ppermute(value, axis, [(i, (i + 1 ^ 1) - 1) for i in range(1, n - 1)])  13 us
    pallas_call x6, Pallas kernels, call(): pl.pallas_call(kernel, out_shape=results if len(results) > 1 else results...  8.7 us
    ppermute x3, waiting for transfers between devices, outer_swap(): lax.ppermute(value, axis, [(i, (i + 1 ^ 1) - 1) for i in range(1, n - 1)])  6.87 us
    ppermute x1, starting transfers between devices, gather_low(): beyond = lax.ppermute(own, 'gy', moves).reshape(9, 1, 10, nz)  6.39 us
    ppermute x1, starting transfers between devices, per_device(): lax.ppermute(high_rows, 'gy', [(i, i + 1) for i in range(n - 1)])  5.49 us
    all_to_all x1, waiting for transfers between devices, gather_low(): row = lax.all_to_all(low, ('gx', 'gy'), 0, 0, axis_index_groups=groups)  5.37 us
    ppermute x1, waiting for transfers between devices, gather_low(): other = lax.ppermute(half, 'gx', moves).reshape(8, 10, nz)  5.14 us
    ppermute x2, starting transfers between devices, inner_swap(): lax.ppermute(value, axis, [(i, i ^ 1) for i in range(lax.axis_size(axis))])  4.22 us
  transfers between devices with their start and end apart: 10, of which 8 were waited for; matrix products, arithmetic and copies ran while one was open for 0% of the time, Pallas kernels for 1%

profile of v7, /device:TPU:224, one launch (start us, length us, event | category | flops | bytes accessed | tf_op | source)
XLA Modules:
  0.0 71.1 jit_solution(8692353252761998137)
XLA Ops:
  0.0 2.0 %shard_map.47 = (f32[108,512]{1,0:T(8,128)}, f32[104,512]{1,0:T(8,128)}) custom-call(s32[4,8,512]{2,1,0:T(8,128)} %density.3, s32[4,8,512]{2,1,0:T(8,128)} %fixed.3, s32[4,8,512]{2,1,0:T(8,128)} %loaded.3, f32[3,4,8,512]{3,2,1,0:T(8,128)} %load.3), custom_call_target="tpu_custom_call" | custom-call | tf_op jit(solution)/shard_map/pallas_call | solution.py:420
  2.0 1.9 %collective-permute-start = (f32[108,512]{1,0:T(8,128)}, f32[108,512]{1,0:T(8,128)S(1)}, u32[]{:S(2)}, u32[]{:S(2)}) collective-permute-start(f32[108,512]{1,0:T(8,128)} %get-tuple-element.9), channel_id=1, source_target_pairs={{1,0},{2,1},{3,2},{4,3},{5,4},{6,5},{7,6},{8,7},{9,8},{10,9},{11,1... | collective-permute-start | bytes 663560 | tf_op jit(solution)/shard_map/ppermute | solution.py:491
  3.9 5.5 %collective-permute-start.1 = (f32[104,512]{1,0:T(8,128)}, f32[104,512]{1,0:T(8,128)S(1)}, u32[]{:S(2)}, u32[]{:S(2)}) collective-permute-start(f32[104,512]{1,0:T(8,128)} %get-tuple-element.10), channel_id=1, source_target_pairs={{0,1},{1,2},{2,3},{3,4},{4,5},{5,6},{6,7},{7,8},{8,9},{9,10},{10,1... | collective-permute-start | bytes 638984 | tf_op jit(solution)/shard_map/ppermute | solution.py:492
  9.5 0.6 shard_map.46.fine
  10.1 4.1 %collective-permute-done.1.high.row_before = f32[104,512]{1,0:T(8,128)S(1)} collective-permute-done((f32[104,512]{1,0:T(8,128)}, f32[104,512]{1,0:T(8,128)S(1)}, u32[]{:S(2)}, u32[]{:S(2)}) %collective-permute-start.1) | collective-permute-done | bytes 213024 | tf_op jit(solution)/shard_map/ppermute | solution.py:492
  14.2 0.1 shard_map.48
  14.3 3.1 %collective-permute-start.2 = (f32[104,512]{1,0:T(8,128)S(1)}, f32[104,512]{1,0:T(8,128)S(1)}, u32[]{:S(2)}, u32[]{:S(2)}) collective-permute-start(f32[104,512]{1,0:T(8,128)S(1)} %get-tuple-element.11), channel_id=1, source_target_pairs={{16,32},{32,16},{48,64},{64,48},{80,96},{96,80},{112,128},{128,112... | collective-permute-start | bytes 638984 | tf_op jit(solution)/shard_map/ppermute | solution.py:436
  17.4 2.3 %collective-permute-start.3 = (f32[96,512]{1,0:T(8,128)S(1)}, f32[96,512]{1,0:T(8,128)S(1)}, u32[]{:S(2)}, u32[]{:S(2)}) collective-permute-start(f32[96,512]{1,0:T(8,128)S(1)} %get-tuple-element.12), channel_id=1, source_target_pairs={{0,16},{16,0},{32,48},{48,32},{64,80},{80,64},{96,112},{112,96},{1... | collective-permute-start | bytes 589832 | tf_op jit(solution)/shard_map/ppermute | solution.py:431
  19.7 1.0 %collective-permute-done.3 = f32[96,512]{1,0:T(8,128)S(1)} collective-permute-done((f32[96,512]{1,0:T(8,128)S(1)}, f32[96,512]{1,0:T(8,128)S(1)}, u32[]{:S(2)}, u32[]{:S(2)}) %collective-permute-start.3) | collective-permute-done | bytes 196640 | tf_op jit(solution)/shard_map/ppermute | solution.py:431
  20.8 4.0 %collective-permute-done.2 = f32[104,512]{1,0:T(8,128)S(1)} collective-permute-done((f32[104,512]{1,0:T(8,128)S(1)}, f32[104,512]{1,0:T(8,128)S(1)}, u32[]{:S(2)}, u32[]{:S(2)}) %collective-permute-start.2) | collective-permute-done | bytes 213024 | tf_op jit(solution)/shard_map/ppermute | solution.py:436
  24.8 2.2 %shard_map.49 = f32[80,256]{1,0:T(8,128)S(1)} custom-call(f32[5,4,8,512]{3,2,1,0:T(8,128)S(1)} %shard_map.46.fine, f32[108,512]{1,0:T(8,128)S(1)} %collective-permute-done.low.row_after, f32[104,512]{1,0:T(8,128)S(1)} %collective-permute-done.1.high.row_before, f32[96,512]{1,0:T(8,128)S(1)} %get-tuple-element.14.before, f32[96,512]{1,0:T(8,128)S(1)} %get-tuple-element.13.after), custom_call_target="tpu_custom_call" | custom-call | tf_op jit(solution)/shard_map/pallas_call | solution.py:420
  27.0 3.1 %collective-permute-start.4 = (f32[88,256]{1,0:T(8,128)S(1)}, f32[88,256]{1,0:T(8,128)S(1)}, u32[]{:S(2)}, u32[]{:S(2)}) collective-permute-start(f32[88,256]{1,0:T(8,128)S(1)} %pad_maximum_fusion), channel_id=1, source_target_pairs={{16,32},{32,16},{48,64},{64,48},{80,96},{96,80},{112,128},{128,112... | collective-permute-start | bytes 270344 | tf_op jit(solution)/shard_map/ppermute | solution.py:436
  30.1 1.9 %collective-permute-start.5 = (f32[80,256]{1,0:T(8,128)S(1)}, f32[80,256]{1,0:T(8,128)S(1)}, u32[]{:S(2)}, u32[]{:S(2)}) collective-permute-start(f32[80,256]{1,0:T(8,128)S(1)} %shard_map.49), channel_id=1, source_target_pairs={{0,16},{16,0},{32,48},{48,32},{64,80},{80,64},{96,112},{112,96},{1... | collective-permute-start | bytes 245768 | tf_op jit(solution)/shard_map/ppermute | solution.py:431
  32.1 1.2 %collective-permute-done.5 = f32[80,256]{1,0:T(8,128)S(1)} collective-permute-done((f32[80,256]{1,0:T(8,128)S(1)}, f32[80,256]{1,0:T(8,128)S(1)}, u32[]{:S(2)}, u32[]{:S(2)}) %collective-permute-start.5) | collective-permute-done | bytes 81952 | tf_op jit(solution)/shard_map/ppermute | solution.py:431
  33.3 2.9 %collective-permute-done.4 = f32[88,256]{1,0:T(8,128)S(1)} collective-permute-done((f32[88,256]{1,0:T(8,128)S(1)}, f32[88,256]{1,0:T(8,128)S(1)}, u32[]{:S(2)}, u32[]{:S(2)}) %collective-permute-start.4) | collective-permute-done | bytes 90144 | tf_op jit(solution)/shard_map/ppermute | solution.py:436
  36.2 1.1 %shard_map.50 = f32[16,10,128]{2,1,0:T(8,128)} custom-call(f32[5,2,8,256]{3,2,1,0:T(8,128)S(1)} %bitcast.10, f32[5,2,8,256]{3,2,1,0:T(8,128)S(1)} %bitcast.6, f32[5,2,8,256]{3,2,1,0:T(8,128)S(1)} %bitcast.8), custom_call_target="tpu_custom_call" | custom-call | tf_op jit(solution)/shard_map/pallas_call | solution.py:420
  37.3 3.4 %all-to-all-start = ((f32[16,10,128]{2,1,0:T(8,128)}), f32[16,10,128]{2,1,0:T(8,128)S(1)}, u32[]{:S(2)}, u32[]{:S(2)}) async-start(f32[16,10,128]{2,1,0:T(8,128)} %shard_map.50), calls=%async_computation | async-start | bytes 262144 | tf_op jit(solution)/shard_map/all_to_all | solution.py:456
  40.7 5.4 %all-to-all-done = f32[16,10,128]{2,1,0:T(8,128)S(1)} async-done(((f32[16,10,128]{2,1,0:T(8,128)}), f32[16,10,128]{2,1,0:T(8,128)S(1)}, u32[]{:S(2)}, u32[]{:S(2)}) %all-to-all-start) | async-done | bytes 81952 | tf_op jit(solution)/shard_map/all_to_all | solution.py:456
  46.1 1.9 %collective-permute-start.6 = (f32[80,128]{1,0:T(8,128)S(1)}, f32[80,128]{1,0:T(8,128)S(1)}, u32[]{:S(2)}, u32[]{:S(2)}) collective-permute-start(f32[80,128]{1,0:T(8,128)S(1)} %reshape.40), channel_id=1, source_target_pairs={{0,128},{16,144},{32,160},{48,176},{128,256},{144,272},{160,288},{... | collective-permute-start | bytes 122888 | tf_op jit(solution)/shard_map/ppermute | solution.py:462
  48.1 5.1 %collective-permute-done.6 = f32[80,128]{1,0:T(8,128)S(1)} collective-permute-done((f32[80,128]{1,0:T(8,128)S(1)}, f32[80,128]{1,0:T(8,128)S(1)}, u32[]{:S(2)}, u32[]{:S(2)}) %collective-permute-start.6) | collective-permute-done | bytes 40992 | tf_op jit(solution)/shard_map/ppermute | solution.py:462
  53.3 6.7 %collective-permute-start.7 = (f32[180,128]{1,0:T(8,128)S(1)}, f32[180,128]{1,0:T(8,128)S(1)}, u32[]{:S(2)}, u32[]{:S(2)}) collective-permute-start(f32[180,128]{1,0:T(8,128)S(1)} %reshape.42), channel_id=1, source_target_pairs={{1,2},{2,1},{3,4},{4,3},{5,6},{6,5},{7,8},{8,7},{9,10},{10,9},{11,... | collective-permute-start | bytes 276488 | tf_op jit(solution)/shard_map/ppermute | solution.py:436
  60.1 6.4 %collective-permute-start.8 = (f32[90,128]{1,0:T(8,128)S(1)}, f32[90,128]{1,0:T(8,128)S(1)}, u32[]{:S(2)}, u32[]{:S(2)}) collective-permute-start(f32[90,128]{1,0:T(8,128)S(1)} %reshape.45), channel_id=1, source_target_pairs={{2,0},{1,3},{4,2},{3,5},{6,4},{5,7},{8,6},{7,9},{10,8},{9,11},{12,... | collective-permute-start | bytes 138248 | tf_op jit(solution)/shard_map/ppermute | solution.py:471
  66.5 1.7 %collective-permute-done.8 = f32[90,128]{1,0:T(8,128)S(1)} collective-permute-done((f32[90,128]{1,0:T(8,128)S(1)}, f32[90,128]{1,0:T(8,128)S(1)}, u32[]{:S(2)}, u32[]{:S(2)}) %collective-permute-start.8) | collective-permute-done | bytes 46112 | tf_op jit(solution)/shard_map/ppermute | solution.py:471
  68.3 2.8 %shard_map.51 = f32[3,4,8,512]{3,2,1,0:T(8,128)} custom-call(f32[9,5,10,128]{3,2,1,0:T(8,128)S(1)} %maximum_select_fusion.low, f32[5,2,8,256]{3,2,1,0:T(8,128)S(1)} %bitcast.11, f32[5,2,8,256]{3,2,1,0:T(8,128)S(1)} %bitcast.7, f32[5,2,8,256]{3,2,1,0:T(8,128)S(1)} %bitcast.9, f32[5,4,8,512]{3,2,1,0:T(8,128)S(1)} %shard_map.46.fine, ...), custom_call_target="tpu_custom_call" | custom-call | tf_op jit(solution)/shard_map/pallas_call | solution.py:420
  (24 shorter events, 0.2 us)
Async XLA Ops:
  0.0 9.4 %copy-start = (f32[3,4,8,512]{3,2,1,0:T(8,128)S(1)}, f32[3,4,8,512]{3,2,1,0:T(8,128)}, u32[]{:S(2)}) copy-start(f32[3,4,8,512]{3,2,1,0:T(8,128)} %load.3) | copy-start | bytes 589828
  0.0 9.4 %copy-start.1 = (s32[4,8,512]{2,1,0:T(8,128)S(1)}, s32[4,8,512]{2,1,0:T(8,128)}, u32[]{:S(2)}) copy-start(s32[4,8,512]{2,1,0:T(8,128)} %density.3) | copy-start | bytes 196612
  0.0 9.4 %copy-start.2 = (s32[4,8,512]{2,1,0:T(8,128)S(1)}, s32[4,8,512]{2,1,0:T(8,128)}, u32[]{:S(2)}) copy-start(s32[4,8,512]{2,1,0:T(8,128)} %fixed.3) | copy-start | bytes 196612
  0.0 9.4 %copy-start.3 = (s32[4,8,512]{2,1,0:T(8,128)S(1)}, s32[4,8,512]{2,1,0:T(8,128)}, u32[]{:S(2)}) copy-start(s32[4,8,512]{2,1,0:T(8,128)} %loaded.3) | copy-start | bytes 196612
  2.0 12.2 %collective-permute-start = (f32[108,512]{1,0:T(8,128)}, f32[108,512]{1,0:T(8,128)S(1)}, u32[]{:S(2)}, u32[]{:S(2)}) collective-permute-start(f32[108,512]{1,0:T(8,128)} %get-tuple-element.9), channel_id=1, source_target_pairs={{1,0},{2,1},{3,2},{4,3},{5,4},{6,5},{7,6},{8,7},{9,8},{10,9},{11,1... | collective-permute-start | bytes 663560 | tf_op jit(solution)/shard_map/ppermute | solution.py:491
  3.9 10.3 %collective-permute-start.1 = (f32[104,512]{1,0:T(8,128)}, f32[104,512]{1,0:T(8,128)S(1)}, u32[]{:S(2)}, u32[]{:S(2)}) collective-permute-start(f32[104,512]{1,0:T(8,128)} %get-tuple-element.10), channel_id=1, source_target_pairs={{0,1},{1,2},{2,3},{3,4},{4,5},{5,6},{6,7},{7,8},{8,9},{9,10},{10,1... | collective-permute-start | bytes 638984 | tf_op jit(solution)/shard_map/ppermute | solution.py:492
  14.3 10.5 %collective-permute-start.2 = (f32[104,512]{1,0:T(8,128)S(1)}, f32[104,512]{1,0:T(8,128)S(1)}, u32[]{:S(2)}, u32[]{:S(2)}) collective-permute-start(f32[104,512]{1,0:T(8,128)S(1)} %get-tuple-element.11), channel_id=1, source_target_pairs={{16,32},{32,16},{48,64},{64,48},{80,96},{96,80},{112,128},{128,112... | collective-permute-start | bytes 638984 | tf_op jit(solution)/shard_map/ppermute | solution.py:436
  17.4 3.4 %collective-permute-start.3 = (f32[96,512]{1,0:T(8,128)S(1)}, f32[96,512]{1,0:T(8,128)S(1)}, u32[]{:S(2)}, u32[]{:S(2)}) collective-permute-start(f32[96,512]{1,0:T(8,128)S(1)} %get-tuple-element.12), channel_id=1, source_target_pairs={{0,16},{16,0},{32,48},{48,32},{64,80},{80,64},{96,112},{112,96},{1... | collective-permute-start | bytes 589832 | tf_op jit(solution)/shard_map/ppermute | solution.py:431
  27.0 9.2 %collective-permute-start.4 = (f32[88,256]{1,0:T(8,128)S(1)}, f32[88,256]{1,0:T(8,128)S(1)}, u32[]{:S(2)}, u32[]{:S(2)}) collective-permute-start(f32[88,256]{1,0:T(8,128)S(1)} %pad_maximum_fusion), channel_id=1, source_target_pairs={{16,32},{32,16},{48,64},{64,48},{80,96},{96,80},{112,128},{128,112... | collective-permute-start | bytes 270344 | tf_op jit(solution)/shard_map/ppermute | solution.py:436
  30.1 3.2 %collective-permute-start.5 = (f32[80,256]{1,0:T(8,128)S(1)}, f32[80,256]{1,0:T(8,128)S(1)}, u32[]{:S(2)}, u32[]{:S(2)}) collective-permute-start(f32[80,256]{1,0:T(8,128)S(1)} %shard_map.49), channel_id=1, source_target_pairs={{0,16},{16,0},{32,48},{48,32},{64,80},{80,64},{96,112},{112,96},{1... | collective-permute-start | bytes 245768 | tf_op jit(solution)/shard_map/ppermute | solution.py:431
  37.3 8.8 %all-to-all-start = ((f32[16,10,128]{2,1,0:T(8,128)}), f32[16,10,128]{2,1,0:T(8,128)S(1)}, u32[]{:S(2)}, u32[]{:S(2)}) async-start(f32[16,10,128]{2,1,0:T(8,128)} %shard_map.50), calls=%async_computation | async-start | bytes 262144 | tf_op jit(solution)/shard_map/all_to_all | solution.py:456
  46.1 7.1 %collective-permute-start.6 = (f32[80,128]{1,0:T(8,128)S(1)}, f32[80,128]{1,0:T(8,128)S(1)}, u32[]{:S(2)}, u32[]{:S(2)}) collective-permute-start(f32[80,128]{1,0:T(8,128)S(1)} %reshape.40), channel_id=1, source_target_pairs={{0,128},{16,144},{32,160},{48,176},{128,256},{144,272},{160,288},{... | collective-permute-start | bytes 122888 | tf_op jit(solution)/shard_map/ppermute | solution.py:462
  53.3 14.9 %collective-permute-start.7 = (f32[180,128]{1,0:T(8,128)S(1)}, f32[180,128]{1,0:T(8,128)S(1)}, u32[]{:S(2)}, u32[]{:S(2)}) collective-permute-start(f32[180,128]{1,0:T(8,128)S(1)} %reshape.42), channel_id=1, source_target_pairs={{1,2},{2,1},{3,4},{4,3},{5,6},{6,5},{7,8},{8,7},{9,10},{10,9},{11,... | collective-permute-start | bytes 276488 | tf_op jit(solution)/shard_map/ppermute | solution.py:436
  60.1 8.1 %collective-permute-start.8 = (f32[90,128]{1,0:T(8,128)S(1)}, f32[90,128]{1,0:T(8,128)S(1)}, u32[]{:S(2)}, u32[]{:S(2)}) collective-permute-start(f32[90,128]{1,0:T(8,128)S(1)} %reshape.45), channel_id=1, source_target_pairs={{2,0},{1,3},{4,2},{3,5},{6,4},{5,7},{8,6},{7,9},{10,8},{9,11},{12,... | collective-permute-start | bytes 138248 | tf_op jit(solution)/shard_map/ppermute | solution.py:471

commit v8 on v7

--- a/solution.py
+++ b/solution.py
@@ -67,11 +67,15 @@
     n = a.shape[0]
     if len(tiles) == 1:
         return pltpu.roll(a, n - 1, 0), pltpu.roll(a, 1, 0)
-    row = iota(a.shape, 0)
-    rim = tiles[1] if n == 8 else jnp.concatenate([tiles[1]] * 2, axis=0)
-    after = pltpu.roll(jnp.where(row == 0, rim, a), n - 1, 0)
-    before = pltpu.roll(jnp.where(row == n - 1, rim, a), 1, 0)
-    return after, before
+    row = iota((8, a.shape[1]), 0)
+    tiles = [tiles[1]] + [a[k : k + 8] for k in range(0, n, 8)] + [tiles[1]]
+    after, before = [], []
+    for k in range(1, len(tiles) - 1):
+        after.append(pltpu.roll(jnp.where(row == 0, tiles[k + 1], tiles[k]), 7, 0))
+        before.append(pltpu.roll(jnp.where(row == 7, tiles[k - 1], tiles[k]), 1, 0))
+    if n == 8:
+        return after[0], before[0]
+    return jnp.concatenate(after, axis=0), jnp.concatenate(before, axis=0)
 
 
 def y_t(tiles):
@@ -122,18 +126,18 @@
     result = {}
     for p in range(planes[0] - 1, planes[-1] + 2):
         for store, field in ((own, v[p]), (scaled, [times(c, s[p]) for c in v[p]])):
-            even, odd = plane_terms(field)
-            store[p] = (
-                [2.0 * e for e in even],
-                [e + o for e, o in zip(even, odd)],
-                [e - o for e, o in zip(even, odd)],
-            )
+            store[p] = plane_terms(field)
         q = p - 1
         if q in planes:
             here = []
             for c in range(3):
-                plain = own[q][0][c] + (own[q + 1][1][c] + own[q - 1][2][c])
-                heavy = scaled[q][0][c] + (scaled[q + 1][1][c] + scaled[q - 1][2][c])
+                sums_x = []
+                for store in (own, scaled):
+                    (e0, o0), (e1, _), (e2, o2) = [
+                        (store[x][0][c], store[x][1][c]) for x in (q - 1, q, q + 1)
+                    ]
+                    sums_x.append((e2 + e0) + 2.0 * e1 + (o2 - o0))
+                plain, heavy = sums_x
                 u, k = v[q][c][0], s[q][0]
                 here.append(8.1 * (k * u) + 0.125 * (u * sums[q] - (k * plain + heavy)))
             result[q] = here
@@ -203,28 +207,30 @@
 
 
 def side_rows(side, k):
-    at = 80 + 2 * k
+    at = 72 + 2 * k
     rim = rim_tile(side[at + 1 : at + 2], side[at : at + 1])
     return side[16 * k : 16 * k + 16], rim
 
 
 def sides_kernel(even, fine, low, high, outer, inner):
     is_even = even[0] == 1
+
+    def put(at, rows, first, last):
+        outer[at : at + rows] = jnp.where(is_even, first, last)
+        inner[at : at + rows] = jnp.where(is_even, last, first)
+
+    for k in range(4):
+        put(16 * k, 16, *[own_rows(fine, low, high, k, p)[0] for p in (0, 3)])
+    put(64, 8, fine[4, 0], fine[4, 3])
     for k in range(5):
-        first, last = [own_rows(fine, low, high, k, p)[0] for p in (0, 3)]
-        outer[16 * k : 16 * k + 16] = jnp.where(is_even, first, last)
-        inner[16 * k : 16 * k + 16] = jnp.where(is_even, last, first)
         ends = []
         for p in (0, 3):
             at = 5 * (4 * k + p)
-            ends.append((high[at : at + 1], low[at + 12 : at + 13]))
+            below, above = (at, at + 12) if k < 4 else (at + 4, at + 8)
+            ends.append((high[below : below + 1], low[above : above + 1]))
         for j in range(2):
-            first, last = ends[0][j], ends[1][j]
-            at = 80 + 2 * k + j
-            outer[at : at + 1] = jnp.where(is_even, first, last)
-            inner[at : at + 1] = jnp.where(is_even, last, first)
-    outer[90:104] = jnp.zeros((14, low.shape[1]), F32)
-    inner[90:96] = jnp.zeros((6, low.shape[1]), F32)
+            put(72 + 2 * k + j, 1, ends[0][j], ends[1][j])
+    outer[82:88] = jnp.zeros((6, low.shape[1]), F32)
 
 
 def fine_tiles(fine, low, high, before, after):
@@ -233,9 +239,12 @@
         here = []
         for k in range(5):
             if p in (0, 5):
-                side, at = before if p == 0 else after, 16 * k
-                main = side[at + 4 : at + 12]
-                rim = rim_tile(side[at + 12 : at + 13], side[at + 3 : at + 4])
+                side = before if p == 0 else after
+                at, below, above = (16 * k + 4, 16 * k + 3, 16 * k + 12)
+                if k == 4:
+                    at, below, above = 64, 80, 81
+                main = side[at : at + 8]
+                rim = rim_tile(side[above : above + 1], side[below : below + 1])
             else:
                 at = 5 * (4 * k + p - 1)
                 main = fine[k, p - 1]
@@ -250,7 +259,7 @@
     for p in range(6):
         if p in (0, 5):
             side = before if p == 0 else after
-            tiles.append([side_rows(side, k) for k in range(5)])
+            tiles.append([side_rows(side, k) for k in range(4)])
         else:
             tiles.append([own_rows(fine, low, high, k, p - 1) for k in range(5)])
     v = [t[:3] for t in tiles]
@@ -495,14 +504,14 @@
     even = lax.axis_index("gx") % 2 == 0
     outer, inner = call(
         sides_kernel,
-        [(104, nz), (96, nz)],
+        [(88, nz), (82, nz)],
         even.astype(jnp.int32).reshape(1),
         fine,
         row_after,
         row_before,
         ins=[SMEM] + [VMEM] * 3,
     )
-    outer, inner = outer_swap(outer, "gx")[:96], inner_swap(inner, "gx")
+    outer, inner = outer_swap(outer, "gx")[:82], inner_swap(inner, "gx")
     before, after = jnp.where(even, outer, inner), jnp.where(even, inner, outer)
     fine_args = (fine, row_after, row_before, before, after)
     mid = call(fine_residual_kernel, [(80, nz // 2)], *fine_args)

time: 71.5 us -> 71.1 us (level)
  no operation moved by 1% of the time
where the time goes in v8:
time: 71.1 us; the launch traced here: 70.7 us
  starting transfers between devices  36.3 us (51%)
  waiting for transfers between devices  25.2 us (35%)
  Pallas kernels  8.64 us (12%)
    ppermute x3, starting transfers between devices, outer_swap(): lax.ppermute(value, axis, [(i, (i + 1 ^ 1) - 1) for i in range(1, n - 1)])  13 us
    pallas_call x6, Pallas kernels, call(): pl.pallas_call(kernel, out_shape=results if len(results) > 1 else results...  8.64 us
    ppermute x3, waiting for transfers between devices, outer_swap(): lax.ppermute(value, axis, [(i, (i + 1 ^ 1) - 1) for i in range(1, n - 1)])  6.54 us
    ppermute x1, starting transfers between devices, gather_low(): beyond = lax.ppermute(own, 'gy', moves).reshape(9, 1, 10, nz)  6.39 us
    ppermute x1, starting transfers between devices, per_device(): lax.ppermute(high_rows, 'gy', [(i, i + 1) for i in range(n - 1)])  5.49 us
    all_to_all x1, waiting for transfers between devices, gather_low(): row = lax.all_to_all(low, ('gx', 'gy'), 0, 0, axis_index_groups=groups)  5.37 us
    ppermute x1, waiting for transfers between devices, gather_low(): other = lax.ppermute(half, 'gx', moves).reshape(8, 10, nz)  5.14 us
    ppermute x2, starting transfers between devices, inner_swap(): lax.ppermute(value, axis, [(i, i ^ 1) for i in range(lax.axis_size(axis))])  4.22 us
  transfers between devices with their start and end apart: 10, of which 8 were waited for; matrix products, arithmetic and copies ran while one was open for 0% of the time, Pallas kernels for 1%

profile of v8, /device:TPU:224, one launch (start us, length us, event | category | flops | bytes accessed | tf_op | source)
XLA Modules:
  0.0 70.7 jit_solution(11444618274462014592)
XLA Ops:
  0.0 2.0 %shard_map.47 = (f32[108,512]{1,0:T(8,128)}, f32[104,512]{1,0:T(8,128)}) custom-call(s32[4,8,512]{2,1,0:T(8,128)} %density.3, s32[4,8,512]{2,1,0:T(8,128)} %fixed.3, s32[4,8,512]{2,1,0:T(8,128)} %loaded.3, f32[3,4,8,512]{3,2,1,0:T(8,128)} %load.3), custom_call_target="tpu_custom_call" | custom-call | tf_op jit(solution)/shard_map/pallas_call | solution.py:429
  2.0 1.9 %collective-permute-start = (f32[108,512]{1,0:T(8,128)}, f32[108,512]{1,0:T(8,128)S(1)}, u32[]{:S(2)}, u32[]{:S(2)}) collective-permute-start(f32[108,512]{1,0:T(8,128)} %get-tuple-element.9), channel_id=1, source_target_pairs={{1,0},{2,1},{3,2},{4,3},{5,4},{6,5},{7,6},{8,7},{9,8},{10,9},{11,1... | collective-permute-start | bytes 663560 | tf_op jit(solution)/shard_map/ppermute | solution.py:500
  3.9 5.5 %collective-permute-start.1 = (f32[104,512]{1,0:T(8,128)}, f32[104,512]{1,0:T(8,128)S(1)}, u32[]{:S(2)}, u32[]{:S(2)}) collective-permute-start(f32[104,512]{1,0:T(8,128)} %get-tuple-element.10), channel_id=1, source_target_pairs={{0,1},{1,2},{2,3},{3,4},{4,5},{5,6},{6,7},{7,8},{8,9},{9,10},{10,1... | collective-permute-start | bytes 638984 | tf_op jit(solution)/shard_map/ppermute | solution.py:501
  9.5 0.6 shard_map.46.fine
  10.1 4.1 %collective-permute-done.1.high.row_before = f32[104,512]{1,0:T(8,128)S(1)} collective-permute-done((f32[104,512]{1,0:T(8,128)}, f32[104,512]{1,0:T(8,128)S(1)}, u32[]{:S(2)}, u32[]{:S(2)}) %collective-permute-start.1) | collective-permute-done | bytes 213024 | tf_op jit(solution)/shard_map/ppermute | solution.py:501
  14.3 3.1 %collective-permute-start.2 = (f32[88,512]{1,0:T(8,128)S(1)}, f32[88,512]{1,0:T(8,128)S(1)}, u32[]{:S(2)}, u32[]{:S(2)}) collective-permute-start(f32[88,512]{1,0:T(8,128)S(1)} %get-tuple-element.11), channel_id=1, source_target_pairs={{16,32},{32,16},{48,64},{64,48},{80,96},{96,80},{112,128},{128,112... | collective-permute-start | bytes 540680 | tf_op jit(solution)/shard_map/ppermute | solution.py:445
  17.4 2.3 %collective-permute-start.3 = (f32[82,512]{1,0:T(8,128)S(1)}, f32[82,512]{1,0:T(8,128)S(1)}, u32[]{:S(2)}, u32[]{:S(2)}) collective-permute-start(f32[82,512]{1,0:T(8,128)S(1)} %get-tuple-element.12), channel_id=1, source_target_pairs={{0,16},{16,0},{32,48},{48,32},{64,80},{80,64},{96,112},{112,96},{1... | collective-permute-start | bytes 503816 | tf_op jit(solution)/shard_map/ppermute | solution.py:440
  19.7 1.0 %collective-permute-done.3 = f32[82,512]{1,0:T(8,128)S(1)} collective-permute-done((f32[82,512]{1,0:T(8,128)S(1)}, f32[82,512]{1,0:T(8,128)S(1)}, u32[]{:S(2)}, u32[]{:S(2)}) %collective-permute-start.3) | collective-permute-done | bytes 167968 | tf_op jit(solution)/shard_map/ppermute | solution.py:440
  20.7 3.7 %collective-permute-done.2 = f32[88,512]{1,0:T(8,128)S(1)} collective-permute-done((f32[88,512]{1,0:T(8,128)S(1)}, f32[88,512]{1,0:T(8,128)S(1)}, u32[]{:S(2)}, u32[]{:S(2)}) %collective-permute-start.2) | collective-permute-done | bytes 180256 | tf_op jit(solution)/shard_map/ppermute | solution.py:445
  24.4 2.1 %shard_map.49 = f32[80,256]{1,0:T(8,128)S(1)} custom-call(f32[5,4,8,512]{3,2,1,0:T(8,128)S(1)} %shard_map.46.fine, f32[108,512]{1,0:T(8,128)S(1)} %collective-permute-done.low.row_after, f32[104,512]{1,0:T(8,128)S(1)} %collective-permute-done.1.high.row_before, f32[82,512]{1,0:T(8,128)S(1)} %get-tuple-element.14.before, f32[82,512]{1,0:T(8,128)S(1)} %get-tuple-element.13.after), custom_call_target="tpu_custom_call" | custom-call | tf_op jit(solution)/shard_map/pallas_call | solution.py:429
  26.6 3.1 %collective-permute-start.4 = (f32[88,256]{1,0:T(8,128)S(1)}, f32[88,256]{1,0:T(8,128)S(1)}, u32[]{:S(2)}, u32[]{:S(2)}) collective-permute-start(f32[88,256]{1,0:T(8,128)S(1)} %pad_maximum_fusion), channel_id=1, source_target_pairs={{16,32},{32,16},{48,64},{64,48},{80,96},{96,80},{112,128},{128,112... | collective-permute-start | bytes 270344 | tf_op jit(solution)/shard_map/ppermute | solution.py:445
  29.7 1.9 %collective-permute-start.5 = (f32[80,256]{1,0:T(8,128)S(1)}, f32[80,256]{1,0:T(8,128)S(1)}, u32[]{:S(2)}, u32[]{:S(2)}) collective-permute-start(f32[80,256]{1,0:T(8,128)S(1)} %shard_map.49), channel_id=1, source_target_pairs={{0,16},{16,0},{32,48},{48,32},{64,80},{80,64},{96,112},{112,96},{1... | collective-permute-start | bytes 245768 | tf_op jit(solution)/shard_map/ppermute | solution.py:440
  31.6 1.2 %collective-permute-done.5 = f32[80,256]{1,0:T(8,128)S(1)} collective-permute-done((f32[80,256]{1,0:T(8,128)S(1)}, f32[80,256]{1,0:T(8,128)S(1)}, u32[]{:S(2)}, u32[]{:S(2)}) %collective-permute-start.5) | collective-permute-done | bytes 81952 | tf_op jit(solution)/shard_map/ppermute | solution.py:440
  32.9 2.9 %collective-permute-done.4 = f32[88,256]{1,0:T(8,128)S(1)} collective-permute-done((f32[88,256]{1,0:T(8,128)S(1)}, f32[88,256]{1,0:T(8,128)S(1)}, u32[]{:S(2)}, u32[]{:S(2)}) %collective-permute-start.4) | collective-permute-done | bytes 90144 | tf_op jit(solution)/shard_map/ppermute | solution.py:445
  35.8 1.1 %shard_map.50 = f32[16,10,128]{2,1,0:T(8,128)} custom-call(f32[5,2,8,256]{3,2,1,0:T(8,128)S(1)} %bitcast.10, f32[5,2,8,256]{3,2,1,0:T(8,128)S(1)} %bitcast.6, f32[5,2,8,256]{3,2,1,0:T(8,128)S(1)} %bitcast.8), custom_call_target="tpu_custom_call" | custom-call | tf_op jit(solution)/shard_map/pallas_call | solution.py:429
  36.8 3.4 %all-to-all-start = ((f32[16,10,128]{2,1,0:T(8,128)}), f32[16,10,128]{2,1,0:T(8,128)S(1)}, u32[]{:S(2)}, u32[]{:S(2)}) async-start(f32[16,10,128]{2,1,0:T(8,128)} %shard_map.50), calls=%async_computation | async-start | bytes 262144 | tf_op jit(solution)/shard_map/all_to_all | solution.py:465
  40.3 5.4 %all-to-all-done = f32[16,10,128]{2,1,0:T(8,128)S(1)} async-done(((f32[16,10,128]{2,1,0:T(8,128)}), f32[16,10,128]{2,1,0:T(8,128)S(1)}, u32[]{:S(2)}, u32[]{:S(2)}) %all-to-all-start) | async-done | bytes 81952 | tf_op jit(solution)/shard_map/all_to_all | solution.py:465
  45.7 1.9 %collective-permute-start.6 = (f32[80,128]{1,0:T(8,128)S(1)}, f32[80,128]{1,0:T(8,128)S(1)}, u32[]{:S(2)}, u32[]{:S(2)}) collective-permute-start(f32[80,128]{1,0:T(8,128)S(1)} %reshape.40), channel_id=1, source_target_pairs={{0,128},{16,144},{32,160},{48,176},{128,256},{144,272},{160,288},{... | collective-permute-start | bytes 122888 | tf_op jit(solution)/shard_map/ppermute | solution.py:471
  47.6 5.1 %collective-permute-done.6 = f32[80,128]{1,0:T(8,128)S(1)} collective-permute-done((f32[80,128]{1,0:T(8,128)S(1)}, f32[80,128]{1,0:T(8,128)S(1)}, u32[]{:S(2)}, u32[]{:S(2)}) %collective-permute-start.6) | collective-permute-done | bytes 40992 | tf_op jit(solution)/shard_map/ppermute | solution.py:471
  52.8 0.1 fusion.1
  52.9 6.7 %collective-permute-start.7 = (f32[180,128]{1,0:T(8,128)S(1)}, f32[180,128]{1,0:T(8,128)S(1)}, u32[]{:S(2)}, u32[]{:S(2)}) collective-permute-start(f32[180,128]{1,0:T(8,128)S(1)} %reshape.42), channel_id=1, source_target_pairs={{1,2},{2,1},{3,4},{4,3},{5,6},{6,5},{7,8},{8,7},{9,10},{10,9},{11,... | collective-permute-start | bytes 276488 | tf_op jit(solution)/shard_map/ppermute | solution.py:445
  59.6 6.4 %collective-permute-start.8 = (f32[90,128]{1,0:T(8,128)S(1)}, f32[90,128]{1,0:T(8,128)S(1)}, u32[]{:S(2)}, u32[]{:S(2)}) collective-permute-start(f32[90,128]{1,0:T(8,128)S(1)} %reshape.45), channel_id=1, source_target_pairs={{2,0},{1,3},{4,2},{3,5},{6,4},{5,7},{8,6},{7,9},{10,8},{9,11},{12,... | collective-permute-start | bytes 138248 | tf_op jit(solution)/shard_map/ppermute | solution.py:480
  66.0 1.7 %collective-permute-done.8 = f32[90,128]{1,0:T(8,128)S(1)} collective-permute-done((f32[90,128]{1,0:T(8,128)S(1)}, f32[90,128]{1,0:T(8,128)S(1)}, u32[]{:S(2)}, u32[]{:S(2)}) %collective-permute-start.8) | collective-permute-done | bytes 46112 | tf_op jit(solution)/shard_map/ppermute | solution.py:480
  67.8 2.9 %shard_map.51 = f32[3,4,8,512]{3,2,1,0:T(8,128)} custom-call(f32[9,5,10,128]{3,2,1,0:T(8,128)S(1)} %maximum_select_fusion.low, f32[5,2,8,256]{3,2,1,0:T(8,128)S(1)} %bitcast.11, f32[5,2,8,256]{3,2,1,0:T(8,128)S(1)} %bitcast.7, f32[5,2,8,256]{3,2,1,0:T(8,128)S(1)} %bitcast.9, f32[5,4,8,512]{3,2,1,0:T(8,128)S(1)} %shard_map.46.fine, ...), custom_call_target="tpu_custom_call" | custom-call | tf_op jit(solution)/shard_map/pallas_call | solution.py:429
  (24 shorter events, 0.2 us)
Async XLA Ops:
  0.0 9.4 %copy-start = (f32[3,4,8,512]{3,2,1,0:T(8,128)S(1)}, f32[3,4,8,512]{3,2,1,0:T(8,128)}, u32[]{:S(2)}) copy-start(f32[3,4,8,512]{3,2,1,0:T(8,128)} %load.3) | copy-start | bytes 589828
  0.0 9.4 %copy-start.1 = (s32[4,8,512]{2,1,0:T(8,128)S(1)}, s32[4,8,512]{2,1,0:T(8,128)}, u32[]{:S(2)}) copy-start(s32[4,8,512]{2,1,0:T(8,128)} %density.3) | copy-start | bytes 196612
  0.0 9.4 %copy-start.2 = (s32[4,8,512]{2,1,0:T(8,128)S(1)}, s32[4,8,512]{2,1,0:T(8,128)}, u32[]{:S(2)}) copy-start(s32[4,8,512]{2,1,0:T(8,128)} %fixed.3) | copy-start | bytes 196612
  0.0 9.4 %copy-start.3 = (s32[4,8,512]{2,1,0:T(8,128)S(1)}, s32[4,8,512]{2,1,0:T(8,128)}, u32[]{:S(2)}) copy-start(s32[4,8,512]{2,1,0:T(8,128)} %loaded.3) | copy-start | bytes 196612
  2.0 12.2 %collective-permute-start = (f32[108,512]{1,0:T(8,128)}, f32[108,512]{1,0:T(8,128)S(1)}, u32[]{:S(2)}, u32[]{:S(2)}) collective-permute-start(f32[108,512]{1,0:T(8,128)} %get-tuple-element.9), channel_id=1, source_target_pairs={{1,0},{2,1},{3,2},{4,3},{5,4},{6,5},{7,6},{8,7},{9,8},{10,9},{11,1... | collective-permute-start | bytes 663560 | tf_op jit(solution)/shard_map/ppermute | solution.py:500
  3.9 10.3 %collective-permute-start.1 = (f32[104,512]{1,0:T(8,128)}, f32[104,512]{1,0:T(8,128)S(1)}, u32[]{:S(2)}, u32[]{:S(2)}) collective-permute-start(f32[104,512]{1,0:T(8,128)} %get-tuple-element.10), channel_id=1, source_target_pairs={{0,1},{1,2},{2,3},{3,4},{4,5},{5,6},{6,7},{7,8},{8,9},{9,10},{10,1... | collective-permute-start | bytes 638984 | tf_op jit(solution)/shard_map/ppermute | solution.py:501
  14.3 10.1 %collective-permute-start.2 = (f32[88,512]{1,0:T(8,128)S(1)}, f32[88,512]{1,0:T(8,128)S(1)}, u32[]{:S(2)}, u32[]{:S(2)}) collective-permute-start(f32[88,512]{1,0:T(8,128)S(1)} %get-tuple-element.11), channel_id=1, source_target_pairs={{16,32},{32,16},{48,64},{64,48},{80,96},{96,80},{112,128},{128,112... | collective-permute-start | bytes 540680 | tf_op jit(solution)/shard_map/ppermute | solution.py:445
  17.4 3.3 %collective-permute-start.3 = (f32[82,512]{1,0:T(8,128)S(1)}, f32[82,512]{1,0:T(8,128)S(1)}, u32[]{:S(2)}, u32[]{:S(2)}) collective-permute-start(f32[82,512]{1,0:T(8,128)S(1)} %get-tuple-element.12), channel_id=1, source_target_pairs={{0,16},{16,0},{32,48},{48,32},{64,80},{80,64},{96,112},{112,96},{1... | collective-permute-start | bytes 503816 | tf_op jit(solution)/shard_map/ppermute | solution.py:440
  26.6 9.2 %collective-permute-start.4 = (f32[88,256]{1,0:T(8,128)S(1)}, f32[88,256]{1,0:T(8,128)S(1)}, u32[]{:S(2)}, u32[]{:S(2)}) collective-permute-start(f32[88,256]{1,0:T(8,128)S(1)} %pad_maximum_fusion), channel_id=1, source_target_pairs={{16,32},{32,16},{48,64},{64,48},{80,96},{96,80},{112,128},{128,112... | collective-permute-start | bytes 270344 | tf_op jit(solution)/shard_map/ppermute | solution.py:445
  29.7 3.2 %collective-permute-start.5 = (f32[80,256]{1,0:T(8,128)S(1)}, f32[80,256]{1,0:T(8,128)S(1)}, u32[]{:S(2)}, u32[]{:S(2)}) collective-permute-start(f32[80,256]{1,0:T(8,128)S(1)} %shard_map.49), channel_id=1, source_target_pairs={{0,16},{16,0},{32,48},{48,32},{64,80},{80,64},{96,112},{112,96},{1... | collective-permute-start | bytes 245768 | tf_op jit(solution)/shard_map/ppermute | solution.py:440
  36.8 8.8 %all-to-all-start = ((f32[16,10,128]{2,1,0:T(8,128)}), f32[16,10,128]{2,1,0:T(8,128)S(1)}, u32[]{:S(2)}, u32[]{:S(2)}) async-start(f32[16,10,128]{2,1,0:T(8,128)} %shard_map.50), calls=%async_computation | async-start | bytes 262144 | tf_op jit(solution)/shard_map/all_to_all | solution.py:465
  45.7 7.1 %collective-permute-start.6 = (f32[80,128]{1,0:T(8,128)S(1)}, f32[80,128]{1,0:T(8,128)S(1)}, u32[]{:S(2)}, u32[]{:S(2)}) collective-permute-start(f32[80,128]{1,0:T(8,128)S(1)} %reshape.40), channel_id=1, source_target_pairs={{0,128},{16,144},{32,160},{48,176},{128,256},{144,272},{160,288},{... | collective-permute-start | bytes 122888 | tf_op jit(solution)/shard_map/ppermute | solution.py:471
  52.9 14.9 %collective-permute-start.7 = (f32[180,128]{1,0:T(8,128)S(1)}, f32[180,128]{1,0:T(8,128)S(1)}, u32[]{:S(2)}, u32[]{:S(2)}) collective-permute-start(f32[180,128]{1,0:T(8,128)S(1)} %reshape.42), channel_id=1, source_target_pairs={{1,2},{2,1},{3,4},{4,3},{5,6},{6,5},{7,8},{8,7},{9,10},{10,9},{11,... | collective-permute-start | bytes 276488 | tf_op jit(solution)/shard_map/ppermute | solution.py:445
  59.6 8.1 %collective-permute-start.8 = (f32[90,128]{1,0:T(8,128)S(1)}, f32[90,128]{1,0:T(8,128)S(1)}, u32[]{:S(2)}, u32[]{:S(2)}) collective-permute-start(f32[90,128]{1,0:T(8,128)S(1)} %reshape.45), channel_id=1, source_target_pairs={{2,0},{1,3},{4,2},{3,5},{6,4},{5,7},{8,6},{7,9},{10,8},{9,11},{12,... | collective-permute-start | bytes 138248 | tf_op jit(solution)/shard_map/ppermute | solution.py:480

commit v9 on v8

--- a/solution.py
+++ b/solution.py
@@ -150,17 +150,6 @@
     return free * 0.8 / (7.1 * stiff + 7.5)
 
 
-def run_copies(pairs, sems):
-    copies = [
-        pltpu.make_async_copy(source, target, sems.at[k])
-        for k, (source, target) in enumerate(pairs)
-    ]
-    for copy in copies:
-        copy.start()
-    for copy in copies:
-        copy.wait()
-
-
 def start_values(density, fixed, loaded, load):
     level = (density.astype(F32) + 1.0) * (1.0 / 256.0)
     stiff = 0.05 + level * level * level
@@ -169,9 +158,12 @@
     return [factor * c for c in load] + [stiff, free]
 
 
-def rows_kernel(density, fixed, loaded, load, low, high, *scratch):
-    run_copies(zip((density, fixed, loaded, load), scratch[:4]), scratch[4])
-    d, x, m, f = scratch[:4]
+def gate_kernel(density, fixed, loaded, load, out):
+    out[0] = 1
+
+
+def rows_kernel(gate, density, fixed, loaded, load, low, high):
+    d, x, m, f = density, fixed, loaded, load
     low[0:8] = jnp.zeros((8, low.shape[1]), F32)
     high[96:104] = jnp.zeros((8, low.shape[1]), F32)
     for p in range(4):
@@ -182,9 +174,7 @@
             high[at : at + 5] = values[k][3:8]
 
 
-def fine_kernel(density, fixed, loaded, load, fine, *scratch):
-    run_copies(zip((density, fixed, loaded, load), scratch[:4]), scratch[4])
-    d, x, m, f = scratch[:4]
+def fine_kernel(d, x, m, f, fine):
     for p in range(4):
         values = start_values(d[p], x[p], m[p], [f[c, p] for c in range(3)])
         for k in range(5):
@@ -490,16 +480,20 @@
     nz = density.shape[2]
     args = (density, fixed, loaded, load)
     sems = pltpu.SemaphoreType.DMA((4,))
-    inputs = dict(
-        ins=[HBM] * 4, scratch=[pltpu.VMEM(a.shape, a.dtype) for a in args] + [sems]
-    )
+    gate = pl.pallas_call(
+        gate_kernel,
+        out_shape=jax.ShapeDtypeStruct((1,), jnp.int32),
+        in_specs=[HBM] * 4,
+        out_specs=SMEM,
+        compiler_params=pltpu.CompilerParams(vmem_limit_bytes=60 << 20),
+    )(*args)
     low_rows, high_rows = call(
-        rows_kernel, [(108, nz), (104, nz)], *args, limit=60, **inputs
+        rows_kernel, [(108, nz), (104, nz)], gate, *args, ins=[SMEM] + [VMEM] * 4
     )
     n = lax.axis_size("gy")
     row_after = lax.ppermute(low_rows, "gy", [(i + 1, i) for i in range(n - 1)])
     row_before = lax.ppermute(high_rows, "gy", [(i, i + 1) for i in range(n - 1)])
-    fine = call(fine_kernel, [(5, 4, 8, nz)], *args, **inputs)
+    fine = call(fine_kernel, [(5, 4, 8, nz)], *args)
 
     even = lax.axis_index("gx") % 2 == 0
     outer, inner = call(

time: 71.1 us -> 70.6 us (level)
  Pallas kernels: 8.64 us -> 7.39 us
    pallas_call x6, Pallas kernels: 8.64 us -> 6.87 us  [call(): pl.pallas_call(kernel, out_shape=results if len(results) > 1 else results...]
  transfers between devices with their start and end apart: 10 -> 10, of which waited for: 8 -> 8; matrix products, arithmetic and copies ran while one was open for 0% -> 0% of each run, Pallas kernels for 1% -> 0%
where the time goes in v9:
time: 70.6 us; the launch traced here: 70.1 us
  starting transfers between devices  36.3 us (51%)
  waiting for transfers between devices  25.5 us (36%)
  Pallas kernels  7.39 us (10%)
    ppermute x3, starting transfers between devices, outer_swap(): lax.ppermute(value, axis, [(i, (i + 1 ^ 1) - 1) for i in range(1, n - 1)])  13.1 us
    pallas_call x6, Pallas kernels, call(): pl.pallas_call(kernel, out_shape=results if len(results) > 1 else results...  6.87 us
    ppermute x3, waiting for transfers between devices, outer_swap(): lax.ppermute(value, axis, [(i, (i + 1 ^ 1) - 1) for i in range(1, n - 1)])  6.54 us
    ppermute x1, starting transfers between devices, gather_low(): beyond = lax.ppermute(own, 'gy', moves).reshape(9, 1, 10, nz)  6.29 us
    ppermute x1, starting transfers between devices, per_device(): lax.ppermute(high_rows, 'gy', [(i, i + 1) for i in range(n - 1)])  5.49 us
    all_to_all x1, waiting for transfers between devices, gather_low(): row = lax.all_to_all(low, ('gx', 'gy'), 0, 0, axis_index_groups=groups)  5.37 us
    ppermute x1, waiting for transfers between devices, gather_low(): other = lax.ppermute(half, 'gx', moves).reshape(8, 10, nz)  5.14 us
    ppermute x1, waiting for transfers between devices, per_device(): lax.ppermute(high_rows, 'gy', [(i, i + 1) for i in range(n - 1)])  4.41 us
  transfers between devices with their start and end apart: 10, of which 8 were waited for; matrix products, arithmetic and copies ran while one was open for 0% of the time, Pallas kernels for 0%

profile of v9, /device:TPU:224, one launch (start us, length us, event | category | flops | bytes accessed | tf_op | source)
XLA Modules:
  0.0 70.1 jit_solution(15379380086580808977)
XLA Ops:
  0.0 0.5 shard_map.47.gate
  0.5 0.4 copy-done
  1.0 0.7 %shard_map.48 = (f32[108,512]{1,0:T(8,128)S(1)}, f32[104,512]{1,0:T(8,128)S(1)}) custom-call(s32[1]{0:T(128)} %shard_map.47.gate, s32[4,8,512]{2,1,0:T(8,128)S(1)} %copy-done.1, s32[4,8,512]{2,1,0:T(8,128)S(1)} %copy-done.2, s32[4,8,512]{2,1,0:T(8,128)S(1)} %copy-done.3, f32[3,4,8,512]{3,2,1,0:T(8,128)S(1)} %copy-done), custom_call_target="tpu_custom_call" | custom-call | tf_op jit(solution)/shard_map/pallas_call | solution.py:419
  1.7 1.9 %collective-permute-start = (f32[108,512]{1,0:T(8,128)S(1)}, f32[108,512]{1,0:T(8,128)S(1)}, u32[]{:S(2)}, u32[]{:S(2)}) collective-permute-start(f32[108,512]{1,0:T(8,128)S(1)} %get-tuple-element.9), channel_id=1, source_target_pairs={{1,0},{2,1},{3,2},{4,3},{5,4},{6,5},{7,6},{8,7},{9,8},{10,9},{11,1... | collective-permute-start | bytes 663560 | tf_op jit(solution)/shard_map/ppermute | solution.py:494
  3.7 5.5 %collective-permute-start.1 = (f32[104,512]{1,0:T(8,128)S(1)}, f32[104,512]{1,0:T(8,128)S(1)}, u32[]{:S(2)}, u32[]{:S(2)}) collective-permute-start(f32[104,512]{1,0:T(8,128)S(1)} %get-tuple-element.10), channel_id=1, source_target_pairs={{0,1},{1,2},{2,3},{3,4},{4,5},{5,6},{6,7},{7,8},{8,9},{9,10},{10,1... | collective-permute-start | bytes 638984 | tf_op jit(solution)/shard_map/ppermute | solution.py:495
  9.2 4.4 %collective-permute-done.1.high.row_before = f32[104,512]{1,0:T(8,128)S(1)} collective-permute-done((f32[104,512]{1,0:T(8,128)S(1)}, f32[104,512]{1,0:T(8,128)S(1)}, u32[]{:S(2)}, u32[]{:S(2)}) %collective-permute-start.1) | collective-permute-done | bytes 213024 | tf_op jit(solution)/shard_map/ppermute | solution.py:495
  13.7 3.1 %collective-permute-start.2 = (f32[88,512]{1,0:T(8,128)S(1)}, f32[88,512]{1,0:T(8,128)S(1)}, u32[]{:S(2)}, u32[]{:S(2)}) collective-permute-start(f32[88,512]{1,0:T(8,128)S(1)} %get-tuple-element.11), channel_id=1, source_target_pairs={{16,32},{32,16},{48,64},{64,48},{80,96},{96,80},{112,128},{128,112... | collective-permute-start | bytes 540680 | tf_op jit(solution)/shard_map/ppermute | solution.py:435
  16.8 2.3 %collective-permute-start.3 = (f32[82,512]{1,0:T(8,128)S(1)}, f32[82,512]{1,0:T(8,128)S(1)}, u32[]{:S(2)}, u32[]{:S(2)}) collective-permute-start(f32[82,512]{1,0:T(8,128)S(1)} %get-tuple-element.12), channel_id=1, source_target_pairs={{0,16},{16,0},{32,48},{48,32},{64,80},{80,64},{96,112},{112,96},{1... | collective-permute-start | bytes 503816 | tf_op jit(solution)/shard_map/ppermute | solution.py:430
  19.1 1.0 %collective-permute-done.3 = f32[82,512]{1,0:T(8,128)S(1)} collective-permute-done((f32[82,512]{1,0:T(8,128)S(1)}, f32[82,512]{1,0:T(8,128)S(1)}, u32[]{:S(2)}, u32[]{:S(2)}) %collective-permute-start.3) | collective-permute-done | bytes 167968 | tf_op jit(solution)/shard_map/ppermute | solution.py:430
  20.2 3.7 %collective-permute-done.2 = f32[88,512]{1,0:T(8,128)S(1)} collective-permute-done((f32[88,512]{1,0:T(8,128)S(1)}, f32[88,512]{1,0:T(8,128)S(1)}, u32[]{:S(2)}, u32[]{:S(2)}) %collective-permute-start.2) | collective-permute-done | bytes 180256 | tf_op jit(solution)/shard_map/ppermute | solution.py:435
  23.9 2.1 %shard_map.50 = f32[80,256]{1,0:T(8,128)S(1)} custom-call(f32[5,4,8,512]{3,2,1,0:T(8,128)S(1)} %shard_map.46.fine, f32[108,512]{1,0:T(8,128)S(1)} %collective-permute-done.low.row_after, f32[104,512]{1,0:T(8,128)S(1)} %collective-permute-done.1.high.row_before, f32[82,512]{1,0:T(8,128)S(1)} %get-tuple-element.14.before, f32[82,512]{1,0:T(8,128)S(1)} %get-tuple-element.13.after), custom_call_target="tpu_custom_call" | custom-call | tf_op jit(solution)/shard_map/pallas_call | solution.py:419
  26.0 3.1 %collective-permute-start.4 = (f32[88,256]{1,0:T(8,128)S(1)}, f32[88,256]{1,0:T(8,128)S(1)}, u32[]{:S(2)}, u32[]{:S(2)}) collective-permute-start(f32[88,256]{1,0:T(8,128)S(1)} %pad_maximum_fusion), channel_id=1, source_target_pairs={{16,32},{32,16},{48,64},{64,48},{80,96},{96,80},{112,128},{128,112... | collective-permute-start | bytes 270344 | tf_op jit(solution)/shard_map/ppermute | solution.py:435
  29.1 1.9 %collective-permute-start.5 = (f32[80,256]{1,0:T(8,128)S(1)}, f32[80,256]{1,0:T(8,128)S(1)}, u32[]{:S(2)}, u32[]{:S(2)}) collective-permute-start(f32[80,256]{1,0:T(8,128)S(1)} %shard_map.50), channel_id=1, source_target_pairs={{0,16},{16,0},{32,48},{48,32},{64,80},{80,64},{96,112},{112,96},{1... | collective-permute-start | bytes 245768 | tf_op jit(solution)/shard_map/ppermute | solution.py:430
  31.1 1.2 %collective-permute-done.5 = f32[80,256]{1,0:T(8,128)S(1)} collective-permute-done((f32[80,256]{1,0:T(8,128)S(1)}, f32[80,256]{1,0:T(8,128)S(1)}, u32[]{:S(2)}, u32[]{:S(2)}) %collective-permute-start.5) | collective-permute-done | bytes 81952 | tf_op jit(solution)/shard_map/ppermute | solution.py:430
  32.3 2.9 %collective-permute-done.4 = f32[88,256]{1,0:T(8,128)S(1)} collective-permute-done((f32[88,256]{1,0:T(8,128)S(1)}, f32[88,256]{1,0:T(8,128)S(1)}, u32[]{:S(2)}, u32[]{:S(2)}) %collective-permute-start.4) | collective-permute-done | bytes 90144 | tf_op jit(solution)/shard_map/ppermute | solution.py:435
  35.2 1.1 %shard_map.51 = f32[16,10,128]{2,1,0:T(8,128)} custom-call(f32[5,2,8,256]{3,2,1,0:T(8,128)S(1)} %bitcast.10, f32[5,2,8,256]{3,2,1,0:T(8,128)S(1)} %bitcast.6, f32[5,2,8,256]{3,2,1,0:T(8,128)S(1)} %bitcast.8), custom_call_target="tpu_custom_call" | custom-call | tf_op jit(solution)/shard_map/pallas_call | solution.py:419
  36.3 3.4 %all-to-all-start = ((f32[16,10,128]{2,1,0:T(8,128)}), f32[16,10,128]{2,1,0:T(8,128)S(1)}, u32[]{:S(2)}, u32[]{:S(2)}) async-start(f32[16,10,128]{2,1,0:T(8,128)} %shard_map.51), calls=%async_computation | async-start | bytes 262144 | tf_op jit(solution)/shard_map/all_to_all | solution.py:455
  39.7 5.4 %all-to-all-done = f32[16,10,128]{2,1,0:T(8,128)S(1)} async-done(((f32[16,10,128]{2,1,0:T(8,128)}), f32[16,10,128]{2,1,0:T(8,128)S(1)}, u32[]{:S(2)}, u32[]{:S(2)}) %all-to-all-start) | async-done | bytes 81952 | tf_op jit(solution)/shard_map/all_to_all | solution.py:455
  45.1 1.9 %collective-permute-start.6 = (f32[80,128]{1,0:T(8,128)S(1)}, f32[80,128]{1,0:T(8,128)S(1)}, u32[]{:S(2)}, u32[]{:S(2)}) collective-permute-start(f32[80,128]{1,0:T(8,128)S(1)} %reshape.40), channel_id=1, source_target_pairs={{0,128},{16,144},{32,160},{48,176},{128,256},{144,272},{160,288},{... | collective-permute-start | bytes 122888 | tf_op jit(solution)/shard_map/ppermute | solution.py:461
  47.1 5.1 %collective-permute-done.6 = f32[80,128]{1,0:T(8,128)S(1)} collective-permute-done((f32[80,128]{1,0:T(8,128)S(1)}, f32[80,128]{1,0:T(8,128)S(1)}, u32[]{:S(2)}, u32[]{:S(2)}) %collective-permute-start.6) | collective-permute-done | bytes 40992 | tf_op jit(solution)/shard_map/ppermute | solution.py:461
  52.3 6.8 %collective-permute-start.7 = (f32[180,128]{1,0:T(8,128)S(1)}, f32[180,128]{1,0:T(8,128)S(1)}, u32[]{:S(2)}, u32[]{:S(2)}) collective-permute-start(f32[180,128]{1,0:T(8,128)S(1)} %reshape.42), channel_id=1, source_target_pairs={{1,2},{2,1},{3,4},{4,3},{5,6},{6,5},{7,8},{8,7},{9,10},{10,9},{11,... | collective-permute-start | bytes 276488 | tf_op jit(solution)/shard_map/ppermute | solution.py:435
  59.2 6.3 %collective-permute-start.8 = (f32[90,128]{1,0:T(8,128)S(1)}, f32[90,128]{1,0:T(8,128)S(1)}, u32[]{:S(2)}, u32[]{:S(2)}) collective-permute-start(f32[90,128]{1,0:T(8,128)S(1)} %reshape.45), channel_id=1, source_target_pairs={{2,0},{1,3},{4,2},{3,5},{6,4},{5,7},{8,6},{7,9},{10,8},{9,11},{12,... | collective-permute-start | bytes 138248 | tf_op jit(solution)/shard_map/ppermute | solution.py:470
  65.5 1.7 %collective-permute-done.8 = f32[90,128]{1,0:T(8,128)S(1)} collective-permute-done((f32[90,128]{1,0:T(8,128)S(1)}, f32[90,128]{1,0:T(8,128)S(1)}, u32[]{:S(2)}, u32[]{:S(2)}) %collective-permute-start.8) | collective-permute-done | bytes 46112 | tf_op jit(solution)/shard_map/ppermute | solution.py:470
  67.3 2.9 %shard_map.52 = f32[3,4,8,512]{3,2,1,0:T(8,128)} custom-call(f32[9,5,10,128]{3,2,1,0:T(8,128)S(1)} %maximum_select_fusion.low, f32[5,2,8,256]{3,2,1,0:T(8,128)S(1)} %bitcast.11, f32[5,2,8,256]{3,2,1,0:T(8,128)S(1)} %bitcast.7, f32[5,2,8,256]{3,2,1,0:T(8,128)S(1)} %bitcast.9, f32[5,4,8,512]{3,2,1,0:T(8,128)S(1)} %shard_map.46.fine, ...), custom_call_target="tpu_custom_call" | custom-call | tf_op jit(solution)/shard_map/pallas_call | solution.py:419
  (25 shorter events, 0.4 us)
Async XLA Ops:
  0.0 0.9 %copy-start = (f32[3,4,8,512]{3,2,1,0:T(8,128)S(1)}, f32[3,4,8,512]{3,2,1,0:T(8,128)}, u32[]{:S(2)}) copy-start(f32[3,4,8,512]{3,2,1,0:T(8,128)} %load.3) | copy-start | bytes 589828
  0.0 0.9 %copy-start.3 = (s32[4,8,512]{2,1,0:T(8,128)S(1)}, s32[4,8,512]{2,1,0:T(8,128)}, u32[]{:S(2)}) copy-start(s32[4,8,512]{2,1,0:T(8,128)} %loaded.3) | copy-start | bytes 196612
  0.0 1.0 %copy-start.2 = (s32[4,8,512]{2,1,0:T(8,128)S(1)}, s32[4,8,512]{2,1,0:T(8,128)}, u32[]{:S(2)}) copy-start(s32[4,8,512]{2,1,0:T(8,128)} %fixed.3) | copy-start | bytes 196612
  0.0 1.0 %copy-start.1 = (s32[4,8,512]{2,1,0:T(8,128)S(1)}, s32[4,8,512]{2,1,0:T(8,128)}, u32[]{:S(2)}) copy-start(s32[4,8,512]{2,1,0:T(8,128)} %density.3) | copy-start | bytes 196612
  1.7 11.9 %collective-permute-start = (f32[108,512]{1,0:T(8,128)S(1)}, f32[108,512]{1,0:T(8,128)S(1)}, u32[]{:S(2)}, u32[]{:S(2)}) collective-permute-start(f32[108,512]{1,0:T(8,128)S(1)} %get-tuple-element.9), channel_id=1, source_target_pairs={{1,0},{2,1},{3,2},{4,3},{5,4},{6,5},{7,6},{8,7},{9,8},{10,9},{11,1... | collective-permute-start | bytes 663560 | tf_op jit(solution)/shard_map/ppermute | solution.py:494
  3.7 10.0 %collective-permute-start.1 = (f32[104,512]{1,0:T(8,128)S(1)}, f32[104,512]{1,0:T(8,128)S(1)}, u32[]{:S(2)}, u32[]{:S(2)}) collective-permute-start(f32[104,512]{1,0:T(8,128)S(1)} %get-tuple-element.10), channel_id=1, source_target_pairs={{0,1},{1,2},{2,3},{3,4},{4,5},{5,6},{6,7},{7,8},{8,9},{9,10},{10,1... | collective-permute-start | bytes 638984 | tf_op jit(solution)/shard_map/ppermute | solution.py:495
  13.7 10.1 %collective-permute-start.2 = (f32[88,512]{1,0:T(8,128)S(1)}, f32[88,512]{1,0:T(8,128)S(1)}, u32[]{:S(2)}, u32[]{:S(2)}) collective-permute-start(f32[88,512]{1,0:T(8,128)S(1)} %get-tuple-element.11), channel_id=1, source_target_pairs={{16,32},{32,16},{48,64},{64,48},{80,96},{96,80},{112,128},{128,112... | collective-permute-start | bytes 540680 | tf_op jit(solution)/shard_map/ppermute | solution.py:435
  16.8 3.3 %collective-permute-start.3 = (f32[82,512]{1,0:T(8,128)S(1)}, f32[82,512]{1,0:T(8,128)S(1)}, u32[]{:S(2)}, u32[]{:S(2)}) collective-permute-start(f32[82,512]{1,0:T(8,128)S(1)} %get-tuple-element.12), channel_id=1, source_target_pairs={{0,16},{16,0},{32,48},{48,32},{64,80},{80,64},{96,112},{112,96},{1... | collective-permute-start | bytes 503816 | tf_op jit(solution)/shard_map/ppermute | solution.py:430
  26.0 9.2 %collective-permute-start.4 = (f32[88,256]{1,0:T(8,128)S(1)}, f32[88,256]{1,0:T(8,128)S(1)}, u32[]{:S(2)}, u32[]{:S(2)}) collective-permute-start(f32[88,256]{1,0:T(8,128)S(1)} %pad_maximum_fusion), channel_id=1, source_target_pairs={{16,32},{32,16},{48,64},{64,48},{80,96},{96,80},{112,128},{128,112... | collective-permute-start | bytes 270344 | tf_op jit(solution)/shard_map/ppermute | solution.py:435
  29.1 3.2 %collective-permute-start.5 = (f32[80,256]{1,0:T(8,128)S(1)}, f32[80,256]{1,0:T(8,128)S(1)}, u32[]{:S(2)}, u32[]{:S(2)}) collective-permute-start(f32[80,256]{1,0:T(8,128)S(1)} %shard_map.50), channel_id=1, source_target_pairs={{0,16},{16,0},{32,48},{48,32},{64,80},{80,64},{96,112},{112,96},{1... | collective-permute-start | bytes 245768 | tf_op jit(solution)/shard_map/ppermute | solution.py:430
  36.3 8.8 %all-to-all-start = ((f32[16,10,128]{2,1,0:T(8,128)}), f32[16,10,128]{2,1,0:T(8,128)S(1)}, u32[]{:S(2)}, u32[]{:S(2)}) async-start(f32[16,10,128]{2,1,0:T(8,128)} %shard_map.51), calls=%async_computation | async-start | bytes 262144 | tf_op jit(solution)/shard_map/all_to_all | solution.py:455
  45.1 7.1 %collective-permute-start.6 = (f32[80,128]{1,0:T(8,128)S(1)}, f32[80,128]{1,0:T(8,128)S(1)}, u32[]{:S(2)}, u32[]{:S(2)}) collective-permute-start(f32[80,128]{1,0:T(8,128)S(1)} %reshape.40), channel_id=1, source_target_pairs={{0,128},{16,144},{32,160},{48,176},{128,256},{144,272},{160,288},{... | collective-permute-start | bytes 122888 | tf_op jit(solution)/shard_map/ppermute | solution.py:461
  52.3 14.9 %collective-permute-start.7 = (f32[180,128]{1,0:T(8,128)S(1)}, f32[180,128]{1,0:T(8,128)S(1)}, u32[]{:S(2)}, u32[]{:S(2)}) collective-permute-start(f32[180,128]{1,0:T(8,128)S(1)} %reshape.42), channel_id=1, source_target_pairs={{1,2},{2,1},{3,4},{4,3},{5,6},{6,5},{7,8},{8,7},{9,10},{10,9},{11,... | collective-permute-start | bytes 276488 | tf_op jit(solution)/shard_map/ppermute | solution.py:435
  59.2 8.0 %collective-permute-start.8 = (f32[90,128]{1,0:T(8,128)S(1)}, f32[90,128]{1,0:T(8,128)S(1)}, u32[]{:S(2)}, u32[]{:S(2)}) collective-permute-start(f32[90,128]{1,0:T(8,128)S(1)} %reshape.45), channel_id=1, source_target_pairs={{2,0},{1,3},{4,2},{3,5},{6,4},{5,7},{8,6},{7,9},{10,8},{9,11},{12,... | collective-permute-start | bytes 138248 | tf_op jit(solution)/shard_map/ppermute | solution.py:470

commit v10 on v9

--- a/solution.py
+++ b/solution.py
@@ -6,7 +6,7 @@
 from jax.sharding import PartitionSpec as P
 
 F32 = jnp.float32
-EXTRA = 8
+EXTRA = 1
 HBM = pl.BlockSpec(memory_space=pltpu.HBM)
 SMEM = pl.BlockSpec(memory_space=pltpu.SMEM)
 VMEM = pl.BlockSpec(memory_space=pltpu.VMEM)

time: 70.6 us -> 70.6 us (level)
  no operation moved by 1% of the time
where the time goes in v10:
time: 70.6 us; the launch traced here: 70.1 us
  starting transfers between devices  36.3 us (51%)
  waiting for transfers between devices  25.5 us (36%)
  Pallas kernels  7.39 us (10%)
    ppermute x3, starting transfers between devices, outer_swap(): lax.ppermute(value, axis, [(i, (i + 1 ^ 1) - 1) for i in range(1, n - 1)])  13.1 us
    pallas_call x6, Pallas kernels, call(): pl.pallas_call(kernel, out_shape=results if len(results) > 1 else results...  6.87 us
    ppermute x3, waiting for transfers between devices, outer_swap(): lax.ppermute(value, axis, [(i, (i + 1 ^ 1) - 1) for i in range(1, n - 1)])  6.54 us
    ppermute x1, starting transfers between devices, gather_low(): beyond = lax.ppermute(own, 'gy', moves).reshape(9, 1, 10, nz)  6.29 us
    ppermute x1, starting transfers between devices, per_device(): lax.ppermute(high_rows, 'gy', [(i, i + 1) for i in range(n - 1)])  5.49 us
    all_to_all x1, waiting for transfers between devices, gather_low(): row = lax.all_to_all(low, ('gx', 'gy'), 0, 0, axis_index_groups=groups)  5.37 us
    ppermute x1, waiting for transfers between devices, gather_low(): other = lax.ppermute(half, 'gx', moves).reshape(8, 10, nz)  5.14 us
    ppermute x1, waiting for transfers between devices, per_device(): lax.ppermute(high_rows, 'gy', [(i, i + 1) for i in range(n - 1)])  4.41 us
  transfers between devices with their start and end apart: 10, of which 8 were waited for; matrix products, arithmetic and copies ran while one was open for 0% of the time, Pallas kernels for 0%

profile of v10, /device:TPU:224, one launch (start us, length us, event | category | flops | bytes accessed | tf_op | source)
XLA Modules:
  0.0 70.1 jit_solution(12872640159642423877)
XLA Ops:
  0.0 0.5 shard_map.47.gate
  0.5 0.4 copy-done
  1.0 0.7 %shard_map.48 = (f32[108,512]{1,0:T(8,128)S(1)}, f32[104,512]{1,0:T(8,128)S(1)}) custom-call(s32[1]{0:T(128)} %shard_map.47.gate, s32[4,8,512]{2,1,0:T(8,128)S(1)} %copy-done.1, s32[4,8,512]{2,1,0:T(8,128)S(1)} %copy-done.2, s32[4,8,512]{2,1,0:T(8,128)S(1)} %copy-done.3, f32[3,4,8,512]{3,2,1,0:T(8,128)S(1)} %copy-done), custom_call_target="tpu_custom_call" | custom-call | tf_op jit(solution)/shard_map/pallas_call | solution.py:419
  1.7 1.9 %collective-permute-start = (f32[108,512]{1,0:T(8,128)S(1)}, f32[108,512]{1,0:T(8,128)S(1)}, u32[]{:S(2)}, u32[]{:S(2)}) collective-permute-start(f32[108,512]{1,0:T(8,128)S(1)} %get-tuple-element.9), channel_id=1, source_target_pairs={{1,0},{2,1},{3,2},{4,3},{5,4},{6,5},{7,6},{8,7},{9,8},{10,9},{11,1... | collective-permute-start | bytes 663560 | tf_op jit(solution)/shard_map/ppermute | solution.py:494
  3.7 5.5 %collective-permute-start.1 = (f32[104,512]{1,0:T(8,128)S(1)}, f32[104,512]{1,0:T(8,128)S(1)}, u32[]{:S(2)}, u32[]{:S(2)}) collective-permute-start(f32[104,512]{1,0:T(8,128)S(1)} %get-tuple-element.10), channel_id=1, source_target_pairs={{0,1},{1,2},{2,3},{3,4},{4,5},{5,6},{6,7},{7,8},{8,9},{9,10},{10,1... | collective-permute-start | bytes 638984 | tf_op jit(solution)/shard_map/ppermute | solution.py:495
  9.2 4.4 %collective-permute-done.1.high.row_before = f32[104,512]{1,0:T(8,128)S(1)} collective-permute-done((f32[104,512]{1,0:T(8,128)S(1)}, f32[104,512]{1,0:T(8,128)S(1)}, u32[]{:S(2)}, u32[]{:S(2)}) %collective-permute-start.1) | collective-permute-done | bytes 213024 | tf_op jit(solution)/shard_map/ppermute | solution.py:495
  13.7 3.1 %collective-permute-start.2 = (f32[88,512]{1,0:T(8,128)S(1)}, f32[88,512]{1,0:T(8,128)S(1)}, u32[]{:S(2)}, u32[]{:S(2)}) collective-permute-start(f32[88,512]{1,0:T(8,128)S(1)} %get-tuple-element.11), channel_id=1, source_target_pairs={{16,32},{32,16},{48,64},{64,48},{80,96},{96,80},{112,128},{128,112... | collective-permute-start | bytes 540680 | tf_op jit(solution)/shard_map/ppermute | solution.py:435
  16.8 2.3 %collective-permute-start.3 = (f32[82,512]{1,0:T(8,128)S(1)}, f32[82,512]{1,0:T(8,128)S(1)}, u32[]{:S(2)}, u32[]{:S(2)}) collective-permute-start(f32[82,512]{1,0:T(8,128)S(1)} %get-tuple-element.12), channel_id=1, source_target_pairs={{0,16},{16,0},{32,48},{48,32},{64,80},{80,64},{96,112},{112,96},{1... | collective-permute-start | bytes 503816 | tf_op jit(solution)/shard_map/ppermute | solution.py:430
  19.1 1.0 %collective-permute-done.3 = f32[82,512]{1,0:T(8,128)S(1)} collective-permute-done((f32[82,512]{1,0:T(8,128)S(1)}, f32[82,512]{1,0:T(8,128)S(1)}, u32[]{:S(2)}, u32[]{:S(2)}) %collective-permute-start.3) | collective-permute-done | bytes 167968 | tf_op jit(solution)/shard_map/ppermute | solution.py:430
  20.2 3.7 %collective-permute-done.2 = f32[88,512]{1,0:T(8,128)S(1)} collective-permute-done((f32[88,512]{1,0:T(8,128)S(1)}, f32[88,512]{1,0:T(8,128)S(1)}, u32[]{:S(2)}, u32[]{:S(2)}) %collective-permute-start.2) | collective-permute-done | bytes 180256 | tf_op jit(solution)/shard_map/ppermute | solution.py:435
  23.9 2.1 %shard_map.50 = f32[80,256]{1,0:T(8,128)S(1)} custom-call(f32[5,4,8,512]{3,2,1,0:T(8,128)S(1)} %shard_map.46.fine, f32[108,512]{1,0:T(8,128)S(1)} %collective-permute-done.low.row_after, f32[104,512]{1,0:T(8,128)S(1)} %collective-permute-done.1.high.row_before, f32[82,512]{1,0:T(8,128)S(1)} %get-tuple-element.14.before, f32[82,512]{1,0:T(8,128)S(1)} %get-tuple-element.13.after), custom_call_target="tpu_custom_call" | custom-call | tf_op jit(solution)/shard_map/pallas_call | solution.py:419
  26.0 3.1 %collective-permute-start.4 = (f32[81,256]{1,0:T(8,128)S(1)}, f32[81,256]{1,0:T(8,128)S(1)}, u32[]{:S(2)}, u32[]{:S(2)}) collective-permute-start(f32[81,256]{1,0:T(8,128)S(1)} %pad_maximum_fusion), channel_id=1, source_target_pairs={{16,32},{32,16},{48,64},{64,48},{80,96},{96,80},{112,128},{128,112... | collective-permute-start | bytes 248840 | tf_op jit(solution)/shard_map/ppermute | solution.py:435
  29.1 1.9 %collective-permute-start.5 = (f32[80,256]{1,0:T(8,128)S(1)}, f32[80,256]{1,0:T(8,128)S(1)}, u32[]{:S(2)}, u32[]{:S(2)}) collective-permute-start(f32[80,256]{1,0:T(8,128)S(1)} %shard_map.50), channel_id=1, source_target_pairs={{0,16},{16,0},{32,48},{48,32},{64,80},{80,64},{96,112},{112,96},{1... | collective-permute-start | bytes 245768 | tf_op jit(solution)/shard_map/ppermute | solution.py:430
  31.1 1.2 %collective-permute-done.5 = f32[80,256]{1,0:T(8,128)S(1)} collective-permute-done((f32[80,256]{1,0:T(8,128)S(1)}, f32[80,256]{1,0:T(8,128)S(1)}, u32[]{:S(2)}, u32[]{:S(2)}) %collective-permute-start.5) | collective-permute-done | bytes 81952 | tf_op jit(solution)/shard_map/ppermute | solution.py:430
  32.3 2.9 %collective-permute-done.4 = f32[81,256]{1,0:T(8,128)S(1)} collective-permute-done((f32[81,256]{1,0:T(8,128)S(1)}, f32[81,256]{1,0:T(8,128)S(1)}, u32[]{:S(2)}, u32[]{:S(2)}) %collective-permute-start.4) | collective-permute-done | bytes 82976 | tf_op jit(solution)/shard_map/ppermute | solution.py:435
  35.2 1.1 %shard_map.51 = f32[16,10,128]{2,1,0:T(8,128)} custom-call(f32[5,2,8,256]{3,2,1,0:T(8,128)S(1)} %bitcast.10, f32[5,2,8,256]{3,2,1,0:T(8,128)S(1)} %bitcast.6, f32[5,2,8,256]{3,2,1,0:T(8,128)S(1)} %bitcast.8), custom_call_target="tpu_custom_call" | custom-call | tf_op jit(solution)/shard_map/pallas_call | solution.py:419
  36.3 3.4 %all-to-all-start = ((f32[16,10,128]{2,1,0:T(8,128)}), f32[16,10,128]{2,1,0:T(8,128)S(1)}, u32[]{:S(2)}, u32[]{:S(2)}) async-start(f32[16,10,128]{2,1,0:T(8,128)} %shard_map.51), calls=%async_computation | async-start | bytes 262144 | tf_op jit(solution)/shard_map/all_to_all | solution.py:455
  39.7 5.4 %all-to-all-done = f32[16,10,128]{2,1,0:T(8,128)S(1)} async-done(((f32[16,10,128]{2,1,0:T(8,128)}), f32[16,10,128]{2,1,0:T(8,128)S(1)}, u32[]{:S(2)}, u32[]{:S(2)}) %all-to-all-start) | async-done | bytes 81952 | tf_op jit(solution)/shard_map/all_to_all | solution.py:455
  45.1 1.9 %collective-permute-start.6 = (f32[80,128]{1,0:T(8,128)S(1)}, f32[80,128]{1,0:T(8,128)S(1)}, u32[]{:S(2)}, u32[]{:S(2)}) collective-permute-start(f32[80,128]{1,0:T(8,128)S(1)} %reshape.40), channel_id=1, source_target_pairs={{0,128},{16,144},{32,160},{48,176},{128,256},{144,272},{160,288},{... | collective-permute-start | bytes 122888 | tf_op jit(solution)/shard_map/ppermute | solution.py:461
  47.1 5.1 %collective-permute-done.6 = f32[80,128]{1,0:T(8,128)S(1)} collective-permute-done((f32[80,128]{1,0:T(8,128)S(1)}, f32[80,128]{1,0:T(8,128)S(1)}, u32[]{:S(2)}, u32[]{:S(2)}) %collective-permute-start.6) | collective-permute-done | bytes 40992 | tf_op jit(solution)/shard_map/ppermute | solution.py:461
  52.3 6.8 %collective-permute-start.7 = (f32[180,128]{1,0:T(8,128)S(1)}, f32[180,128]{1,0:T(8,128)S(1)}, u32[]{:S(2)}, u32[]{:S(2)}) collective-permute-start(f32[180,128]{1,0:T(8,128)S(1)} %reshape.42), channel_id=1, source_target_pairs={{1,2},{2,1},{3,4},{4,3},{5,6},{6,5},{7,8},{8,7},{9,10},{10,9},{11,... | collective-permute-start | bytes 276488 | tf_op jit(solution)/shard_map/ppermute | solution.py:435
  59.2 6.3 %collective-permute-start.8 = (f32[90,128]{1,0:T(8,128)S(1)}, f32[90,128]{1,0:T(8,128)S(1)}, u32[]{:S(2)}, u32[]{:S(2)}) collective-permute-start(f32[90,128]{1,0:T(8,128)S(1)} %reshape.45), channel_id=1, source_target_pairs={{2,0},{1,3},{4,2},{3,5},{6,4},{5,7},{8,6},{7,9},{10,8},{9,11},{12,... | collective-permute-start | bytes 138248 | tf_op jit(solution)/shard_map/ppermute | solution.py:470
  65.5 1.7 %collective-permute-done.8 = f32[90,128]{1,0:T(8,128)S(1)} collective-permute-done((f32[90,128]{1,0:T(8,128)S(1)}, f32[90,128]{1,0:T(8,128)S(1)}, u32[]{:S(2)}, u32[]{:S(2)}) %collective-permute-start.8) | collective-permute-done | bytes 46112 | tf_op jit(solution)/shard_map/ppermute | solution.py:470
  67.3 2.9 %shard_map.52 = f32[3,4,8,512]{3,2,1,0:T(8,128)} custom-call(f32[9,5,10,128]{3,2,1,0:T(8,128)S(1)} %maximum_select_fusion.low, f32[5,2,8,256]{3,2,1,0:T(8,128)S(1)} %bitcast.11, f32[5,2,8,256]{3,2,1,0:T(8,128)S(1)} %bitcast.7, f32[5,2,8,256]{3,2,1,0:T(8,128)S(1)} %bitcast.9, f32[5,4,8,512]{3,2,1,0:T(8,128)S(1)} %shard_map.46.fine, ...), custom_call_target="tpu_custom_call" | custom-call | tf_op jit(solution)/shard_map/pallas_call | solution.py:419
  (25 shorter events, 0.4 us)
Async XLA Ops:
  0.0 0.9 %copy-start = (f32[3,4,8,512]{3,2,1,0:T(8,128)S(1)}, f32[3,4,8,512]{3,2,1,0:T(8,128)}, u32[]{:S(2)}) copy-start(f32[3,4,8,512]{3,2,1,0:T(8,128)} %load.3) | copy-start | bytes 589828
  0.0 0.9 %copy-start.3 = (s32[4,8,512]{2,1,0:T(8,128)S(1)}, s32[4,8,512]{2,1,0:T(8,128)}, u32[]{:S(2)}) copy-start(s32[4,8,512]{2,1,0:T(8,128)} %loaded.3) | copy-start | bytes 196612
  0.0 1.0 %copy-start.2 = (s32[4,8,512]{2,1,0:T(8,128)S(1)}, s32[4,8,512]{2,1,0:T(8,128)}, u32[]{:S(2)}) copy-start(s32[4,8,512]{2,1,0:T(8,128)} %fixed.3) | copy-start | bytes 196612
  0.0 1.0 %copy-start.1 = (s32[4,8,512]{2,1,0:T(8,128)S(1)}, s32[4,8,512]{2,1,0:T(8,128)}, u32[]{:S(2)}) copy-start(s32[4,8,512]{2,1,0:T(8,128)} %density.3) | copy-start | bytes 196612
  1.7 11.9 %collective-permute-start = (f32[108,512]{1,0:T(8,128)S(1)}, f32[108,512]{1,0:T(8,128)S(1)}, u32[]{:S(2)}, u32[]{:S(2)}) collective-permute-start(f32[108,512]{1,0:T(8,128)S(1)} %get-tuple-element.9), channel_id=1, source_target_pairs={{1,0},{2,1},{3,2},{4,3},{5,4},{6,5},{7,6},{8,7},{9,8},{10,9},{11,1... | collective-permute-start | bytes 663560 | tf_op jit(solution)/shard_map/ppermute | solution.py:494
  3.7 10.0 %collective-permute-start.1 = (f32[104,512]{1,0:T(8,128)S(1)}, f32[104,512]{1,0:T(8,128)S(1)}, u32[]{:S(2)}, u32[]{:S(2)}) collective-permute-start(f32[104,512]{1,0:T(8,128)S(1)} %get-tuple-element.10), channel_id=1, source_target_pairs={{0,1},{1,2},{2,3},{3,4},{4,5},{5,6},{6,7},{7,8},{8,9},{9,10},{10,1... | collective-permute-start | bytes 638984 | tf_op jit(solution)/shard_map/ppermute | solution.py:495
  13.7 10.1 %collective-permute-start.2 = (f32[88,512]{1,0:T(8,128)S(1)}, f32[88,512]{1,0:T(8,128)S(1)}, u32[]{:S(2)}, u32[]{:S(2)}) collective-permute-start(f32[88,512]{1,0:T(8,128)S(1)} %get-tuple-element.11), channel_id=1, source_target_pairs={{16,32},{32,16},{48,64},{64,48},{80,96},{96,80},{112,128},{128,112... | collective-permute-start | bytes 540680 | tf_op jit(solution)/shard_map/ppermute | solution.py:435
  16.8 3.3 %collective-permute-start.3 = (f32[82,512]{1,0:T(8,128)S(1)}, f32[82,512]{1,0:T(8,128)S(1)}, u32[]{:S(2)}, u32[]{:S(2)}) collective-permute-start(f32[82,512]{1,0:T(8,128)S(1)} %get-tuple-element.12), channel_id=1, source_target_pairs={{0,16},{16,0},{32,48},{48,32},{64,80},{80,64},{96,112},{112,96},{1... | collective-permute-start | bytes 503816 | tf_op jit(solution)/shard_map/ppermute | solution.py:430
  26.0 9.2 %collective-permute-start.4 = (f32[81,256]{1,0:T(8,128)S(1)}, f32[81,256]{1,0:T(8,128)S(1)}, u32[]{:S(2)}, u32[]{:S(2)}) collective-permute-start(f32[81,256]{1,0:T(8,128)S(1)} %pad_maximum_fusion), channel_id=1, source_target_pairs={{16,32},{32,16},{48,64},{64,48},{80,96},{96,80},{112,128},{128,112... | collective-permute-start | bytes 248840 | tf_op jit(solution)/shard_map/ppermute | solution.py:435
  29.1 3.2 %collective-permute-start.5 = (f32[80,256]{1,0:T(8,128)S(1)}, f32[80,256]{1,0:T(8,128)S(1)}, u32[]{:S(2)}, u32[]{:S(2)}) collective-permute-start(f32[80,256]{1,0:T(8,128)S(1)} %shard_map.50), channel_id=1, source_target_pairs={{0,16},{16,0},{32,48},{48,32},{64,80},{80,64},{96,112},{112,96},{1... | collective-permute-start | bytes 245768 | tf_op jit(solution)/shard_map/ppermute | solution.py:430
  36.3 8.8 %all-to-all-start = ((f32[16,10,128]{2,1,0:T(8,128)}), f32[16,10,128]{2,1,0:T(8,128)S(1)}, u32[]{:S(2)}, u32[]{:S(2)}) async-start(f32[16,10,128]{2,1,0:T(8,128)} %shard_map.51), calls=%async_computation | async-start | bytes 262144 | tf_op jit(solution)/shard_map/all_to_all | solution.py:455
  45.1 7.1 %collective-permute-start.6 = (f32[80,128]{1,0:T(8,128)S(1)}, f32[80,128]{1,0:T(8,128)S(1)}, u32[]{:S(2)}, u32[]{:S(2)}) collective-permute-start(f32[80,128]{1,0:T(8,128)S(1)} %reshape.40), channel_id=1, source_target_pairs={{0,128},{16,144},{32,160},{48,176},{128,256},{144,272},{160,288},{... | collective-permute-start | bytes 122888 | tf_op jit(solution)/shard_map/ppermute | solution.py:461
  52.3 14.9 %collective-permute-start.7 = (f32[180,128]{1,0:T(8,128)S(1)}, f32[180,128]{1,0:T(8,128)S(1)}, u32[]{:S(2)}, u32[]{:S(2)}) collective-permute-start(f32[180,128]{1,0:T(8,128)S(1)} %reshape.42), channel_id=1, source_target_pairs={{1,2},{2,1},{3,4},{4,3},{5,6},{6,5},{7,8},{8,7},{9,10},{10,9},{11,... | collective-permute-start | bytes 276488 | tf_op jit(solution)/shard_map/ppermute | solution.py:435
  59.2 8.0 %collective-permute-start.8 = (f32[90,128]{1,0:T(8,128)S(1)}, f32[90,128]{1,0:T(8,128)S(1)}, u32[]{:S(2)}, u32[]{:S(2)}) collective-permute-start(f32[90,128]{1,0:T(8,128)S(1)} %reshape.45), channel_id=1, source_target_pairs={{2,0},{1,3},{4,2},{3,5},{6,4},{5,7},{8,6},{7,9},{10,8},{9,11},{12,... | collective-permute-start | bytes 138248 | tf_op jit(solution)/shard_map/ppermute | solution.py:470
